TPU v7x, 32 devices: a whole 2x2x4 slice. The times are simulated.
32 devices in a mesh: member: 4 (over y, x), lat: 2 (over core), lon: 4 (over z).
Axes of the slice: x: 2, y: 2, z: 4, core: 2. Of those that a mesh axis runs over, the one named last changes fastest.
Arguments:
- inputs: bfloat16 [4, 96, 2, 4, 23040], P('member', None, 'lat', 'lon'), may hold values from -6 to 6
- weight: bfloat16 [9, 8064], replicated, may hold values from -0.21875 to 0.21875
- bias: float32 [84], replicated, may hold values from -3 to 3
- analysis: bfloat16 [84, 2, 4, 23040], P(None, 'lat', 'lon'), may hold values from -7 to 7
- field_weight: float32 [84], replicated, may hold values from 0.25 to 2.5
Outputs:
- grad_input: bfloat16 [4, 96, 2, 4, 23040], P('member', None, 'lat', 'lon')
- grad_weight: float32 [9, 8064], replicated
- grad_bias: float32 [84], replicated
All inputs are finite; a program needn't handle non-finite values.
Results may differ from a plain program's by a relative error of at most 0.0053.
Values may be sent and summed in bfloat16 or wider, within the bound.
No kernel may reach another device: no remote copies, remote signals or barrier semaphores. Data moves between devices by JAX's collectives and lax.ppermute only.
A program may use at most 128 MiB of HBM per device.

v0:
```python
import functools

import jax
import jax.numpy as jnp
from jax import lax
from jax.experimental import pallas as pl
from jax.experimental.pallas import tpu as pltpu
from jax.sharding import PartitionSpec as P

LAT_DEV = 64
LANES = 128
ROW_GROUP = 2
FLAT_LANES = 1024
SLACK = 3 * 1024 * 1024
F32 = jnp.float32
BF16 = jnp.bfloat16


def round_up(value, step):
    return -(-value // step) * step


def params(*held):
    total = sum(round_up(rows, 16) * round_up(lanes, LANES) * size for rows, lanes, size in held)
    return pltpu.CompilerParams(vmem_limit_bytes=total + SLACK)


def kept_in_hbm(value):
    return pltpu.with_memory_space_constraint(value, pltpu.HBM)


def kept_in_vmem(value):
    return pltpu.with_memory_space_constraint(value, pltpu.VMEM)


def shape_of(dims, dtype=BF16):
    return jax.ShapeDtypeStruct(dims, dtype)


def cost(flops, moved):
    return pl.CostEstimate(flops=int(flops), bytes_accessed=int(moved), transcendentals=0)


def in_vmem():
    return pl.BlockSpec(memory_space=pltpu.VMEM)


def in_smem():
    return pl.BlockSpec(memory_space=pltpu.SMEM)


def in_hbm():
    return pl.BlockSpec(memory_space=pltpu.HBM)


def anywhere():
    return pl.BlockSpec(memory_space=pl.ANY)


def nt_dot(left, right):
    return lax.dot_general(left, right, (((1,), (1,)), ((), ())), preferred_element_type=F32)


class Grid:
    def __init__(self, cells, members):
        self.cells = cells
        self.columns = cells // LAT_DEV
        self.pitch = round_up(self.columns, LANES)
        self.halo = round_up(self.columns + 1, LANES)
        self.padded = round_up(cells, members * LANES)

    def rows(self, first, width):
        return first // self.columns, -(-min(first + width, self.cells) // self.columns)

    def layout(self, ranges):
        out, row, lane = [], 0, 0
        for first, width in ranges:
            r0, r1 = self.rows(first, width)
            out.append((first, width, r0, r1, row, lane))
            row, lane = row + r1 - r0 + 2, lane + width
        return out, row, lane


def take(ref, start, width):
    low = start // LANES * LANES
    off = start - low
    if off == 0:
        return ref[:, low : low + width]
    return ref[:, low : low + width + LANES][:, off : off + width]


def side_column(refs, grid, row, right):
    own, top, bottom = refs
    slot = LAT_DEV if right else 0
    if row < 0:
        ref, lane = top, grid.halo + slot + LAT_DEV - 1
    elif row >= LAT_DEV:
        ref, lane = bottom, grid.halo + slot
    else:
        ref, lane = own, slot + row
    return ref[:, lane : lane + 1]


def take_cells(sources, start, width):
    parts, at, end = [], start, start + width
    for ref, begin, last, lane in sorted(sources, key=lambda source: source[1]):
        shift = lane - begin
        base = (start + shift) // LANES * LANES
        if begin <= start and end <= last and base + width + LANES <= ref.shape[1]:
            return take(ref, start + shift, width)
        low, high = max(at, begin), min(end, last)
        if low < high:
            if low > at:
                parts.append(jnp.zeros((ref.shape[0], low - at), BF16))
            base = (low + shift) // LANES * LANES
            top = min(round_up(high + shift, LANES), ref.shape[1])
            parts.append(ref[:, base:top][:, low + shift - base : high + shift - base])
            at = high
    if at < end:
        parts.append(jnp.zeros((sources[0][0].shape[0], end - at), BF16))
    return jnp.concatenate(parts, axis=1) if len(parts) > 1 else parts[0]


def row_cells(grid, row, sources, top, bottom):
    if row < 0 and top is not None:
        return take_cells([(top, 0, top.shape[1], 0)], grid.halo - grid.columns, grid.pitch)
    if row >= LAT_DEV and bottom is not None:
        return take_cells([(bottom, 0, bottom.shape[1], 0)], 0, grid.pitch)
    return take_cells(sources, row * grid.columns, grid.pitch)


def build_taps(grid, origin, low, high, sources, sides, taps, backwards=False):
    rows = sources[0][0].shape[0]
    own, top, bottom = sides
    for row in range(low, high):
        base = (row - origin) * grid.pitch
        value = row_cells(grid, row, sources, top, bottom)
        left = side_column(sides, grid, row, False)
        right = side_column(sides, grid, row, True)
        before = jnp.concatenate([left, value[:, : grid.pitch - 1]], axis=1)
        after = [value[:, 1 : grid.columns], right]
        if grid.columns < grid.pitch:
            after.append(jnp.zeros((rows, grid.pitch - grid.columns), BF16))
        for b, part in enumerate((before, value, jnp.concatenate(after, axis=1))):
            block = pl.ds((2 - b if backwards else b) * rows, rows)
            taps[block, base : base + grid.pitch] = part


def stacked_rows(grid, taps, row, count, order=(0, 1, 2)):
    width = count * grid.pitch
    return jnp.concatenate(
        [taps[:, (row + a) * grid.pitch : (row + a) * grid.pitch + width] for a in order],
        axis=0,
    )


def groups_of(count, size=ROW_GROUP):
    return [(row, min(size, count - row)) for row in range(0, count, size)]


def flat_piece(grid, pitched, skip, low, high, count):
    parts, at = [], low
    while at < high:
        row, column = divmod(at + skip, grid.columns)
        if row >= count:
            parts.append(jnp.zeros((pitched.shape[0], high - at), BF16))
            break
        size = min(grid.columns - column, high - at)
        begin = row * grid.pitch + column
        parts.append(pitched[:, begin : begin + size])
        at += size
    return jnp.concatenate(parts, axis=1) if len(parts) > 1 else parts[0]


def convolve(grid, first, width, place, sources, sides, taps, weight, bias, pitched, flat,
             backwards=False, emit=None, fetch=None):
    r0, r1 = grid.rows(first, width)
    skip = first - r0 * grid.columns
    taps_row, lane = place
    built, done = r0 - 1, 0
    order = (2, 1, 0) if backwards else (0, 1, 2)
    for row, count in groups_of(r1 - r0):
        ready = min(r0 + row + count + 1 + ROW_GROUP, r1 + 1)
        if fetch is not None:
            fetch(ready)
        build_taps(
            grid, r0 - 1 - taps_row, built, ready, sources, sides, taps, backwards
        )
        built = ready
        stacked = stacked_rows(grid, taps, taps_row + row, count, order)
        value = jnp.dot(weight, stacked, preferred_element_type=F32)
        if bias is not None:
            value = value + bias
        pitched[:, row * grid.pitch : (row + count) * grid.pitch] = value.astype(BF16)
        last = row + count == r1 - r0
        while done < width:
            end = min(done + FLAT_LANES, width)
            if not last and end + skip > row * grid.columns:
                break
            piece = flat_piece(grid, pitched, skip, done, end, r1 - r0)
            flat[:, lane + done : lane + end] = piece
            if emit is not None:
                emit(done, end)
            done = end


def edges_kernel(grid, places, tiles, x_ref, out_ref, row_ref, held, sem, row_sem):
    last = jnp.where(lax.axis_index("lat") == 0, (grid.cells - grid.halo) // LANES, 0)
    row_copy = pltpu.make_async_copy(
        x_ref.at[:, pl.ds(pl.multiple_of(last * LANES, LANES), grid.halo)],
        row_ref,
        row_sem.at[0],
    )
    row_copy.start()
    copies = [
        pltpu.make_async_copy(
            x_ref.at[:, pl.ds(tile * LANES, LANES)],
            held.at[:, pl.ds(number * LANES, LANES)],
            sem.at[number],
        )
        for number, tile in enumerate(tiles)
    ]
    for copy in copies:
        copy.start()
    for copy in copies:
        copy.wait()
    columns = []
    for cell in places:
        at = tiles.index(cell // LANES) * LANES + cell % LANES
        columns.append(held[:, at : at + 1])
    out_ref[...] = jnp.concatenate(columns, axis=1)
    row_copy.wait()


def edges_of(grid, field):
    rows = field.shape[0]
    places = [i for i in range(0, grid.cells, grid.columns)]
    places += [i for i in range(grid.columns - 1, grid.cells, grid.columns)]
    tiles = sorted({cell // LANES for cell in places})
    return pl.pallas_call(
        functools.partial(edges_kernel, grid, places, tiles),
        in_specs=[in_hbm()],
        out_specs=[in_vmem()] * 2,
        out_shape=[shape_of((rows, 2 * LAT_DEV)), shape_of((rows, grid.halo))],
        scratch_shapes=[
            pltpu.VMEM((rows, len(tiles) * LANES), BF16),
            pltpu.SemaphoreType.DMA((len(tiles),)),
            pltpu.SemaphoreType.DMA((1,)),
        ],
        compiler_params=params((rows, (len(tiles) + 1) * LANES + grid.halo, 2)),
        cost_estimate=cost(rows, rows),
        name="edges",
    )(kept_in_hbm(field))


def lon_halo(edges, odd):
    peers = lax.axis_size("lon")
    first, last = edges[:, :LAT_DEV], edges[:, LAT_DEV:]
    if peers % 2:
        right = [(i, (i + 1) % peers) for i in range(peers)]
        left = [(j, i) for i, j in right]
        before, after = lax.ppermute(last, "lon", right), lax.ppermute(first, "lon", left)
        return jnp.concatenate([before, after], axis=1)
    near = [(i, i ^ 1) for i in range(peers)]
    far = [(i, (i + 1 if i % 2 else i - 1) % peers) for i in range(peers)]
    inner = lax.ppermute(jnp.where(odd, first, last), "lon", near)
    outer = lax.ppermute(jnp.where(odd, last, first), "lon", far)
    return jnp.where(
        odd,
        jnp.concatenate([inner, outer], axis=1),
        jnp.concatenate([outer, inner], axis=1),
    )


def lat_halo(first_rows, last_rows, sides, upper, chosen=None):
    peers = lax.axis_size("lat")
    if peers == 2:
        if chosen is None:
            chosen = jnp.where(upper, last_rows, first_rows)
        sent = jnp.concatenate([chosen, sides], axis=1)
        other = lax.ppermute(sent, "lat", [(0, 1), (1, 0)])
        none = jnp.zeros_like(other)
        return jnp.where(upper, none, other), jnp.where(upper, other, none)
    up = [(i, i + 1) for i in range(peers - 1)]
    down = [(j, i) for i, j in up]
    top = lax.ppermute(jnp.concatenate([last_rows, sides], axis=1), "lat", up)
    bottom = lax.ppermute(jnp.concatenate([first_rows, sides], axis=1), "lat", down)
    return top, bottom


def stages_of(grid, ranges):
    stages, got = [], []
    for first, width in ranges:
        r0, r1 = grid.rows(first, width)
        low = max((r0 - 1) * grid.columns - 1, 0) // LANES * LANES
        high = min(round_up((r1 + 1) * grid.columns + 1, LANES), grid.cells)
        low = max([low] + [end for begin, end in got if begin <= low])
        step = round_up(max((high - low) // 3, LANES), LANES)
        stages += [(at, min(at + step, high)) for at in range(low, high, step)]
        got.append((low, high))
    at = 0
    for low, high in sorted(got) + [(grid.cells, grid.cells)]:
        if at < low:
            stages.append((at, low))
        at = max(at, high)
    return stages


def forward_kernel(grid, ranges, has_top, has_bottom, members, load, waits, *refs):
    refs = list(refs)
    x_ref, sides_ref = refs[:2]
    del refs[:2]
    top_ref = refs.pop(0) if has_top else None
    bottom_ref = refs.pop(0) if has_bottom else None
    weight_ref, bias_ref, analysis_ref = refs[:3]
    del refs[: 3 + waits]
    outs = refs[:members]
    target_ref, taps = refs[members : members + 2]
    pitched, pred, target_sem, load_sem = refs[-4:]
    me = lax.axis_index("member")
    places, _, width = grid.layout(ranges)
    piece = width // members
    pending = []
    if load:
        held = refs[members + 2]
        for begin, end in stages_of(grid, ranges):
            copies = []
            for low in range(0, x_ref.shape[0], 32):
                at = (pl.ds(low, min(32, x_ref.shape[0] - low)), pl.ds(begin, end - begin))
                sem = load_sem.at[len(pending), len(copies)]
                copies.append(pltpu.make_async_copy(x_ref.at[at], held.at[at], sem))
                copies[-1].start()
            pending.append((begin, end, copies))
        x_ref = held

    def fetch(low, high):
        for stage in list(pending):
            if stage[0] < high * grid.columns + 1 and stage[1] > low * grid.columns - 1:
                for copy in stage[2]:
                    copy.wait()
                pending.remove(stage)

    each = members // len(ranges)
    index = me // each
    begin = places[0][0] + me * piece
    if len(ranges) > 1:
        begin = jnp.where(index == 0, begin, places[1][0] + (me - each) * piece)
    begin = pl.multiple_of(begin, LANES)
    target_copy = pltpu.make_async_copy(
        analysis_ref.at[:, pl.ds(begin, piece)], target_ref, target_sem.at[0]
    )
    target_copy.start()
    sides = (sides_ref, top_ref, bottom_ref)
    weight, bias = weight_ref[...], bias_ref[...]
    for first, size, r0, r1, row, lane in places:
        convolve(
            grid, first, size, (row, lane), [(x_ref, 0, grid.cells, 0)], sides, taps, weight,
            bias, pitched, pred, fetch=lambda ready, r0=r0: fetch(r0 - 1, ready),
        )
    for d in range(members):
        begin = pl.multiple_of((me ^ d) * piece, LANES)
        outs[d][...] = pred[:, pl.ds(begin, piece)]
    target_copy.wait()
    fetch(0, LAT_DEV)


def forward(
    grid, ranges, members, x, load, sides, top, bottom, weight, bias, analysis, after
):
    channels = x.shape[0]
    fields = weight.shape[0]
    places, tap_rows, width = grid.layout(ranges)
    most = max(place[3] - place[2] for place in places)
    has_top = any(place[2] == 0 for place in places)
    has_bottom = any(place[3] == LAT_DEV for place in places)
    piece = width // members
    held = (3 * channels, tap_rows * grid.pitch)
    operands = [kept_in_hbm(x) if load else kept_in_vmem(x), sides]
    if has_top:
        operands.append(top)
    if has_bottom:
        operands.append(bottom)
    operands += [weight, bias]
    specs = [in_hbm() if load else in_vmem()] + [in_vmem()] * (len(operands) - 1) + [in_hbm()]
    operands += [kept_in_hbm(analysis), *after]
    specs += [anywhere()] * len(after)
    shapes = [shape_of((fields, piece))] * (members + 1) + [pltpu.VMEM(held, BF16)]
    if load:
        shapes.append(pltpu.VMEM((channels, grid.cells), BF16))
    return pl.pallas_call(
        functools.partial(
            forward_kernel, grid, ranges, has_top, has_bottom, members, load, len(after)
        ),
        in_specs=specs,
        out_specs=[in_vmem()] * len(shapes),
        out_shape=shapes,
        scratch_shapes=[
            pltpu.VMEM((fields, most * grid.pitch), BF16),
            pltpu.VMEM((fields, width), BF16),
            pltpu.SemaphoreType.DMA((1,)),
            pltpu.SemaphoreType.DMA((12, -(-channels // 32))),
        ],
        compiler_params=params(
            (2 * fields, most * grid.pitch, 2),
            (2 * fields, 2 * width, 2),
            (fields, 9 * channels, 2),
        ),
        cost_estimate=cost(81 * channels * fields * width, 0),
        name=f"forward_{ranges[0][0]}",
    )(*operands)


def slope(values):
    return values * lax.rsqrt(values * values + 1.0)


def score_kernel(members, target_ref, scale_ref, *refs):
    pieces = refs[:members]
    outs = refs[-members:]
    fields, piece = pieces[0].shape
    tiles = piece // LANES
    several = max(k for k in (1, 2, 3) if tiles % k == 0)

    def tile(index, carry):
        for part in range(several * -(-fields // 16)):
            low = part // several * 16
            at = (index * several + part % several) * LANES
            span = pl.ds(pl.multiple_of(at, LANES), LANES)
            rows = pl.ds(low, min(16, fields - low))
            values = [ref[rows, span].astype(F32) for ref in pieces]
            target = target_ref[rows, span].astype(F32)
            scale = scale_ref[rows, :]
            sums = [None] * members
            for i in range(members):
                for j in range(i + 1, members):
                    both = slope(values[i] - values[j])
                    sums[i] = both if sums[i] is None else sums[i] + both
                    sums[j] = -both if sums[j] is None else sums[j] - both
            for i in range(members):
                grad = slope(values[i] - target) * (1.0 / members) - sums[i] * (
                    1.0 / (members * (members - 1))
                )
                outs[i][rows, span] = (scale * grad).astype(BF16)
        return carry

    lax.fori_loop(0, tiles // several, tile, 0)


def score(first, target, scale, pieces, after):
    members = len(pieces)
    fields, piece = pieces[0].shape
    return pl.pallas_call(
        functools.partial(score_kernel, members),
        in_specs=[in_vmem()] * (2 + members) + [anywhere()] * len(after),
        out_specs=[in_vmem()] * members,
        out_shape=[shape_of((fields, piece))] * members,
        compiler_params=params((9 * round_up(fields, 16), piece, 2), (fields, LANES, 4)),
        cost_estimate=cost(13000 * fields * piece, 0),
        name=f"score_{first}",
    )(target, scale, *pieces, *after)


def gather_kernel(grid, ranges, members, *refs):
    me = lax.axis_index("member")
    pieces = refs[:members]
    out_ref, edge_ref = refs[members:]
    fields, piece = pieces[0].shape
    rows, width = out_ref.shape
    base = fields // 16 * 16
    if base < rows:
        out_ref[pl.ds(base, rows - base), :] = jnp.zeros((rows - base, width), BF16)
    for d in range(members):
        begin = pl.multiple_of((me ^ d) * piece, LANES)
        value = pieces[d][...]
        if grid.padded != grid.cells:
            cell = lax.broadcasted_iota(jnp.int32, (1, piece), 1) + begin
            value = jnp.where(cell < grid.cells, value.astype(F32), 0.0).astype(BF16)
        out_ref[pl.ds(0, fields), pl.ds(begin, piece)] = value
    columns = []
    for side in (0, grid.columns - 1):
        for row in range(LAT_DEV):
            cell = row * grid.columns + side
            for first, size, *_, lane in grid.layout(ranges)[0]:
                if first <= cell < first + size:
                    at = lane + cell - first
                    columns.append(out_ref[:, at : at + 1])
                    break
            else:
                columns.append(jnp.zeros((rows, 1), BF16))
    edge_ref[...] = jnp.concatenate(columns, axis=1)


def gather(grid, ranges, rows, pieces, after):
    members = len(pieces)
    width = members * pieces[0].shape[1]

    def kernel(*refs):
        gather_kernel(grid, ranges, members, *refs[:members], *refs[-2:])

    return pl.pallas_call(
        kernel,
        in_specs=[in_vmem()] * members + [anywhere()] * len(after),
        out_specs=[in_vmem()] * 2,
        out_shape=[shape_of((rows, width)), shape_of((rows, 2 * LAT_DEV))],
        compiler_params=params((rows, 2 * width + 2 * LAT_DEV, 2)),
        cost_estimate=cost(width, 0),
        name=f"gather_{ranges[0][0]}",
    )(*pieces, *after)


def weight_kernel(grid, ranges, chained, waits, halves, taps, part_ref, *refs):
    before_ref = refs[0] if chained else None
    refs = refs[chained + waits :]
    pitched, sum_ref = refs[-1], refs[-2]
    rows = part_ref.shape[0]
    keep = jnp.where(
        lax.broadcasted_iota(jnp.int32, (1, LANES), 1) < grid.columns % LANES, 1.0, 0.0
    ).astype(BF16)
    started = False
    for first, width, r0, r1, taps_row, place in grid.layout(ranges)[0]:
        source = [(part_ref, first, first + width, place)]
        for row, count in groups_of(r1 - r0):
            for at in range(row, row + count):
                value = take_cells(source, (r0 + at) * grid.columns, grid.pitch)
                to = at * grid.pitch
                for lane in range(0, grid.pitch, LANES):
                    part = value[:, lane : lane + LANES]
                    if lane + LANES > grid.columns:
                        part = part * keep
                    pitched[:, to + lane : to + lane + LANES] = part
            stacked = stacked_rows(grid, taps, taps_row + row, count)
            lanes = round_up(stacked.shape[0] + 1, LANES)
            ones = jnp.ones((lanes - stacked.shape[0], stacked.shape[1]), BF16)
            part = nt_dot(
                pitched[:, row * grid.pitch : (row + count) * grid.pitch],
                jnp.concatenate([stacked, ones], axis=0),
            )
            if started:
                sum_ref[:, :lanes] += part
            else:
                sum_ref[:, :lanes] = part + before_ref[:, :lanes] if chained else part
            started = True
    if lanes < sum_ref.shape[1]:
        sum_ref[:, lanes:] = jnp.zeros((rows, sum_ref.shape[1] - lanes), F32)
    if halves:
        keep_ref, send_ref = refs[:2]
        half = rows // 2
        upper = lax.axis_index("lat") & 1
        keep_ref[...] = sum_ref[pl.ds(pl.multiple_of(upper * half, 8), half), :]
        send_ref[...] = sum_ref[pl.ds(pl.multiple_of((1 - upper) * half, 8), half), :]


def weight_part(grid, ranges, members, taps, part, before, after, halves):
    rows = part.shape[0]
    channels = taps.shape[0] // 3
    places, _, width = grid.layout(ranges)
    most = max(place[3] - place[2] for place in places)
    sums = round_up(9 * channels + 1, members * LANES)
    chained = [] if before is None else [before]
    whole = []
    if halves:
        shapes = [shape_of((rows // 2, sums), F32)] * 2
        whole = [pltpu.VMEM((rows, sums), F32)]
    else:
        shapes = [shape_of((rows, sums), F32)]
    return pl.pallas_call(
        functools.partial(weight_kernel, grid, ranges, len(chained), len(after), halves),
        in_specs=[in_vmem()] * (2 + len(chained)) + [anywhere()] * len(after),
        out_specs=[in_vmem()] * len(shapes),
        out_shape=shapes,
        scratch_shapes=whole + [pltpu.VMEM((rows, most * grid.pitch), BF16)],
        compiler_params=params(
            (rows, width, 2),
            (rows, most * grid.pitch, 2),
            (rows, 3 * sums, 4),
        ),
        cost_estimate=cost(width, 0),
        name=f"weight_{ranges[0][0]}",
    )(kept_in_vmem(taps), part, *chained, *after)


def input_kernel(grid, r0, r1, chunks, aliased, *refs):
    refs = list(refs)
    parts = refs[: len(chunks)]
    del refs[: len(chunks)]
    sides_ref, weight_ref = refs[:2]
    del refs[:2]
    top_ref = refs.pop(0) if r0 == 0 else None
    bottom_ref = refs.pop(0) if r1 == LAT_DEV else None
    del refs[:aliased]
    out_ref, taps, pitched, flat, out_sem = refs
    sources = []
    for ref, ranges in zip(parts, chunks):
        for first, width, *_, lane in grid.layout(ranges)[0]:
            sources.append((ref, first, min(first + width, grid.cells), lane))
    sides = (sides_ref, top_ref, bottom_ref)
    copies = []

    def emit(low, high):
        at = r0 * grid.columns + low
        copies.append(
            pltpu.make_async_copy(
                flat.at[:, pl.ds(low, high - low)],
                out_ref.at[:, pl.ds(at, high - low)],
                out_sem.at[len(copies)],
            )
        )
        copies[-1].start()

    width = (r1 - r0) * grid.columns
    convolve(
        grid, r0 * grid.columns, width, (0, 0), sources, sides, taps, weight_ref[...], None,
        pitched, flat, backwards=True, emit=emit,
    )
    for copy in copies:
        copy.wait()


def input_part(grid, r0, r1, chunks, parts, sides, top, bottom, weight, before, slow):
    rows = parts[0].shape[0]
    channels = weight.shape[0]
    width = (r1 - r0) * grid.columns
    held = (3 * rows, (r1 - r0 + 2) * grid.pitch)
    begin, end = (r0 - 1) * grid.columns - 1, (r1 + 1) * grid.columns + 1
    near = [
        (ranges, part)
        for ranges, part in zip(chunks, parts)
        if any(first < end and first + size > begin for first, size in ranges)
    ]
    chunks, parts = [pair[0] for pair in near], [pair[1] for pair in near]
    operands = [*parts, sides, weight] + [top] * (r0 == 0) + [bottom] * (r1 == LAT_DEV)
    specs = [in_vmem()] * len(operands)
    alias = {}
    if before is not None:
        alias = {len(operands): 0}
        operands.append(before)
        specs.append(anywhere())
    return pl.pallas_call(
        functools.partial(input_kernel, grid, r0, r1, chunks, len(alias)),
        in_specs=specs,
        out_specs=anywhere(),
        out_shape=shape_of((channels, grid.cells)),
        input_output_aliases=alias,
        scratch_shapes=[
            pltpu.VMEM(held, BF16),
            pltpu.VMEM((channels, (r1 - r0) * grid.pitch), BF16),
            pltpu.VMEM((channels, width), BF16),
            pltpu.SemaphoreType.DMA((-(-width // FLAT_LANES),)),
        ],
        compiler_params=params(
            (rows, sum(part.shape[1] for part in parts), 2),
            (*held, 2),
            (2 * channels, (r1 - r0) * grid.pitch, 2),
            (channels, 9 * rows, 2),
        ),
        cost_estimate=cost((80 if slow else 1) * channels * rows * width, width),
        name=f"input_{r0}",
    )(*operands)


def split_kernel(members, count, *refs):
    me = lax.axis_index("member")
    lanes = refs[count].shape[1]
    for d in range(members):
        span = pl.ds(pl.multiple_of((me ^ d) * lanes, LANES), lanes)
        total = refs[0][:, span]
        for ref in refs[1:count]:
            total += ref[:, span]
        refs[count + d][...] = total


def split_by_member(values, members):
    rows, lanes = values[0].shape
    return pl.pallas_call(
        functools.partial(split_kernel, members, len(values)),
        in_specs=[in_vmem()] * len(values),
        out_specs=[in_vmem()] * members,
        out_shape=[shape_of((rows, lanes // members), F32)] * members,
        compiler_params=params((rows, 3 * lanes, 4)),
        cost_estimate=cost(rows * lanes, 12 * rows * lanes),
        name="split",
    )(*values)


def join_kernel(members, *refs):
    me = lax.axis_index("member")
    lanes = refs[0].shape[1]
    for d in range(members):
        span = pl.ds(pl.multiple_of((me ^ d) * lanes, LANES), lanes)
        refs[members][:, span] = refs[d][...]


def join_members(pieces):
    members = len(pieces)
    rows, lanes = pieces[0].shape
    return pl.pallas_call(
        functools.partial(join_kernel, members),
        in_specs=[in_vmem()] * members,
        out_specs=in_vmem(),
        out_shape=shape_of((rows, members * lanes), F32),
        compiler_params=params((rows, 2 * members * lanes, 4)),
        cost_estimate=cost(rows * lanes, 12 * rows * lanes),
        name="join",
    )(*pieces)


def swap(value, axis, bits):
    return lax.ppermute(value, axis, [(i, i ^ bits) for i in range(lax.axis_size(axis))])


def sum_axis(value, axis, bit):
    size = lax.axis_size(axis)
    while bit < size:
        if 2 * bit < size:
            near, far, both = [swap(value, axis, k * bit) for k in (1, 2, 3)]
            value = (value + near) + (far + both)
        else:
            value = value + swap(value, axis, bit)
        bit *= 4
    return value


def sum_all(keep, send, upper, late):
    members = lax.axis_size("member")
    other = swap(send, "lat", 1)
    values = [keep, other]
    if lax.axis_size("lat") > 2:
        values = [sum_axis(keep + other, "lat", 2)]
    pieces = split_by_member(values, members)
    moved = [swap(pieces[d], "member", d) for d in range(1, members)]
    value = functools.reduce(jnp.add, moved, pieces[0])
    value, late = lax.optimization_barrier((value, late))
    value = sum_axis(value, "lon", 1)
    half = join_members([value] + [swap(value, "member", d) for d in range(1, members)])
    other = swap(half, "lat", 1)
    total = jnp.where(
        upper,
        jnp.concatenate([other, half], axis=0),
        jnp.concatenate([half, other], axis=0),
    )
    return total, late


def weights_kernel(taps_ref, forward_ref, backward_ref):
    count, channels, fields = taps_ref.shape
    rows = backward_ref.shape[1] // count
    taps = [taps_ref[t] for t in range(count)]
    forward_ref[...] = jnp.concatenate(
        [tap.astype(F32).T for tap in taps], axis=1
    ).astype(BF16)
    none = [jnp.zeros((channels, rows - fields), BF16)] * (rows > fields)
    backward_ref[...] = jnp.concatenate([part for tap in taps for part in (tap, *none)], axis=1)


def prepare_weights(taps, rows):
    count, channels, fields = taps.shape
    return pl.pallas_call(
        weights_kernel,
        in_specs=[in_vmem()],
        out_specs=[in_vmem()] * 2,
        out_shape=[shape_of((fields, count * channels)), shape_of((channels, count * rows))],
        compiler_params=params((4 * channels, count * LANES, 4)),
        cost_estimate=cost(channels, 8 * count * channels * rows),
        name="weights",
    )(taps)


def chunks_of(grid, members):
    unit = members * LANES
    units = grid.padded // unit
    if units < 15 or grid.padded != grid.cells or members % 2:
        return [[(0, grid.padded)]]
    outer = (units // 2 + 2) // 2 * unit
    return [
        [(0, outer), (grid.cells - outer, outer)],
        [(outer, grid.cells - 2 * outer)],
    ]


def parts_of(grid, wanted):
    step = LAT_DEV // wanted
    if step * grid.columns % LANES:
        return [(0, LAT_DEV)]
    ranges = [(row, row + step) for row in range(0, LAT_DEV, step)]
    return ranges[1:-1] + [ranges[0], ranges[-1]]


def local(inputs, weight, bias, analysis, field_weight):
    channels, cells = inputs.shape[1], inputs.shape[4]
    fields = analysis.shape[0]
    members = lax.axis_size("member")
    grid = Grid(cells, members)
    x = inputs.reshape(channels, cells)
    target = analysis.reshape(fields, cells)
    if grid.padded != cells:
        target = jnp.pad(target, ((0, 0), (0, grid.padded - cells)))
    rows = round_up(fields, 16)
    taps = weight.reshape(9, channels, fields)
    forward_weight, backward_weight = prepare_weights(taps, rows)
    scale = jnp.broadcast_to(field_weight[:, None], (fields, LANES))
    shift = bias[:, None]
    upper = (lax.axis_index("lat") & 1) != 0
    odd = (lax.axis_index("lon") & 1) != 0
    x_edges, x_row = edges_of(grid, x)
    x_sides = lon_halo(x_edges, odd)
    x_sides, forward_weight, backward_weight, scale, shift, upper, odd = (
        lax.optimization_barrier(
            (x_sides, forward_weight, backward_weight, scale, shift, upper, odd)
        )
    )
    first_lat = jnp.logical_not(upper)
    def to_members(pieces):
        moved = {0: pieces[0]}
        for d in range(members - 1, 0, -1):
            moved[d] = swap(pieces[d], "member", d)
        return [moved[d] for d in range(members)]

    chunks = chunks_of(grid, members)
    x_top, x_bottom = lat_halo(
        x[:, : grid.halo], x[:, cells - grid.halo :], x_sides, first_lat, x_row
    )
    received, targets, taken, held = [], [], [], None
    for ranges in chunks:
        out = forward(
            grid, ranges, members, x if held is None else held, held is None, x_sides, x_top,
            x_bottom, forward_weight, shift, target, [],
        )
        targets.append(out[members])
        taken.append(out[members + 1])
        held = out[members + 2] if held is None else held
        received.append(to_members(out[:members]))
    returned = []
    for ranges, pieces, goal in zip(chunks, received, targets):
        grads = score(ranges[0][0], goal, scale, pieces, targets[-1:])
        returned.append(to_members(grads))

    blocks = parts_of(grid, 4)
    parts, edges, sums, grad_input = [], [], [None], None
    for number, ranges in enumerate(chunks):
        final = number == len(chunks) - 1
        after = [returned[-1][0]] if number == 0 else [kept_in_hbm(grad_input)]
        part, edge = gather(grid, ranges, rows, returned[number], after)
        sums = list(
            weight_part(grid, ranges, members, taken[number], part, sums[0], [], final)
        )
        parts.append(part)
        edges.append(edge)
        if number == 0:
            end = part.shape[1] - grid.padded + cells
            outer_rows = (part[:, : grid.halo], part[:, end - grid.halo : end])
        if final:
            break
        g_sides = lon_halo(edge, odd)
        g_sides, sums[0] = lax.optimization_barrier((g_sides, sums[0]))
        g_top, g_bottom = lat_halo(*outer_rows, g_sides, first_lat)
        for _ in range(2):
            grad_input = input_part(
                grid, *blocks.pop(), chunks[:1], parts[:1], g_sides, g_top, g_bottom,
                backward_weight, grad_input, False,
            )
    total, late_edges = sum_all(*sums, upper, edges[-1])
    late_sides = lon_halo(late_edges, odd)
    if len(chunks) == 1:
        g_top, g_bottom = lat_halo(*outer_rows, late_sides, first_lat)
    else:
        late_sides = late_sides + g_sides
    for r0, r1 in blocks:
        grad_input = input_part(
            grid, r0, r1, chunks, parts, late_sides, g_top, g_bottom, backward_weight,
            grad_input, True,
        )
    total = total / (cells * lax.axis_size("lat") * lax.axis_size("lon"))
    grad_weight = total[:fields, : 9 * channels].T.reshape(9, channels * fields)
    grad_bias = total[:fields, 9 * channels]
    return (grad_input.reshape(1, channels, 1, 1, cells), grad_weight, grad_bias)


def solution(mesh):
    placed = (P("member", None, "lat", "lon", None), P(), P(), P(None, "lat", "lon", None), P())
    return jax.shard_map(
        local,
        mesh=mesh,
        in_specs=placed,
        out_specs=(P("member", None, "lat", "lon", None), P(), P()),
        check_vma=False,
    )
```

profile of v0, /device:TPU:0, one launch (start us, length us, event | category | flops | bytes accessed | tf_op | source)
XLA Modules:
  0.0 150.6 jit_solution(7442178722716768917)
XLA Ops:
  0.7 3.0 %edges.1 = (bf16[96,128]{1,0:T(8,128)(2,1)S(1)}, bf16[96,384]{1,0:T(8,128)(2,1)S(1)}) custom-call(bf16[96,23040]{1,0:T(8,128)(2,1)} %bitcast.7), custom_call_target="tpu_custom_call" | custom-call | flops 96 | bytes 96 | tf_op jit(solution)/shard_map/edges/pallas_call | solution.py:240
  3.8 3.0 %collective-permute-start = (bf16[96,64]{1,0:T(8,128)(2,1)S(1)}, bf16[96,64]{1,0:T(8,128)(2,1)S(1)}, u32[]{:S(2)}, u32[]{:S(2)}) collective-permute-start(bf16[96,64]{1,0:T(8,128)(2,1)S(1)} %get-tuple-element.103), channel_id=1, source_target_pairs={{0,1},{1,0},{2,3},{3,2},{4,5},{5,4},{6,7},{7,6},{8,9},{9,8},{10,11... | collective-permute-start | bytes 36872 | tf_op jit(solution)/shard_map/ppermute | solution.py:266
  6.8 2.5 %collective-permute-start.1 = (bf16[96,64]{1,0:T(8,128)(2,1)S(1)}, bf16[96,64]{1,0:T(8,128)(2,1)S(1)}, u32[]{:S(2)}, u32[]{:S(2)}) collective-permute-start(bf16[96,64]{1,0:T(8,128)(2,1)S(1)} %get-tuple-element.104), channel_id=1, source_target_pairs={{0,3},{1,2},{2,1},{3,0},{4,7},{5,6},{6,5},{7,4},{8,11},{9,10},{10,... | collective-permute-start | bytes 36872 | tf_op jit(solution)/shard_map/ppermute | solution.py:267
  9.3 0.8 reshape.23.taps_ref
  10.4 2.1 %collective-permute-done.1 = bf16[96,64]{1,0:T(8,128)(2,1)S(1)} collective-permute-done((bf16[96,64]{1,0:T(8,128)(2,1)S(1)}, bf16[96,64]{1,0:T(8,128)(2,1)S(1)}, u32[]{:S(2)}, u32[]{:S(2)}) %collective-permute-start.1) | collective-permute-done | bytes 12320 | tf_op jit(solution)/shard_map/ppermute | solution.py:267
  12.9 1.2 collective-permute-done.2
  14.0 7.4 %forward_0.1 = (bf16[84,3072]{1,0:T(8,128)(2,1)S(1)}, bf16[84,3072]{1,0:T(8,128)(2,1)S(1)}, bf16[84,3072]{1,0:T(8,128)(2,1)S(1)}, bf16[84,3072]{1,0:T(8,128)(2,1...) custom-call(bf16[96,23040]{1,0:T(8,128)(2,1)} %bitcast.8, ...), custom_call_target="tpu_custom_call" | custom-call | flops 8026324992 | tf_op jit(solution)/shard_map/forward_0/pallas_call | solution.py:390
  21.5 1.6 %collective-permute-start.3 = (bf16[84,3072]{1,0:T(8,128)(2,1)S(1)}, bf16[84,3072]{1,0:T(8,128)(2,1)S(1)}, u32[]{:S(2)}, u32[]{:S(2)}) collective-permute-start(bf16[84,3072]{1,0:T(8,128)(2,1)S(1)} %get-tuple-element.60), channel_id=1, source_target_pairs={{0,8},{8,0},{16,24},{24,16},{1,9},{9,1},{17,25},{25,17},{2,10},{10... | collective-permute-start | bytes 1548296 | tf_op jit(solution)/shard_map/ppermute | solution.py:708
  23.0 1.5 %collective-permute-start.4 = (bf16[84,3072]{1,0:T(8,128)(2,1)S(1)}, bf16[84,3072]{1,0:T(8,128)(2,1)S(1)}, u32[]{:S(2)}, u32[]{:S(2)}) collective-permute-start(bf16[84,3072]{1,0:T(8,128)(2,1)S(1)} %get-tuple-element.61), channel_id=1, source_target_pairs={{0,16},{8,24},{16,0},{24,8},{1,17},{9,25},{17,1},{25,9},{2,18},{10... | collective-permute-start | bytes 1548296 | tf_op jit(solution)/shard_map/ppermute | solution.py:708
  25.0 5.4 %forward_6144.1 = (bf16[84,2688]{1,0:T(8,128)(2,1)S(1)}, bf16[84,2688]{1,0:T(8,128)(2,1)S(1)}, bf16[84,2688]{1,0:T(8,128)(2,1)S(1)}, bf16[84,2688]{1,0:T(8,128)(...) custom-call(bf16[96,23040]{1,0:T(8,128)(2,1)S(1)} %get-tuple-element.63.refs_0_, ...), custom_call_target="tpu_custom_call" | custom-call | flops 7023034368 | tf_op jit(solution)/shard_map/forward_6144/pallas_call | solution.py:390
  30.4 1.6 %collective-permute-start.9 = (bf16[84,2688]{1,0:T(8,128)(2,1)S(1)}, bf16[84,2688]{1,0:T(8,128)(2,1)S(1)}, u32[]{:S(2)}, u32[]{:S(2)}) collective-permute-start(bf16[84,2688]{1,0:T(8,128)(2,1)S(1)} %get-tuple-element.70), channel_id=1, source_target_pairs={{0,8},{8,0},{16,24},{24,16},{1,9},{9,1},{17,25},{25,17},{2,10},{10... | collective-permute-start | bytes 1354760 | tf_op jit(solution)/shard_map/ppermute | solution.py:708
  32.0 1.5 %collective-permute-start.10 = (bf16[84,2688]{1,0:T(8,128)(2,1)S(1)}, bf16[84,2688]{1,0:T(8,128)(2,1)S(1)}, u32[]{:S(2)}, u32[]{:S(2)}) collective-permute-start(bf16[84,2688]{1,0:T(8,128)(2,1)S(1)} %get-tuple-element.71), channel_id=1, source_target_pairs={{0,16},{8,24},{16,0},{24,8},{1,17},{9,25},{17,1},{25,9},{2,18},{10... | collective-permute-start | bytes 1354760 | tf_op jit(solution)/shard_map/ppermute | solution.py:708
  33.5 3.1 %collective-permute-done.3.refs_1_ = bf16[84,3072]{1,0:T(8,128)(2,1)S(1)} collective-permute-done((bf16[84,3072]{1,0:T(8,128)(2,1)S(1)}, bf16[84,3072]{1,0:T(8,128)(2,1)S(1)}, u32[]{:S(2)}, u32[]{:S(2)}) %collective-permute-start.3) | collective-permute-done | bytes 516128 | tf_op jit(solution)/shard_map/ppermute | solution.py:708
  36.7 2.5 %collective-permute-start.11 = (bf16[84,2688]{1,0:T(8,128)(2,1)S(1)}, bf16[84,2688]{1,0:T(8,128)(2,1)S(1)}, u32[]{:S(2)}, u32[]{:S(2)}) collective-permute-start(bf16[84,2688]{1,0:T(8,128)(2,1)S(1)} %get-tuple-element.72), channel_id=1, source_target_pairs={{0,24},{8,16},{16,8},{24,0},{1,25},{9,17},{17,9},{25,1},{2,26},{10... | collective-permute-start | bytes 1354760 | tf_op jit(solution)/shard_map/ppermute | solution.py:708
  39.1 10.6 %collective-permute-done.4.refs_2_ = bf16[84,3072]{1,0:T(8,128)(2,1)S(1)} collective-permute-done((bf16[84,3072]{1,0:T(8,128)(2,1)S(1)}, bf16[84,3072]{1,0:T(8,128)(2,1)S(1)}, u32[]{:S(2)}, u32[]{:S(2)}) %collective-permute-start.4) | collective-permute-done | bytes 516128 | tf_op jit(solution)/shard_map/ppermute | solution.py:708
  49.8 3.1 %score_0.1 = (bf16[84,3072]{1,0:T(8,128)(2,1)S(1)}, bf16[84,3072]{1,0:T(8,128)(2,1)S(1)}, bf16[84,3072]{1,0:T(8,128)(2,1)S(1)}, bf16[84,3072]{1,0:T(8,128)(2,1)S(1)}) custom-call(bf16[84,3072]{1,0:T(8,128)(2,1)S(1)} %get-tuple-element.57.target_ref, f32[84,128]{1,0:T(8,128)S(1)} %broadcast_in_dim.4.scale_ref, ...), custom_call_target="tpu_custom_call" | custom-call | flops 3354624000 | tf_op jit(solution)/shard_map/score_0/pallas_call | solution.py:452
  52.9 1.0 collective-permute-start.6
  54.0 1.1 collective-permute-start.7
  55.0 3.4 %collective-permute-done.9.refs_1_ = bf16[84,2688]{1,0:T(8,128)(2,1)S(1)} collective-permute-done((bf16[84,2688]{1,0:T(8,128)(2,1)S(1)}, bf16[84,2688]{1,0:T(8,128)(2,1)S(1)}, u32[]{:S(2)}, u32[]{:S(2)}) %collective-permute-start.9) | collective-permute-done | bytes 451616 | tf_op jit(solution)/shard_map/ppermute | solution.py:708
  58.4 2.5 %collective-permute-start.8 = (bf16[84,3072]{1,0:T(8,128)(2,1)S(1)}, bf16[84,3072]{1,0:T(8,128)(2,1)S(1)}, u32[]{:S(2)}, u32[]{:S(2)}) collective-permute-start(bf16[84,3072]{1,0:T(8,128)(2,1)S(1)} %get-tuple-element.68), channel_id=1, source_target_pairs={{0,24},{8,16},{16,8},{24,0},{1,25},{9,17},{17,9},{25,1},{2,26},{10... | collective-permute-start | bytes 1548296 | tf_op jit(solution)/shard_map/ppermute | solution.py:708
  60.9 9.2 %collective-permute-done.10.refs_2_ = bf16[84,2688]{1,0:T(8,128)(2,1)S(1)} collective-permute-done((bf16[84,2688]{1,0:T(8,128)(2,1)S(1)}, bf16[84,2688]{1,0:T(8,128)(2,1)S(1)}, u32[]{:S(2)}, u32[]{:S(2)}) %collective-permute-start.10) | collective-permute-done | bytes 451616 | tf_op jit(solution)/shard_map/ppermute | solution.py:708
  70.1 2.9 %score_6144.1 = (bf16[84,2688]{1,0:T(8,128)(2,1)S(1)}, bf16[84,2688]{1,0:T(8,128)(2,1)S(1)}, bf16[84,2688]{1,0:T(8,128)(2,1)S(1)}, bf16[84,2688]{1,0:T(8,128)(2,1)S(1)}) custom-call(bf16[84,2688]{1,0:T(8,128)(2,1)S(1)} %get-tuple-element.64.refs_4_.target_ref, f32[84,128]{1,0:T(8,128)S(1)} %broadcast_in_dim.4.scale_ref, ...), custom_call_target="tpu_custom_call" | custom-call | flops 2935296000 | tf_op jit(solution)/shard_map/score_6144/pallas_call | solution.py:452
  72.9 1.1 collective-permute-start.12
  74.0 1.0 collective-permute-start.13
  75.1 5.1 %collective-permute-done.6.refs_1_ = bf16[84,3072]{1,0:T(8,128)(2,1)S(1)} collective-permute-done((bf16[84,3072]{1,0:T(8,128)(2,1)S(1)}, bf16[84,3072]{1,0:T(8,128)(2,1)S(1)}, u32[]{:S(2)}, u32[]{:S(2)}) %collective-permute-start.6) | collective-permute-done | bytes 516128 | tf_op jit(solution)/shard_map/ppermute | solution.py:708
  80.2 2.5 %collective-permute-start.14 = (bf16[84,2688]{1,0:T(8,128)(2,1)S(1)}, bf16[84,2688]{1,0:T(8,128)(2,1)S(1)}, u32[]{:S(2)}, u32[]{:S(2)}) collective-permute-start(bf16[84,2688]{1,0:T(8,128)(2,1)S(1)} %get-tuple-element.77), channel_id=1, source_target_pairs={{0,24},{8,16},{16,8},{24,0},{1,25},{9,17},{17,9},{25,1},{2,26},{10... | collective-permute-start | bytes 1354760 | tf_op jit(solution)/shard_map/ppermute | solution.py:708
  82.7 10.6 %collective-permute-done.7.refs_2_ = bf16[84,3072]{1,0:T(8,128)(2,1)S(1)} collective-permute-done((bf16[84,3072]{1,0:T(8,128)(2,1)S(1)}, bf16[84,3072]{1,0:T(8,128)(2,1)S(1)}, u32[]{:S(2)}, u32[]{:S(2)}) %collective-permute-start.7) | collective-permute-done | bytes 516128 | tf_op jit(solution)/shard_map/ppermute | solution.py:708
  94.0 2.5 %collective-permute-start.16 = (bf16[96,64]{1,0:T(8,128)(2,1)S(1)}, bf16[96,64]{1,0:T(8,128)(2,1)S(1)}, u32[]{:S(2)}, u32[]{:S(2)}) collective-permute-start(bf16[96,64]{1,0:T(8,128)(2,1)S(1)} %get-tuple-element.102), channel_id=1, source_target_pairs={{0,3},{1,2},{2,1},{3,0},{4,7},{5,6},{6,5},{7,4},{8,11},{9,10},{10,... | collective-permute-start | bytes 36872 | tf_op jit(solution)/shard_map/ppermute | solution.py:267
  96.6 7.3 %weight_0.1.refs_0_ = f32[96,1024]{1,0:T(8,128)S(1)} custom-call(bf16[288,15360]{1,0:T(8,128)(2,1)S(1)} %get-tuple-element.80.taps, bf16[96,12288]{1,0:T(8,128)(2,1)S(1)} %get-tuple-element.74.part_ref.refs_0_), custom_call_target="tpu_custom_call" | custom-call | flops 12288 | tf_op jit(solution)/shard_map/weight_0/pallas_call | solution.py:566
  104.1 1.3 collective-permute-done.17
  105.4 3.2 %input_48.1.refs_4_ = bf16[96,23040]{1,0:T(8,128)(2,1)} custom-call(bf16[96,12288]{1,0:T(8,128)(2,1)S(1)} %get-tuple-element.74.part_ref.refs_0_, bf16[96,128]{1,0:T(8,128)(2,1)S(1)} %maximum_select_fusion.2.refs_1_, bf16[96,864]{1,0:T(8,128)(2,1)S(1)} %get-tuple-element.82.refs_2_.refs_3_, bf16[96,512]{1,0:T(8,128)(2,1)S(1)} %get-tuple-element.95.refs_3_), custom_call_target="tpu_custom_call" | custom-call | flops 53084160 | bytes 5760 | tf_op jit(solution)/shard_map/input_48/pallas_call | solution.py:638
  108.7 3.2 %input_0.1.refs_4_ = bf16[96,23040]{1,0:T(8,128)(2,1)} custom-call(bf16[96,12288]{1,0:T(8,128)(2,1)S(1)} %get-tuple-element.74.part_ref.refs_0_, bf16[96,128]{1,0:T(8,128)(2,1)S(1)} %maximum_select_fusion.2.refs_1_, bf16[96,864]{1,0:T(8,128)(2,1)S(1)} %get-tuple-element.82.refs_2_.refs_3_, ...), custom_call_target="tpu_custom_call", output_to_operand_aliasing={{}: (4, {})} | custom-call | flops 53084160 | bytes 5760 | tf_op jit(solution)/shard_map/input_0/pallas_call | solution.py:638
  113.0 6.5 %weight_6144.1 = (f32[48,1024]{1,0:T(8,128)S(1)}, f32[48,1024]{1,0:T(8,128)S(1)}) custom-call(bf16[288,12288]{1,0:T(8,128)(2,1)S(1)} %get-tuple-element.84.taps, bf16[96,10752]{1,0:T(8,128)(2,1)S(1)} %get-tuple-element.83.part_ref.refs_1_, f32[96,1024]{1,0:T(8,128)S(1)} %weight_0.1.refs_0_), custom_call_target="tpu_custom_call" | custom-call | flops 10752 | tf_op jit(solution)/shard_map/weight_6144/pallas_call | solution.py:566
  119.6 1.4 collective-permute-done.18.refs_1_
  121.0 1.5 collective-permute-start.19
  123.1 1.4 collective-permute-start.21
  125.2 1.9 %collective-permute-done.20 = f32[48,256]{1,0:T(8,128)S(1)} collective-permute-done((f32[48,256]{1,0:T(8,128)S(1)}, f32[48,256]{1,0:T(8,128)S(1)}, u32[]{:S(2)}, u32[]{:S(2)}) %collective-permute-start.20) | collective-permute-done | bytes 49184 | tf_op jit(solution)/shard_map/ppermute | solution.py:708
  127.1 1.0 collective-permute-done.21
  128.9 1.9 %collective-permute-start.23 = (bf16[96,64]{1,0:T(8,128)(2,1)S(1)}, bf16[96,64]{1,0:T(8,128)(2,1)S(1)}, u32[]{:S(2)}, u32[]{:S(2)}) collective-permute-start(bf16[96,64]{1,0:T(8,128)(2,1)S(1)} %get-tuple-element.100), channel_id=1, source_target_pairs={{0,3},{1,2},{2,1},{3,0},{4,7},{5,6},{6,5},{7,4},{8,11},{9,10},{10,... | collective-permute-start | bytes 36872 | tf_op jit(solution)/shard_map/ppermute | solution.py:267
  130.8 1.9 %collective-permute-start.26 = (f32[48,256]{1,0:T(8,128)S(1)}, f32[48,256]{1,0:T(8,128)S(1)}, u32[]{:S(2)}, u32[]{:S(2)}) collective-permute-start(f32[48,256]{1,0:T(8,128)S(1)} %add_add_fusion.1), channel_id=1, source_target_pairs={{0,3},{1,2},{2,1},{3,0},{4,7},{5,6},{6,5},{7,4},{8,11},{9,10},{10,... | collective-permute-start | bytes 147464 | tf_op jit(solution)/shard_map/ppermute | solution.py:708
  133.3 1.9 %collective-permute-start.24 = (f32[48,256]{1,0:T(8,128)S(1)}, f32[48,256]{1,0:T(8,128)S(1)}, u32[]{:S(2)}, u32[]{:S(2)}) collective-permute-start(f32[48,256]{1,0:T(8,128)S(1)} %add_add_fusion.1), channel_id=1, source_target_pairs={{0,1},{1,0},{2,3},{3,2},{4,5},{5,4},{6,7},{7,6},{8,9},{9,8},{10,11... | collective-permute-start | bytes 147464 | tf_op jit(solution)/shard_map/ppermute | solution.py:708
  135.3 1.4 collective-permute-done.26
  136.7 1.2 collective-permute-done.25
  137.9 1.5 collective-permute-start.29
  139.5 1.5 %collective-permute-start.28 = (f32[48,256]{1,0:T(8,128)S(1)}, f32[48,256]{1,0:T(8,128)S(1)}, u32[]{:S(2)}, u32[]{:S(2)}) collective-permute-start(f32[48,256]{1,0:T(8,128)S(1)} %add_add_fusion.refs_0_), channel_id=1, source_target_pairs={{0,16},{8,24},{16,0},{24,8},{1,17},{9,25},{17,1},{25,9},{2,18},{10... | collective-permute-start | bytes 147464 | tf_op jit(solution)/shard_map/ppermute | solution.py:708
  141.5 3.3 %input_16.1.refs_4_ = bf16[96,23040]{1,0:T(8,128)(2,1)} custom-call(bf16[96,12288]{1,0:T(8,128)(2,1)S(1)} %get-tuple-element.74.part_ref.refs_0_, bf16[96,10752]{1,0:T(8,128)(2,1)S(1)} %get-tuple-element.83.part_ref.refs_1_, bf16[96,128]{1,0:T(8,128)(2,1)S(1)} %fusion.1.refs_2_, ...), custom_call_target="tpu_custom_call", output_to_operand_aliasing={{}: (4, {})} | custom-call | flops 4246732800 | bytes 5760 | tf_op jit(solution)/shard_map/input_16/pallas_call | solution.py:638
  145.2 3.2 %input_32.1 = bf16[96,23040]{1,0:T(8,128)(2,1)} custom-call(bf16[96,12288]{1,0:T(8,128)(2,1)S(1)} %get-tuple-element.74.part_ref.refs_0_, bf16[96,10752]{1,0:T(8,128)(2,1)S(1)} %get-tuple-element.83.part_ref.refs_1_, bf16[96,128]{1,0:T(8,128)(2,1)S(1)} %fusion.1.refs_2_, ...), custom_call_target="tpu_custom_call", output_to_operand_aliasing={{}: (4, {})} | custom-call | flops 4246732800 | bytes 5760 | tf_op jit(solution)/shard_map/input_32/pallas_call | solution.py:638
  149.4 1.2 reshape.26
  (57 shorter events, 8.0 us)
Async XLA Ops:
  0.6 8.7 %copy-start = (bf16[9,8064]{1,0:T(8,128)(2,1)S(1)}, bf16[9,8064]{1,0:T(8,128)(2,1)}, u32[]{:S(2)}) copy-start(bf16[9,8064]{1,0:T(8,128)(2,1)} %param.6) | copy-start | bytes 435460
  0.6 12.1 %copy-start.2 = (f32[84]{0:T(128)S(1)}, f32[84]{0:T(128)}, u32[]{:S(2)}) copy-start(f32[84]{0:T(128)} %param.7) | copy-start | bytes 1012
  0.7 11.9 %copy-start.1 = (f32[84]{0:T(128)S(1)}, f32[84]{0:T(128)}, u32[]{:S(2)}) copy-start(f32[84]{0:T(128)} %param.9) | copy-start | bytes 1012
  3.8 6.6 %collective-permute-start = (bf16[96,64]{1,0:T(8,128)(2,1)S(1)}, bf16[96,64]{1,0:T(8,128)(2,1)S(1)}, u32[]{:S(2)}, u32[]{:S(2)}) collective-permute-start(bf16[96,64]{1,0:T(8,128)(2,1)S(1)} %get-tuple-element.103), channel_id=1, source_target_pairs={{0,1},{1,0},{2,3},{3,2},{4,5},{5,4},{6,7},{7,6},{8,9},{9,8},{10,11... | collective-permute-start | bytes 36872 | tf_op jit(solution)/shard_map/ppermute | solution.py:266
  6.8 5.6 %collective-permute-start.1 = (bf16[96,64]{1,0:T(8,128)(2,1)S(1)}, bf16[96,64]{1,0:T(8,128)(2,1)S(1)}, u32[]{:S(2)}, u32[]{:S(2)}) collective-permute-start(bf16[96,64]{1,0:T(8,128)(2,1)S(1)} %get-tuple-element.104), channel_id=1, source_target_pairs={{0,3},{1,2},{2,1},{3,0},{4,7},{5,6},{6,5},{7,4},{8,11},{9,10},{10,... | collective-permute-start | bytes 36872 | tf_op jit(solution)/shard_map/ppermute | solution.py:267
  12.7 1.4 collective-permute-start.2
  21.5 15.2 %collective-permute-start.3 = (bf16[84,3072]{1,0:T(8,128)(2,1)S(1)}, bf16[84,3072]{1,0:T(8,128)(2,1)S(1)}, u32[]{:S(2)}, u32[]{:S(2)}) collective-permute-start(bf16[84,3072]{1,0:T(8,128)(2,1)S(1)} %get-tuple-element.60), channel_id=1, source_target_pairs={{0,8},{8,0},{16,24},{24,16},{1,9},{9,1},{17,25},{25,17},{2,10},{10... | collective-permute-start | bytes 1548296 | tf_op jit(solution)/shard_map/ppermute | solution.py:708
  23.0 26.7 %collective-permute-start.4 = (bf16[84,3072]{1,0:T(8,128)(2,1)S(1)}, bf16[84,3072]{1,0:T(8,128)(2,1)S(1)}, u32[]{:S(2)}, u32[]{:S(2)}) collective-permute-start(bf16[84,3072]{1,0:T(8,128)(2,1)S(1)} %get-tuple-element.61), channel_id=1, source_target_pairs={{0,16},{8,24},{16,0},{24,8},{1,17},{9,25},{17,1},{25,9},{2,18},{10... | collective-permute-start | bytes 1548296 | tf_op jit(solution)/shard_map/ppermute | solution.py:708
  24.6 25.2 %collective-permute-start.5 = (bf16[84,3072]{1,0:T(8,128)(2,1)S(1)}, bf16[84,3072]{1,0:T(8,128)(2,1)S(1)}, u32[]{:S(2)}, u32[]{:S(2)}) collective-permute-start(bf16[84,3072]{1,0:T(8,128)(2,1)S(1)} %get-tuple-element.62), channel_id=1, source_target_pairs={{0,24},{8,16},{16,8},{24,0},{1,25},{9,17},{17,9},{25,1},{2,26},{10... | collective-permute-start | bytes 1548296 | tf_op jit(solution)/shard_map/ppermute | solution.py:708
  30.4 28.0 %collective-permute-start.9 = (bf16[84,2688]{1,0:T(8,128)(2,1)S(1)}, bf16[84,2688]{1,0:T(8,128)(2,1)S(1)}, u32[]{:S(2)}, u32[]{:S(2)}) collective-permute-start(bf16[84,2688]{1,0:T(8,128)(2,1)S(1)} %get-tuple-element.70), channel_id=1, source_target_pairs={{0,8},{8,0},{16,24},{24,16},{1,9},{9,1},{17,25},{25,17},{2,10},{10... | collective-permute-start | bytes 1354760 | tf_op jit(solution)/shard_map/ppermute | solution.py:708
  32.0 38.1 %collective-permute-start.10 = (bf16[84,2688]{1,0:T(8,128)(2,1)S(1)}, bf16[84,2688]{1,0:T(8,128)(2,1)S(1)}, u32[]{:S(2)}, u32[]{:S(2)}) collective-permute-start(bf16[84,2688]{1,0:T(8,128)(2,1)S(1)} %get-tuple-element.71), channel_id=1, source_target_pairs={{0,16},{8,24},{16,0},{24,8},{1,17},{9,25},{17,1},{25,9},{2,18},{10... | collective-permute-start | bytes 1354760 | tf_op jit(solution)/shard_map/ppermute | solution.py:708
  36.7 33.4 %collective-permute-start.11 = (bf16[84,2688]{1,0:T(8,128)(2,1)S(1)}, bf16[84,2688]{1,0:T(8,128)(2,1)S(1)}, u32[]{:S(2)}, u32[]{:S(2)}) collective-permute-start(bf16[84,2688]{1,0:T(8,128)(2,1)S(1)} %get-tuple-element.72), channel_id=1, source_target_pairs={{0,24},{8,16},{16,8},{24,0},{1,25},{9,17},{17,9},{25,1},{2,26},{10... | collective-permute-start | bytes 1354760 | tf_op jit(solution)/shard_map/ppermute | solution.py:708
  52.9 27.3 %collective-permute-start.6 = (bf16[84,3072]{1,0:T(8,128)(2,1)S(1)}, bf16[84,3072]{1,0:T(8,128)(2,1)S(1)}, u32[]{:S(2)}, u32[]{:S(2)}) collective-permute-start(bf16[84,3072]{1,0:T(8,128)(2,1)S(1)} %get-tuple-element.66), channel_id=1, source_target_pairs={{0,8},{8,0},{16,24},{24,16},{1,9},{9,1},{17,25},{25,17},{2,10},{10... | collective-permute-start | bytes 1548296 | tf_op jit(solution)/shard_map/ppermute | solution.py:708
  54.0 39.3 %collective-permute-start.7 = (bf16[84,3072]{1,0:T(8,128)(2,1)S(1)}, bf16[84,3072]{1,0:T(8,128)(2,1)S(1)}, u32[]{:S(2)}, u32[]{:S(2)}) collective-permute-start(bf16[84,3072]{1,0:T(8,128)(2,1)S(1)} %get-tuple-element.67), channel_id=1, source_target_pairs={{0,16},{8,24},{16,0},{24,8},{1,17},{9,25},{17,1},{25,9},{2,18},{10... | collective-permute-start | bytes 1548296 | tf_op jit(solution)/shard_map/ppermute | solution.py:708
  58.4 34.8 %collective-permute-start.8 = (bf16[84,3072]{1,0:T(8,128)(2,1)S(1)}, bf16[84,3072]{1,0:T(8,128)(2,1)S(1)}, u32[]{:S(2)}, u32[]{:S(2)}) collective-permute-start(bf16[84,3072]{1,0:T(8,128)(2,1)S(1)} %get-tuple-element.68), channel_id=1, source_target_pairs={{0,24},{8,16},{16,8},{24,0},{1,25},{9,17},{17,9},{25,1},{2,26},{10... | collective-permute-start | bytes 1548296 | tf_op jit(solution)/shard_map/ppermute | solution.py:708
  72.9 39.0 %collective-permute-start.12 = (bf16[84,2688]{1,0:T(8,128)(2,1)S(1)}, bf16[84,2688]{1,0:T(8,128)(2,1)S(1)}, u32[]{:S(2)}, u32[]{:S(2)}) collective-permute-start(bf16[84,2688]{1,0:T(8,128)(2,1)S(1)} %get-tuple-element.75), channel_id=1, source_target_pairs={{0,8},{8,0},{16,24},{24,16},{1,9},{9,1},{17,25},{25,17},{2,10},{10... | collective-permute-start | bytes 1354760 | tf_op jit(solution)/shard_map/ppermute | solution.py:708
  74.0 38.4 %collective-permute-start.13 = (bf16[84,2688]{1,0:T(8,128)(2,1)S(1)}, bf16[84,2688]{1,0:T(8,128)(2,1)S(1)}, u32[]{:S(2)}, u32[]{:S(2)}) collective-permute-start(bf16[84,2688]{1,0:T(8,128)(2,1)S(1)} %get-tuple-element.76), channel_id=1, source_target_pairs={{0,16},{8,24},{16,0},{24,8},{1,17},{9,25},{17,1},{25,9},{2,18},{10... | collective-permute-start | bytes 1354760 | tf_op jit(solution)/shard_map/ppermute | solution.py:708
  80.2 32.2 %collective-permute-start.14 = (bf16[84,2688]{1,0:T(8,128)(2,1)S(1)}, bf16[84,2688]{1,0:T(8,128)(2,1)S(1)}, u32[]{:S(2)}, u32[]{:S(2)}) collective-permute-start(bf16[84,2688]{1,0:T(8,128)(2,1)S(1)} %get-tuple-element.77), channel_id=1, source_target_pairs={{0,24},{8,16},{16,8},{24,0},{1,25},{9,17},{17,9},{25,1},{2,26},{10... | collective-permute-start | bytes 1354760 | tf_op jit(solution)/shard_map/ppermute | solution.py:708
  94.0 9.9 %collective-permute-start.15 = (bf16[96,64]{1,0:T(8,128)(2,1)S(1)}, bf16[96,64]{1,0:T(8,128)(2,1)S(1)}, u32[]{:S(2)}, u32[]{:S(2)}) collective-permute-start(bf16[96,64]{1,0:T(8,128)(2,1)S(1)} %get-tuple-element.101), channel_id=1, source_target_pairs={{0,1},{1,0},{2,3},{3,2},{4,5},{5,4},{6,7},{7,6},{8,9},{9,8},{10,11... | collective-permute-start | bytes 36872 | tf_op jit(solution)/shard_map/ppermute | solution.py:266
  94.0 9.9 %collective-permute-start.16 = (bf16[96,64]{1,0:T(8,128)(2,1)S(1)}, bf16[96,64]{1,0:T(8,128)(2,1)S(1)}, u32[]{:S(2)}, u32[]{:S(2)}) collective-permute-start(bf16[96,64]{1,0:T(8,128)(2,1)S(1)} %get-tuple-element.102), channel_id=1, source_target_pairs={{0,3},{1,2},{2,1},{3,0},{4,7},{5,6},{6,5},{7,4},{8,11},{9,10},{10,... | collective-permute-start | bytes 36872 | tf_op jit(solution)/shard_map/ppermute | solution.py:267
  104.0 1.4 collective-permute-start.17
  119.5 1.5 %collective-permute-start.18 = (f32[48,1024]{1,0:T(8,128)S(1)}, f32[48,1024]{1,0:T(8,128)S(1)}, u32[]{:S(2)}, u32[]{:S(2)}) collective-permute-start(f32[48,1024]{1,0:T(8,128)S(1)} %get-tuple-element.87), channel_id=1, source_target_pairs={{0,4},{4,0},{1,5},{5,1},{2,6},{6,2},{3,7},{7,3},{8,12},{12,8},{9,1... | collective-permute-start | bytes 589832 | tf_op jit(solution)/shard_map/ppermute | solution.py:708
  121.0 4.2 %collective-permute-start.19 = (f32[48,256]{1,0:T(8,128)S(1)}, f32[48,256]{1,0:T(8,128)S(1)}, u32[]{:S(2)}, u32[]{:S(2)}) collective-permute-start(f32[48,256]{1,0:T(8,128)S(1)} %get-tuple-element.89), channel_id=1, source_target_pairs={{0,8},{8,0},{16,24},{24,16},{1,9},{9,1},{17,25},{25,17},{2,10},{10... | collective-permute-start | bytes 147464 | tf_op jit(solution)/shard_map/ppermute | solution.py:708
  122.5 4.6 %collective-permute-start.20 = (f32[48,256]{1,0:T(8,128)S(1)}, f32[48,256]{1,0:T(8,128)S(1)}, u32[]{:S(2)}, u32[]{:S(2)}) collective-permute-start(f32[48,256]{1,0:T(8,128)S(1)} %get-tuple-element.90), channel_id=1, source_target_pairs={{0,16},{8,24},{16,0},{24,8},{1,17},{9,25},{17,1},{25,9},{2,18},{10... | collective-permute-start | bytes 147464 | tf_op jit(solution)/shard_map/ppermute | solution.py:708
  123.1 5.0 %collective-permute-start.21 = (f32[48,256]{1,0:T(8,128)S(1)}, f32[48,256]{1,0:T(8,128)S(1)}, u32[]{:S(2)}, u32[]{:S(2)}) collective-permute-start(f32[48,256]{1,0:T(8,128)S(1)} %get-tuple-element.91), channel_id=1, source_target_pairs={{0,24},{8,16},{16,8},{24,0},{1,25},{9,17},{17,9},{25,1},{2,26},{10... | collective-permute-start | bytes 147464 | tf_op jit(solution)/shard_map/ppermute | solution.py:708
  128.2 7.0 %collective-permute-start.22 = (bf16[96,64]{1,0:T(8,128)(2,1)S(1)}, bf16[96,64]{1,0:T(8,128)(2,1)S(1)}, u32[]{:S(2)}, u32[]{:S(2)}) collective-permute-start(bf16[96,64]{1,0:T(8,128)(2,1)S(1)} %get-tuple-element.99), channel_id=1, source_target_pairs={{0,1},{1,0},{2,3},{3,2},{4,5},{5,4},{6,7},{7,6},{8,9},{9,8},{10,11... | collective-permute-start | bytes 36872 | tf_op jit(solution)/shard_map/ppermute | solution.py:266
  128.9 6.3 %collective-permute-start.23 = (bf16[96,64]{1,0:T(8,128)(2,1)S(1)}, bf16[96,64]{1,0:T(8,128)(2,1)S(1)}, u32[]{:S(2)}, u32[]{:S(2)}) collective-permute-start(bf16[96,64]{1,0:T(8,128)(2,1)S(1)} %get-tuple-element.100), channel_id=1, source_target_pairs={{0,3},{1,2},{2,1},{3,0},{4,7},{5,6},{6,5},{7,4},{8,11},{9,10},{10,... | collective-permute-start | bytes 36872 | tf_op jit(solution)/shard_map/ppermute | solution.py:267
  130.8 5.9 %collective-permute-start.26 = (f32[48,256]{1,0:T(8,128)S(1)}, f32[48,256]{1,0:T(8,128)S(1)}, u32[]{:S(2)}, u32[]{:S(2)}) collective-permute-start(f32[48,256]{1,0:T(8,128)S(1)} %add_add_fusion.1), channel_id=1, source_target_pairs={{0,3},{1,2},{2,1},{3,0},{4,7},{5,6},{6,5},{7,4},{8,11},{9,10},{10,... | collective-permute-start | bytes 147464 | tf_op jit(solution)/shard_map/ppermute | solution.py:708
  132.7 5.2 %collective-permute-start.25 = (f32[48,256]{1,0:T(8,128)S(1)}, f32[48,256]{1,0:T(8,128)S(1)}, u32[]{:S(2)}, u32[]{:S(2)}) collective-permute-start(f32[48,256]{1,0:T(8,128)S(1)} %add_add_fusion.1), channel_id=1, source_target_pairs={{0,2},{1,3},{2,0},{3,1},{4,6},{5,7},{6,4},{7,5},{8,10},{9,11},{10,... | collective-permute-start | bytes 147464 | tf_op jit(solution)/shard_map/ppermute | solution.py:708
  133.3 4.6 %collective-permute-start.24 = (f32[48,256]{1,0:T(8,128)S(1)}, f32[48,256]{1,0:T(8,128)S(1)}, u32[]{:S(2)}, u32[]{:S(2)}) collective-permute-start(f32[48,256]{1,0:T(8,128)S(1)} %add_add_fusion.1), channel_id=1, source_target_pairs={{0,1},{1,0},{2,3},{3,2},{4,5},{5,4},{6,7},{7,6},{8,9},{9,8},{10,11... | collective-permute-start | bytes 147464 | tf_op jit(solution)/shard_map/ppermute | solution.py:708
  137.9 6.8 %collective-permute-start.29 = (f32[48,256]{1,0:T(8,128)S(1)}, f32[48,256]{1,0:T(8,128)S(1)}, u32[]{:S(2)}, u32[]{:S(2)}) collective-permute-start(f32[48,256]{1,0:T(8,128)S(1)} %add_add_fusion.refs_0_), channel_id=1, source_target_pairs={{0,24},{8,16},{16,8},{24,0},{1,25},{9,17},{17,9},{25,1},{2,26},{10... | collective-permute-start | bytes 147464 | tf_op jit(solution)/shard_map/ppermute | solution.py:708
  139.5 5.3 %collective-permute-start.28 = (f32[48,256]{1,0:T(8,128)S(1)}, f32[48,256]{1,0:T(8,128)S(1)}, u32[]{:S(2)}, u32[]{:S(2)}) collective-permute-start(f32[48,256]{1,0:T(8,128)S(1)} %add_add_fusion.refs_0_), channel_id=1, source_target_pairs={{0,16},{8,24},{16,0},{24,8},{1,17},{9,25},{17,1},{25,9},{2,18},{10... | collective-permute-start | bytes 147464 | tf_op jit(solution)/shard_map/ppermute | solution.py:708
  141.0 4.1 %collective-permute-start.27 = (f32[48,256]{1,0:T(8,128)S(1)}, f32[48,256]{1,0:T(8,128)S(1)}, u32[]{:S(2)}, u32[]{:S(2)}) collective-permute-start(f32[48,256]{1,0:T(8,128)S(1)} %add_add_fusion.refs_0_), channel_id=1, source_target_pairs={{0,8},{8,0},{16,24},{24,16},{1,9},{9,1},{17,25},{25,17},{2,10},{10... | collective-permute-start | bytes 147464 | tf_op jit(solution)/shard_map/ppermute | solution.py:708
  145.1 3.3 %collective-permute-start.30 = (f32[48,1024]{1,0:T(8,128)S(1)}, f32[48,1024]{1,0:T(8,128)S(1)}, u32[]{:S(2)}, u32[]{:S(2)}) collective-permute-start(f32[48,1024]{1,0:T(8,128)S(1)} %join.1), channel_id=1, source_target_pairs={{0,4},{4,0},{1,5},{5,1},{2,6},{6,2},{3,7},{7,3},{8,12},{12,8},{9,1... | collective-permute-start | bytes 589832 | tf_op jit(solution)/shard_map/ppermute | solution.py:708
where the time goes:
time: 151 us
  waiting for transfers between devices  54.9 us (36%)
  Pallas kernels  50.2 us (33%)
  starting transfers between devices  40.7 us (27%)
  local copies, waits for them, and re-layouts  3.1 us (2%)
    ppermute x23, waiting for transfers between devices, swap(): lax.ppermute(value, axis, [(i, i ^ bits) for i in range(lax.axis_size(axi...  50.4 us
    ppermute x23, starting transfers between devices, swap(): lax.ppermute(value, axis, [(i, i ^ bits) for i in range(lax.axis_size(axi...  29.9 us
    pallas_call x2, Pallas kernels, weight_part(): pl.pallas_call(functools.partial(weight_kernel, grid, ranges, len(chained...  13.8 us
    pallas_call x4, Pallas kernels, input_part(): pl.pallas_call(functools.partial(input_kernel, grid, r0, r1, chunks, len(...  12.9 us
    pallas_call x2, Pallas kernels, forward(): pl.pallas_call(functools.partial(forward_kernel, grid, ranges, has_top, h...  12.8 us
    ppermute x3, starting transfers between devices, lon_halo(): outer = lax.ppermute(jnp.where(odd, last, first), 'lon', far)  6.96 us
    pallas_call x2, Pallas kernels, score(): pl.pallas_call(functools.partial(score_kernel, members), in_specs=[in_vme...  6.02 us
    ppermute x3, starting transfers between devices, lon_halo(): inner = lax.ppermute(jnp.where(odd, first, last), 'lon', near)  3.7 us
  transfers between devices with their start and end apart: 31, of which 18 were waited for; matrix products, arithmetic and copies ran while one was open for 1% of the time, Pallas kernels for 22%

commit v1 on v0

--- a/solution.py
+++ b/solution.py
@@ -253,10 +253,10 @@
     )(kept_in_hbm(field))
 
 
-def lon_halo(edges, odd):
+def lon_halo(edges, odd=None):
     peers = lax.axis_size("lon")
     first, last = edges[:, :LAT_DEV], edges[:, LAT_DEV:]
-    if peers % 2:
+    if peers % 2 or odd is None:
         right = [(i, (i + 1) % peers) for i in range(peers)]
         left = [(j, i) for i, j in right]
         before, after = lax.ppermute(last, "lon", right), lax.ppermute(first, "lon", left)
@@ -720,7 +720,7 @@
     return value
 
 
-def sum_all(keep, send, upper, late):
+def sum_all(keep, send, upper, between):
     members = lax.axis_size("member")
     other = swap(send, "lat", 1)
     values = [keep, other]
@@ -729,8 +729,8 @@
     pieces = split_by_member(values, members)
     moved = [swap(pieces[d], "member", d) for d in range(1, members)]
     value = functools.reduce(jnp.add, moved, pieces[0])
-    value, late = lax.optimization_barrier((value, late))
-    value = sum_axis(value, "lon", 1)
+    value = sum_axis(between(value), "lon", 1)
+    value = between(value)
     half = join_members([value] + [swap(value, "member", d) for d in range(1, members)])
     other = swap(half, "lat", 1)
     total = jnp.where(
@@ -738,7 +738,7 @@
         jnp.concatenate([other, half], axis=0),
         jnp.concatenate([half, other], axis=0),
     )
-    return total, late
+    return total
 
 
 def weights_kernel(taps_ref, forward_ref, backward_ref):
@@ -802,7 +802,7 @@
     upper = (lax.axis_index("lat") & 1) != 0
     odd = (lax.axis_index("lon") & 1) != 0
     x_edges, x_row = edges_of(grid, x)
-    x_sides = lon_halo(x_edges, odd)
+    x_sides = lon_halo(x_edges)
     x_sides, forward_weight, backward_weight, scale, shift, upper, odd = (
         lax.optimization_barrier(
             (x_sides, forward_weight, backward_weight, scale, shift, upper, odd)
@@ -835,38 +835,40 @@
         returned.append(to_members(grads))
 
     blocks = parts_of(grid, 4)
-    parts, edges, sums, grad_input = [], [], [None], None
+    parts, sums, grad_input = [], [None], None
     for number, ranges in enumerate(chunks):
         final = number == len(chunks) - 1
         after = [returned[-1][0]] if number == 0 else [kept_in_hbm(grad_input)]
         part, edge = gather(grid, ranges, rows, returned[number], after)
-        sums = list(
-            weight_part(grid, ranges, members, taken[number], part, sums[0], [], final)
-        )
+        sides = lon_halo(edge, odd)
+        sums = weight_part(grid, ranges, members, taken[number], part, sums[0], [], final)
+        sides, sums = lax.optimization_barrier((sides, list(sums)))
         parts.append(part)
-        edges.append(edge)
+        g_sides = sides if number == 0 else g_sides + sides
         if number == 0:
             end = part.shape[1] - grid.padded + cells
             outer_rows = (part[:, : grid.halo], part[:, end - grid.halo : end])
-        if final:
-            break
-        g_sides = lon_halo(edge, odd)
-        g_sides, sums[0] = lax.optimization_barrier((g_sides, sums[0]))
-        g_top, g_bottom = lat_halo(*outer_rows, g_sides, first_lat)
-        for _ in range(2):
+            g_top, g_bottom = lat_halo(*outer_rows, g_sides, first_lat)
+        for _ in range(0 if final else 2):
             grad_input = input_part(
                 grid, *blocks.pop(), chunks[:1], parts[:1], g_sides, g_top, g_bottom,
                 backward_weight, grad_input, False,
             )
-    total, late_edges = sum_all(*sums, upper, edges[-1])
-    late_sides = lon_halo(late_edges, odd)
-    if len(chunks) == 1:
-        g_top, g_bottom = lat_halo(*outer_rows, late_sides, first_lat)
-    else:
-        late_sides = late_sides + g_sides
-    for r0, r1 in blocks:
+
+    def between(value):
+        nonlocal grad_input
+        for _ in range(min((len(blocks) + 1) // 2, len(blocks))):
+            grad_input = input_part(
+                grid, *blocks.pop(), chunks, parts, g_sides, g_top, g_bottom, backward_weight,
+                grad_input, True,
+            )
+            value, grad_input = lax.optimization_barrier((value, grad_input))
+        return value
+
+    total = sum_all(*sums, upper, between)
+    while blocks:
         grad_input = input_part(
-            grid, r0, r1, chunks, parts, late_sides, g_top, g_bottom, backward_weight,
+            grid, *blocks.pop(), chunks, parts, g_sides, g_top, g_bottom, backward_weight,
             grad_input, True,
         )
     total = total / (cells * lax.axis_size("lat") * lax.axis_size("lon"))

time: 151 us -> 149 us (0.987)
  waiting for transfers between devices: 54.9 us -> 52.2 us
    ppermute x0 -> x2, starting transfers between devices: none -> 5.11 us  [the longest x1 3.03 us: lon_halo(): lax.ppermute(last, 'lon', right)]
    ppermute x3 -> x2, starting transfers between devices: 6.96 us -> 4.5 us  [lon_halo(): outer = lax.ppermute(jnp.where(odd, last, first), 'lon', far)]
    ppermute x3 -> x2, waiting for transfers between devices: 2.1 us -> 0.01 us  [lon_halo(): outer = lax.ppermute(jnp.where(odd, last, first), 'lon', far)]
    ppermute x23, waiting for transfers between devices: 50.4 us -> 48.8 us  [swap(): lax.ppermute(value, axis, [(i, i ^ bits) for i in range(lax.axis_size(axi...]
    ppermute x3 -> x2, starting transfers between devices: 3.7 us -> 2.39 us  [lon_halo(): inner = lax.ppermute(jnp.where(odd, first, last), 'lon', near)]
  transfers between devices with their start and end apart: 31 -> 31, of which waited for: 18 -> 16; matrix products, arithmetic and copies ran while one was open for 1% -> 1% of each run, Pallas kernels for 22% -> 26%
where the time goes in v1:
time: 149 us
  waiting for transfers between devices  52.2 us (35%)
  Pallas kernels  50.2 us (34%)
  starting transfers between devices  42.1 us (28%)
  local copies, waits for them, and re-layouts  3.18 us (2%)
    ppermute x23, waiting for transfers between devices, swap(): lax.ppermute(value, axis, [(i, i ^ bits) for i in range(lax.axis_size(axi...  48.8 us
    ppermute x23, starting transfers between devices, swap(): lax.ppermute(value, axis, [(i, i ^ bits) for i in range(lax.axis_size(axi...  30 us
    pallas_call x2, Pallas kernels, weight_part(): pl.pallas_call(functools.partial(weight_kernel, grid, ranges, len(chained...  13.8 us
    pallas_call x4, Pallas kernels, input_part(): pl.pallas_call(functools.partial(input_kernel, grid, r0, r1, chunks, len(...  12.9 us
    pallas_call x2, Pallas kernels, forward(): pl.pallas_call(functools.partial(forward_kernel, grid, ranges, has_top, h...  12.8 us
    pallas_call x2, Pallas kernels, score(): pl.pallas_call(functools.partial(score_kernel, members), in_specs=[in_vme...  6.02 us
    ppermute x2, starting transfers between devices, lon_halo(): outer = lax.ppermute(jnp.where(odd, last, first), 'lon', far)  4.5 us
    ppermute x1, starting transfers between devices, lon_halo(): lax.ppermute(last, 'lon', right)  3.03 us
  transfers between devices with their start and end apart: 31, of which 16 were waited for; matrix products, arithmetic and copies ran while one was open for 1% of the time, Pallas kernels for 26%

profile of v1, /device:TPU:0, one launch (start us, length us, event | category | flops | bytes accessed | tf_op | source)
XLA Modules:
  0.0 149.3 jit_solution(13323687494693633492)
XLA Ops:
  0.7 3.0 %edges.1 = (bf16[96,128]{1,0:T(8,128)(2,1)S(1)}, bf16[96,384]{1,0:T(8,128)(2,1)S(1)}) custom-call(bf16[96,23040]{1,0:T(8,128)(2,1)} %bitcast.7), custom_call_target="tpu_custom_call" | custom-call | flops 96 | bytes 96 | tf_op jit(solution)/shard_map/edges/pallas_call | solution.py:240
  3.8 3.0 %collective-permute-start = (bf16[96,64]{1,0:T(8,128)(2,1)S(1)}, bf16[96,64]{1,0:T(8,128)(2,1)S(1)}, u32[]{:S(2)}, u32[]{:S(2)}) collective-permute-start(bf16[96,64]{1,0:T(8,128)(2,1)S(1)} %get-tuple-element.113), channel_id=1, source_target_pairs={{0,1},{1,2},{2,3},{3,0},{4,5},{5,6},{6,7},{7,4},{8,9},{9,10},{10,1... | collective-permute-start | bytes 36872 | tf_op jit(solution)/shard_map/ppermute | solution.py:262
  6.8 2.1 %collective-permute-start.1 = (bf16[96,64]{1,0:T(8,128)(2,1)S(1)}, bf16[96,64]{1,0:T(8,128)(2,1)S(1)}, u32[]{:S(2)}, u32[]{:S(2)}) collective-permute-start(bf16[96,64]{1,0:T(8,128)(2,1)S(1)} %get-tuple-element.114), channel_id=1, source_target_pairs={{1,0},{2,1},{3,2},{0,3},{5,4},{6,5},{7,6},{4,7},{9,8},{10,9},{11,1... | collective-permute-start | bytes 36872 | tf_op jit(solution)/shard_map/ppermute | solution.py:262
  9.9 0.8 collective-permute-done
  11.3 1.2 collective-permute-done.2
  12.5 7.4 %forward_0.1 = (bf16[84,3072]{1,0:T(8,128)(2,1)S(1)}, bf16[84,3072]{1,0:T(8,128)(2,1)S(1)}, bf16[84,3072]{1,0:T(8,128)(2,1)S(1)}, bf16[84,3072]{1,0:T(8,128)(2,1...) custom-call(bf16[96,23040]{1,0:T(8,128)(2,1)} %bitcast.8, ...), custom_call_target="tpu_custom_call" | custom-call | flops 8026324992 | tf_op jit(solution)/shard_map/forward_0/pallas_call | solution.py:390
  19.9 1.6 %collective-permute-start.9 = (bf16[84,3072]{1,0:T(8,128)(2,1)S(1)}, bf16[84,3072]{1,0:T(8,128)(2,1)S(1)}, u32[]{:S(2)}, u32[]{:S(2)}) collective-permute-start(bf16[84,3072]{1,0:T(8,128)(2,1)S(1)} %get-tuple-element.76), channel_id=1, source_target_pairs={{0,8},{8,0},{16,24},{24,16},{1,9},{9,1},{17,25},{25,17},{2,10},{10... | collective-permute-start | bytes 1548296 | tf_op jit(solution)/shard_map/ppermute | solution.py:708
  21.4 1.5 %collective-permute-start.10 = (bf16[84,3072]{1,0:T(8,128)(2,1)S(1)}, bf16[84,3072]{1,0:T(8,128)(2,1)S(1)}, u32[]{:S(2)}, u32[]{:S(2)}) collective-permute-start(bf16[84,3072]{1,0:T(8,128)(2,1)S(1)} %get-tuple-element.77), channel_id=1, source_target_pairs={{0,16},{8,24},{16,0},{24,8},{1,17},{9,25},{17,1},{25,9},{2,18},{10... | collective-permute-start | bytes 1548296 | tf_op jit(solution)/shard_map/ppermute | solution.py:708
  23.4 5.4 %forward_6144.1 = (bf16[84,2688]{1,0:T(8,128)(2,1)S(1)}, bf16[84,2688]{1,0:T(8,128)(2,1)S(1)}, bf16[84,2688]{1,0:T(8,128)(2,1)S(1)}, bf16[84,2688]{1,0:T(8,128)(...) custom-call(bf16[96,23040]{1,0:T(8,128)(2,1)S(1)} %get-tuple-element.63.refs_0_, ...), custom_call_target="tpu_custom_call" | custom-call | flops 7023034368 | tf_op jit(solution)/shard_map/forward_6144/pallas_call | solution.py:390
  28.8 1.6 %collective-permute-start.3 = (bf16[84,2688]{1,0:T(8,128)(2,1)S(1)}, bf16[84,2688]{1,0:T(8,128)(2,1)S(1)}, u32[]{:S(2)}, u32[]{:S(2)}) collective-permute-start(bf16[84,2688]{1,0:T(8,128)(2,1)S(1)} %get-tuple-element.67), channel_id=1, source_target_pairs={{0,8},{8,0},{16,24},{24,16},{1,9},{9,1},{17,25},{25,17},{2,10},{10... | collective-permute-start | bytes 1354760 | tf_op jit(solution)/shard_map/ppermute | solution.py:708
  30.4 1.5 %collective-permute-start.4 = (bf16[84,2688]{1,0:T(8,128)(2,1)S(1)}, bf16[84,2688]{1,0:T(8,128)(2,1)S(1)}, u32[]{:S(2)}, u32[]{:S(2)}) collective-permute-start(bf16[84,2688]{1,0:T(8,128)(2,1)S(1)} %get-tuple-element.68), channel_id=1, source_target_pairs={{0,16},{8,24},{16,0},{24,8},{1,17},{9,25},{17,1},{25,9},{2,18},{10... | collective-permute-start | bytes 1354760 | tf_op jit(solution)/shard_map/ppermute | solution.py:708
  31.9 3.1 %collective-permute-done.9.refs_1_ = bf16[84,3072]{1,0:T(8,128)(2,1)S(1)} collective-permute-done((bf16[84,3072]{1,0:T(8,128)(2,1)S(1)}, bf16[84,3072]{1,0:T(8,128)(2,1)S(1)}, u32[]{:S(2)}, u32[]{:S(2)}) %collective-permute-start.9) | collective-permute-done | bytes 516128 | tf_op jit(solution)/shard_map/ppermute | solution.py:708
  35.1 2.5 %collective-permute-start.5 = (bf16[84,2688]{1,0:T(8,128)(2,1)S(1)}, bf16[84,2688]{1,0:T(8,128)(2,1)S(1)}, u32[]{:S(2)}, u32[]{:S(2)}) collective-permute-start(bf16[84,2688]{1,0:T(8,128)(2,1)S(1)} %get-tuple-element.69), channel_id=1, source_target_pairs={{0,24},{8,16},{16,8},{24,0},{1,25},{9,17},{17,9},{25,1},{2,26},{10... | collective-permute-start | bytes 1354760 | tf_op jit(solution)/shard_map/ppermute | solution.py:708
  37.5 10.7 %collective-permute-done.10.refs_2_ = bf16[84,3072]{1,0:T(8,128)(2,1)S(1)} collective-permute-done((bf16[84,3072]{1,0:T(8,128)(2,1)S(1)}, bf16[84,3072]{1,0:T(8,128)(2,1)S(1)}, u32[]{:S(2)}, u32[]{:S(2)}) %collective-permute-start.10) | collective-permute-done | bytes 516128 | tf_op jit(solution)/shard_map/ppermute | solution.py:708
  48.2 3.1 %score_0.1 = (bf16[84,3072]{1,0:T(8,128)(2,1)S(1)}, bf16[84,3072]{1,0:T(8,128)(2,1)S(1)}, bf16[84,3072]{1,0:T(8,128)(2,1)S(1)}, bf16[84,3072]{1,0:T(8,128)(2,1)S(1)}) custom-call(bf16[84,3072]{1,0:T(8,128)(2,1)S(1)} %get-tuple-element.74.target_ref, f32[84,128]{1,0:T(8,128)S(1)} %broadcast_in_dim.4.scale_ref, ...), custom_call_target="tpu_custom_call" | custom-call | flops 3354624000 | tf_op jit(solution)/shard_map/score_0/pallas_call | solution.py:452
  51.3 1.0 collective-permute-start.12
  52.4 1.1 collective-permute-start.13
  53.4 3.4 %collective-permute-done.3.refs_1_ = bf16[84,2688]{1,0:T(8,128)(2,1)S(1)} collective-permute-done((bf16[84,2688]{1,0:T(8,128)(2,1)S(1)}, bf16[84,2688]{1,0:T(8,128)(2,1)S(1)}, u32[]{:S(2)}, u32[]{:S(2)}) %collective-permute-start.3) | collective-permute-done | bytes 451616 | tf_op jit(solution)/shard_map/ppermute | solution.py:708
  56.8 2.5 %collective-permute-start.14 = (bf16[84,3072]{1,0:T(8,128)(2,1)S(1)}, bf16[84,3072]{1,0:T(8,128)(2,1)S(1)}, u32[]{:S(2)}, u32[]{:S(2)}) collective-permute-start(bf16[84,3072]{1,0:T(8,128)(2,1)S(1)} %get-tuple-element.82), channel_id=1, source_target_pairs={{0,24},{8,16},{16,8},{24,0},{1,25},{9,17},{17,9},{25,1},{2,26},{10... | collective-permute-start | bytes 1548296 | tf_op jit(solution)/shard_map/ppermute | solution.py:708
  59.3 9.2 %collective-permute-done.4.refs_2_ = bf16[84,2688]{1,0:T(8,128)(2,1)S(1)} collective-permute-done((bf16[84,2688]{1,0:T(8,128)(2,1)S(1)}, bf16[84,2688]{1,0:T(8,128)(2,1)S(1)}, u32[]{:S(2)}, u32[]{:S(2)}) %collective-permute-start.4) | collective-permute-done | bytes 451616 | tf_op jit(solution)/shard_map/ppermute | solution.py:708
  68.5 2.9 %score_6144.1 = (bf16[84,2688]{1,0:T(8,128)(2,1)S(1)}, bf16[84,2688]{1,0:T(8,128)(2,1)S(1)}, bf16[84,2688]{1,0:T(8,128)(2,1)S(1)}, bf16[84,2688]{1,0:T(8,128)(2,1)S(1)}) custom-call(bf16[84,2688]{1,0:T(8,128)(2,1)S(1)} %get-tuple-element.64.target_ref.refs_4_, f32[84,128]{1,0:T(8,128)S(1)} %broadcast_in_dim.4.scale_ref, ...), custom_call_target="tpu_custom_call" | custom-call | flops 2935296000 | tf_op jit(solution)/shard_map/score_6144/pallas_call | solution.py:452
  71.4 1.1 collective-permute-start.6
  72.5 1.0 collective-permute-start.7
  73.5 5.1 %collective-permute-done.12.refs_1_ = bf16[84,3072]{1,0:T(8,128)(2,1)S(1)} collective-permute-done((bf16[84,3072]{1,0:T(8,128)(2,1)S(1)}, bf16[84,3072]{1,0:T(8,128)(2,1)S(1)}, u32[]{:S(2)}, u32[]{:S(2)}) %collective-permute-start.12) | collective-permute-done | bytes 516128 | tf_op jit(solution)/shard_map/ppermute | solution.py:708
  78.6 2.5 %collective-permute-start.8 = (bf16[84,2688]{1,0:T(8,128)(2,1)S(1)}, bf16[84,2688]{1,0:T(8,128)(2,1)S(1)}, u32[]{:S(2)}, u32[]{:S(2)}) collective-permute-start(bf16[84,2688]{1,0:T(8,128)(2,1)S(1)} %get-tuple-element.73), channel_id=1, source_target_pairs={{0,24},{8,16},{16,8},{24,0},{1,25},{9,17},{17,9},{25,1},{2,26},{10... | collective-permute-start | bytes 1354760 | tf_op jit(solution)/shard_map/ppermute | solution.py:708
  81.1 10.6 %collective-permute-done.13.refs_2_ = bf16[84,3072]{1,0:T(8,128)(2,1)S(1)} collective-permute-done((bf16[84,3072]{1,0:T(8,128)(2,1)S(1)}, bf16[84,3072]{1,0:T(8,128)(2,1)S(1)}, u32[]{:S(2)}, u32[]{:S(2)}) %collective-permute-start.13) | collective-permute-done | bytes 516128 | tf_op jit(solution)/shard_map/ppermute | solution.py:708
  92.4 1.3 collective-permute-start.15
  93.7 2.6 %collective-permute-start.16 = (bf16[96,64]{1,0:T(8,128)(2,1)S(1)}, bf16[96,64]{1,0:T(8,128)(2,1)S(1)}, u32[]{:S(2)}, u32[]{:S(2)}) collective-permute-start(bf16[96,64]{1,0:T(8,128)(2,1)S(1)} %get-tuple-element.112), channel_id=1, source_target_pairs={{0,3},{1,2},{2,1},{3,0},{4,7},{5,6},{6,5},{7,4},{8,11},{9,10},{10,... | collective-permute-start | bytes 36872 | tf_op jit(solution)/shard_map/ppermute | solution.py:267
  96.3 7.3 %weight_0.1.refs_0_ = f32[96,1024]{1,0:T(8,128)S(1)} custom-call(bf16[288,15360]{1,0:T(8,128)(2,1)S(1)} %get-tuple-element.85.taps, bf16[96,12288]{1,0:T(8,128)(2,1)S(1)} %get-tuple-element.83.part_ref.refs_0_), custom_call_target="tpu_custom_call" | custom-call | flops 12288 | tf_op jit(solution)/shard_map/weight_0/pallas_call | solution.py:566
  103.8 1.3 collective-permute-done.17
  105.2 3.2 %input_48.1.refs_4_ = bf16[96,23040]{1,0:T(8,128)(2,1)} custom-call(bf16[96,12288]{1,0:T(8,128)(2,1)S(1)} %get-tuple-element.83.part_ref.refs_0_, bf16[96,128]{1,0:T(8,128)(2,1)S(1)} %maximum_select_fusion.1.refs_1_, bf16[96,864]{1,0:T(8,128)(2,1)S(1)} %get-tuple-element.87.refs_2_.refs_3_, bf16[96,512]{1,0:T(8,128)(2,1)S(1)} %get-tuple-element.105.refs_3_), custom_call_target="tpu_custom_call" | custom-call | flops 53084160 | bytes 5760 | tf_op jit(solution)/shard_map/input_48/pallas_call | solution.py:638
  108.4 3.2 %input_0.1.refs_4_ = bf16[96,23040]{1,0:T(8,128)(2,1)} custom-call(bf16[96,12288]{1,0:T(8,128)(2,1)S(1)} %get-tuple-element.83.part_ref.refs_0_, bf16[96,128]{1,0:T(8,128)(2,1)S(1)} %maximum_select_fusion.1.refs_1_, bf16[96,864]{1,0:T(8,128)(2,1)S(1)} %get-tuple-element.87.refs_2_.refs_3_, ...), custom_call_target="tpu_custom_call", output_to_operand_aliasing={{}: (4, {})} | custom-call | flops 53084160 | bytes 5760 | tf_op jit(solution)/shard_map/input_0/pallas_call | solution.py:638
  112.4 1.1 collective-permute-start.18
  113.4 2.0 %collective-permute-start.19 = (bf16[96,64]{1,0:T(8,128)(2,1)S(1)}, bf16[96,64]{1,0:T(8,128)(2,1)S(1)}, u32[]{:S(2)}, u32[]{:S(2)}) collective-permute-start(bf16[96,64]{1,0:T(8,128)(2,1)S(1)} %get-tuple-element.110), channel_id=1, source_target_pairs={{0,3},{1,2},{2,1},{3,0},{4,7},{5,6},{6,5},{7,4},{8,11},{9,10},{10,... | collective-permute-start | bytes 36872 | tf_op jit(solution)/shard_map/ppermute | solution.py:267
  115.4 6.5 %weight_6144.1 = (f32[48,1024]{1,0:T(8,128)S(1)}, f32[48,1024]{1,0:T(8,128)S(1)}) custom-call(bf16[288,12288]{1,0:T(8,128)(2,1)S(1)} %get-tuple-element.89.taps, bf16[96,10752]{1,0:T(8,128)(2,1)S(1)} %get-tuple-element.90.part_ref.refs_1_, f32[96,1024]{1,0:T(8,128)S(1)} %weight_0.1.refs_0_), custom_call_target="tpu_custom_call" | custom-call | flops 10752 | tf_op jit(solution)/shard_map/weight_6144/pallas_call | solution.py:566
  122.1 1.4 collective-permute-done.20.refs_1_
  123.5 1.5 collective-permute-start.21
  125.6 1.4 collective-permute-start.23
  127.1 3.2 %input_32.1.refs_4_ = bf16[96,23040]{1,0:T(8,128)(2,1)} custom-call(bf16[96,12288]{1,0:T(8,128)(2,1)S(1)} %get-tuple-element.83.part_ref.refs_0_, bf16[96,10752]{1,0:T(8,128)(2,1)S(1)} %get-tuple-element.90.part_ref.refs_1_, bf16[96,128]{1,0:T(8,128)(2,1)S(1)} %add.24.refs_2_, ...), custom_call_target="tpu_custom_call", output_to_operand_aliasing={{}: (4, {})} | custom-call | flops 4246732800 | bytes 5760 | tf_op jit(solution)/shard_map/input_32/pallas_call | solution.py:638
  130.6 1.9 %collective-permute-start.26 = (f32[48,256]{1,0:T(8,128)S(1)}, f32[48,256]{1,0:T(8,128)S(1)}, u32[]{:S(2)}, u32[]{:S(2)}) collective-permute-start(f32[48,256]{1,0:T(8,128)S(1)} %add_add_fusion.1), channel_id=1, source_target_pairs={{0,3},{1,2},{2,1},{3,0},{4,7},{5,6},{6,5},{7,4},{8,11},{9,10},{10,... | collective-permute-start | bytes 147464 | tf_op jit(solution)/shard_map/ppermute | solution.py:708
  133.2 1.9 %collective-permute-start.24 = (f32[48,256]{1,0:T(8,128)S(1)}, f32[48,256]{1,0:T(8,128)S(1)}, u32[]{:S(2)}, u32[]{:S(2)}) collective-permute-start(f32[48,256]{1,0:T(8,128)S(1)} %add_add_fusion.1), channel_id=1, source_target_pairs={{0,1},{1,0},{2,3},{3,2},{4,5},{5,4},{6,7},{7,6},{8,9},{9,8},{10,11... | collective-permute-start | bytes 147464 | tf_op jit(solution)/shard_map/ppermute | solution.py:708
  135.1 3.3 %input_16.1 = bf16[96,23040]{1,0:T(8,128)(2,1)} custom-call(bf16[96,12288]{1,0:T(8,128)(2,1)S(1)} %get-tuple-element.83.part_ref.refs_0_, bf16[96,10752]{1,0:T(8,128)(2,1)S(1)} %get-tuple-element.90.part_ref.refs_1_, bf16[96,128]{1,0:T(8,128)(2,1)S(1)} %add.24.refs_2_, ...), custom_call_target="tpu_custom_call", output_to_operand_aliasing={{}: (4, {})} | custom-call | flops 4246732800 | bytes 5760 | tf_op jit(solution)/shard_map/input_16/pallas_call | solution.py:638
  138.4 1.5 %collective-permute-start.29 = (f32[48,256]{1,0:T(8,128)S(1)}, f32[48,256]{1,0:T(8,128)S(1)}, u32[]{:S(2)}, u32[]{:S(2)}) collective-permute-start(f32[48,256]{1,0:T(8,128)S(1)} %add_add_fusion.refs_0_), channel_id=1, source_target_pairs={{0,24},{8,16},{16,8},{24,0},{1,25},{9,17},{17,9},{25,1},{2,26},{10... | collective-permute-start | bytes 147464 | tf_op jit(solution)/shard_map/ppermute | solution.py:708
  139.9 1.6 %collective-permute-start.28 = (f32[48,256]{1,0:T(8,128)S(1)}, f32[48,256]{1,0:T(8,128)S(1)}, u32[]{:S(2)}, u32[]{:S(2)}) collective-permute-start(f32[48,256]{1,0:T(8,128)S(1)} %add_add_fusion.refs_0_), channel_id=1, source_target_pairs={{0,16},{8,24},{16,0},{24,8},{1,17},{9,25},{17,1},{25,9},{2,18},{10... | collective-permute-start | bytes 147464 | tf_op jit(solution)/shard_map/ppermute | solution.py:708
  142.0 1.5 %collective-permute-done.29.refs_3_ = f32[48,256]{1,0:T(8,128)S(1)} collective-permute-done((f32[48,256]{1,0:T(8,128)S(1)}, f32[48,256]{1,0:T(8,128)S(1)}, u32[]{:S(2)}, u32[]{:S(2)}) %collective-permute-start.29) | collective-permute-done | bytes 49184 | tf_op jit(solution)/shard_map/ppermute | solution.py:708
  144.0 1.6 %collective-permute-done.27.refs_1_ = f32[48,256]{1,0:T(8,128)S(1)} collective-permute-done((f32[48,256]{1,0:T(8,128)S(1)}, f32[48,256]{1,0:T(8,128)S(1)}, u32[]{:S(2)}, u32[]{:S(2)}) %collective-permute-start.27) | collective-permute-done | bytes 49184 | tf_op jit(solution)/shard_map/ppermute | solution.py:708
  145.7 1.4 collective-permute-done.30
  148.1 1.2 reshape.26
  (58 shorter events, 7.7 us)
Async XLA Ops:
  0.6 8.3 %copy-start = (bf16[9,8064]{1,0:T(8,128)(2,1)S(1)}, bf16[9,8064]{1,0:T(8,128)(2,1)}, u32[]{:S(2)}) copy-start(bf16[9,8064]{1,0:T(8,128)(2,1)} %param.6) | copy-start | bytes 435460
  0.6 10.5 %copy-start.2 = (f32[84]{0:T(128)S(1)}, f32[84]{0:T(128)}, u32[]{:S(2)}) copy-start(f32[84]{0:T(128)} %param.7) | copy-start | bytes 1012
  0.7 10.3 %copy-start.1 = (f32[84]{0:T(128)S(1)}, f32[84]{0:T(128)}, u32[]{:S(2)}) copy-start(f32[84]{0:T(128)} %param.9) | copy-start | bytes 1012
  3.8 7.0 %collective-permute-start = (bf16[96,64]{1,0:T(8,128)(2,1)S(1)}, bf16[96,64]{1,0:T(8,128)(2,1)S(1)}, u32[]{:S(2)}, u32[]{:S(2)}) collective-permute-start(bf16[96,64]{1,0:T(8,128)(2,1)S(1)} %get-tuple-element.113), channel_id=1, source_target_pairs={{0,1},{1,2},{2,3},{3,0},{4,5},{5,6},{6,7},{7,4},{8,9},{9,10},{10,1... | collective-permute-start | bytes 36872 | tf_op jit(solution)/shard_map/ppermute | solution.py:262
  6.8 4.1 %collective-permute-start.1 = (bf16[96,64]{1,0:T(8,128)(2,1)S(1)}, bf16[96,64]{1,0:T(8,128)(2,1)S(1)}, u32[]{:S(2)}, u32[]{:S(2)}) collective-permute-start(bf16[96,64]{1,0:T(8,128)(2,1)S(1)} %get-tuple-element.114), channel_id=1, source_target_pairs={{1,0},{2,1},{3,2},{0,3},{5,4},{6,5},{7,6},{4,7},{9,8},{10,9},{11,1... | collective-permute-start | bytes 36872 | tf_op jit(solution)/shard_map/ppermute | solution.py:262
  11.1 1.4 collective-permute-start.2
  19.9 15.2 %collective-permute-start.9 = (bf16[84,3072]{1,0:T(8,128)(2,1)S(1)}, bf16[84,3072]{1,0:T(8,128)(2,1)S(1)}, u32[]{:S(2)}, u32[]{:S(2)}) collective-permute-start(bf16[84,3072]{1,0:T(8,128)(2,1)S(1)} %get-tuple-element.76), channel_id=1, source_target_pairs={{0,8},{8,0},{16,24},{24,16},{1,9},{9,1},{17,25},{25,17},{2,10},{10... | collective-permute-start | bytes 1548296 | tf_op jit(solution)/shard_map/ppermute | solution.py:708
  21.4 26.7 %collective-permute-start.10 = (bf16[84,3072]{1,0:T(8,128)(2,1)S(1)}, bf16[84,3072]{1,0:T(8,128)(2,1)S(1)}, u32[]{:S(2)}, u32[]{:S(2)}) collective-permute-start(bf16[84,3072]{1,0:T(8,128)(2,1)S(1)} %get-tuple-element.77), channel_id=1, source_target_pairs={{0,16},{8,24},{16,0},{24,8},{1,17},{9,25},{17,1},{25,9},{2,18},{10... | collective-permute-start | bytes 1548296 | tf_op jit(solution)/shard_map/ppermute | solution.py:708
  23.0 25.2 %collective-permute-start.11 = (bf16[84,3072]{1,0:T(8,128)(2,1)S(1)}, bf16[84,3072]{1,0:T(8,128)(2,1)S(1)}, u32[]{:S(2)}, u32[]{:S(2)}) collective-permute-start(bf16[84,3072]{1,0:T(8,128)(2,1)S(1)} %get-tuple-element.78), channel_id=1, source_target_pairs={{0,24},{8,16},{16,8},{24,0},{1,25},{9,17},{17,9},{25,1},{2,26},{10... | collective-permute-start | bytes 1548296 | tf_op jit(solution)/shard_map/ppermute | solution.py:708
  28.8 28.0 %collective-permute-start.3 = (bf16[84,2688]{1,0:T(8,128)(2,1)S(1)}, bf16[84,2688]{1,0:T(8,128)(2,1)S(1)}, u32[]{:S(2)}, u32[]{:S(2)}) collective-permute-start(bf16[84,2688]{1,0:T(8,128)(2,1)S(1)} %get-tuple-element.67), channel_id=1, source_target_pairs={{0,8},{8,0},{16,24},{24,16},{1,9},{9,1},{17,25},{25,17},{2,10},{10... | collective-permute-start | bytes 1354760 | tf_op jit(solution)/shard_map/ppermute | solution.py:708
  30.4 38.1 %collective-permute-start.4 = (bf16[84,2688]{1,0:T(8,128)(2,1)S(1)}, bf16[84,2688]{1,0:T(8,128)(2,1)S(1)}, u32[]{:S(2)}, u32[]{:S(2)}) collective-permute-start(bf16[84,2688]{1,0:T(8,128)(2,1)S(1)} %get-tuple-element.68), channel_id=1, source_target_pairs={{0,16},{8,24},{16,0},{24,8},{1,17},{9,25},{17,1},{25,9},{2,18},{10... | collective-permute-start | bytes 1354760 | tf_op jit(solution)/shard_map/ppermute | solution.py:708
  35.1 33.4 %collective-permute-start.5 = (bf16[84,2688]{1,0:T(8,128)(2,1)S(1)}, bf16[84,2688]{1,0:T(8,128)(2,1)S(1)}, u32[]{:S(2)}, u32[]{:S(2)}) collective-permute-start(bf16[84,2688]{1,0:T(8,128)(2,1)S(1)} %get-tuple-element.69), channel_id=1, source_target_pairs={{0,24},{8,16},{16,8},{24,0},{1,25},{9,17},{17,9},{25,1},{2,26},{10... | collective-permute-start | bytes 1354760 | tf_op jit(solution)/shard_map/ppermute | solution.py:708
  51.3 27.3 %collective-permute-start.12 = (bf16[84,3072]{1,0:T(8,128)(2,1)S(1)}, bf16[84,3072]{1,0:T(8,128)(2,1)S(1)}, u32[]{:S(2)}, u32[]{:S(2)}) collective-permute-start(bf16[84,3072]{1,0:T(8,128)(2,1)S(1)} %get-tuple-element.80), channel_id=1, source_target_pairs={{0,8},{8,0},{16,24},{24,16},{1,9},{9,1},{17,25},{25,17},{2,10},{10... | collective-permute-start | bytes 1548296 | tf_op jit(solution)/shard_map/ppermute | solution.py:708
  52.4 39.3 %collective-permute-start.13 = (bf16[84,3072]{1,0:T(8,128)(2,1)S(1)}, bf16[84,3072]{1,0:T(8,128)(2,1)S(1)}, u32[]{:S(2)}, u32[]{:S(2)}) collective-permute-start(bf16[84,3072]{1,0:T(8,128)(2,1)S(1)} %get-tuple-element.81), channel_id=1, source_target_pairs={{0,16},{8,24},{16,0},{24,8},{1,17},{9,25},{17,1},{25,9},{2,18},{10... | collective-permute-start | bytes 1548296 | tf_op jit(solution)/shard_map/ppermute | solution.py:708
  56.8 34.8 %collective-permute-start.14 = (bf16[84,3072]{1,0:T(8,128)(2,1)S(1)}, bf16[84,3072]{1,0:T(8,128)(2,1)S(1)}, u32[]{:S(2)}, u32[]{:S(2)}) collective-permute-start(bf16[84,3072]{1,0:T(8,128)(2,1)S(1)} %get-tuple-element.82), channel_id=1, source_target_pairs={{0,24},{8,16},{16,8},{24,0},{1,25},{9,17},{17,9},{25,1},{2,26},{10... | collective-permute-start | bytes 1548296 | tf_op jit(solution)/shard_map/ppermute | solution.py:708
  71.4 40.3 %collective-permute-start.6 = (bf16[84,2688]{1,0:T(8,128)(2,1)S(1)}, bf16[84,2688]{1,0:T(8,128)(2,1)S(1)}, u32[]{:S(2)}, u32[]{:S(2)}) collective-permute-start(bf16[84,2688]{1,0:T(8,128)(2,1)S(1)} %get-tuple-element.71), channel_id=1, source_target_pairs={{0,8},{8,0},{16,24},{24,16},{1,9},{9,1},{17,25},{25,17},{2,10},{10... | collective-permute-start | bytes 1354760 | tf_op jit(solution)/shard_map/ppermute | solution.py:708
  72.5 39.2 %collective-permute-start.7 = (bf16[84,2688]{1,0:T(8,128)(2,1)S(1)}, bf16[84,2688]{1,0:T(8,128)(2,1)S(1)}, u32[]{:S(2)}, u32[]{:S(2)}) collective-permute-start(bf16[84,2688]{1,0:T(8,128)(2,1)S(1)} %get-tuple-element.72), channel_id=1, source_target_pairs={{0,16},{8,24},{16,0},{24,8},{1,17},{9,25},{17,1},{25,9},{2,18},{10... | collective-permute-start | bytes 1354760 | tf_op jit(solution)/shard_map/ppermute | solution.py:708
  78.6 33.0 %collective-permute-start.8 = (bf16[84,2688]{1,0:T(8,128)(2,1)S(1)}, bf16[84,2688]{1,0:T(8,128)(2,1)S(1)}, u32[]{:S(2)}, u32[]{:S(2)}) collective-permute-start(bf16[84,2688]{1,0:T(8,128)(2,1)S(1)} %get-tuple-element.73), channel_id=1, source_target_pairs={{0,24},{8,16},{16,8},{24,0},{1,25},{9,17},{17,9},{25,1},{2,26},{10... | collective-permute-start | bytes 1354760 | tf_op jit(solution)/shard_map/ppermute | solution.py:708
  92.4 11.2 %collective-permute-start.15 = (bf16[96,64]{1,0:T(8,128)(2,1)S(1)}, bf16[96,64]{1,0:T(8,128)(2,1)S(1)}, u32[]{:S(2)}, u32[]{:S(2)}) collective-permute-start(bf16[96,64]{1,0:T(8,128)(2,1)S(1)} %get-tuple-element.111), channel_id=1, source_target_pairs={{0,1},{1,0},{2,3},{3,2},{4,5},{5,4},{6,7},{7,6},{8,9},{9,8},{10,11... | collective-permute-start | bytes 36872 | tf_op jit(solution)/shard_map/ppermute | solution.py:266
  93.7 9.9 %collective-permute-start.16 = (bf16[96,64]{1,0:T(8,128)(2,1)S(1)}, bf16[96,64]{1,0:T(8,128)(2,1)S(1)}, u32[]{:S(2)}, u32[]{:S(2)}) collective-permute-start(bf16[96,64]{1,0:T(8,128)(2,1)S(1)} %get-tuple-element.112), channel_id=1, source_target_pairs={{0,3},{1,2},{2,1},{3,0},{4,7},{5,6},{6,5},{7,4},{8,11},{9,10},{10,... | collective-permute-start | bytes 36872 | tf_op jit(solution)/shard_map/ppermute | solution.py:267
  103.8 1.4 collective-permute-start.17
  112.4 9.5 %collective-permute-start.18 = (bf16[96,64]{1,0:T(8,128)(2,1)S(1)}, bf16[96,64]{1,0:T(8,128)(2,1)S(1)}, u32[]{:S(2)}, u32[]{:S(2)}) collective-permute-start(bf16[96,64]{1,0:T(8,128)(2,1)S(1)} %get-tuple-element.109), channel_id=1, source_target_pairs={{0,1},{1,0},{2,3},{3,2},{4,5},{5,4},{6,7},{7,6},{8,9},{9,8},{10,11... | collective-permute-start | bytes 36872 | tf_op jit(solution)/shard_map/ppermute | solution.py:266
  113.4 8.4 %collective-permute-start.19 = (bf16[96,64]{1,0:T(8,128)(2,1)S(1)}, bf16[96,64]{1,0:T(8,128)(2,1)S(1)}, u32[]{:S(2)}, u32[]{:S(2)}) collective-permute-start(bf16[96,64]{1,0:T(8,128)(2,1)S(1)} %get-tuple-element.110), channel_id=1, source_target_pairs={{0,3},{1,2},{2,1},{3,0},{4,7},{5,6},{6,5},{7,4},{8,11},{9,10},{10,... | collective-permute-start | bytes 36872 | tf_op jit(solution)/shard_map/ppermute | solution.py:267
  122.0 1.5 %collective-permute-start.20 = (f32[48,1024]{1,0:T(8,128)S(1)}, f32[48,1024]{1,0:T(8,128)S(1)}, u32[]{:S(2)}, u32[]{:S(2)}) collective-permute-start(f32[48,1024]{1,0:T(8,128)S(1)} %get-tuple-element.95), channel_id=1, source_target_pairs={{0,4},{4,0},{1,5},{5,1},{2,6},{6,2},{3,7},{7,3},{8,12},{12,8},{9,1... | collective-permute-start | bytes 589832 | tf_op jit(solution)/shard_map/ppermute | solution.py:708
  123.5 6.8 %collective-permute-start.21 = (f32[48,256]{1,0:T(8,128)S(1)}, f32[48,256]{1,0:T(8,128)S(1)}, u32[]{:S(2)}, u32[]{:S(2)}) collective-permute-start(f32[48,256]{1,0:T(8,128)S(1)} %get-tuple-element.97), channel_id=1, source_target_pairs={{0,8},{8,0},{16,24},{24,16},{1,9},{9,1},{17,25},{25,17},{2,10},{10... | collective-permute-start | bytes 147464 | tf_op jit(solution)/shard_map/ppermute | solution.py:708
  125.0 5.3 %collective-permute-start.22 = (f32[48,256]{1,0:T(8,128)S(1)}, f32[48,256]{1,0:T(8,128)S(1)}, u32[]{:S(2)}, u32[]{:S(2)}) collective-permute-start(f32[48,256]{1,0:T(8,128)S(1)} %get-tuple-element.98), channel_id=1, source_target_pairs={{0,16},{8,24},{16,0},{24,8},{1,17},{9,25},{17,1},{25,9},{2,18},{10... | collective-permute-start | bytes 147464 | tf_op jit(solution)/shard_map/ppermute | solution.py:708
  125.6 5.0 %collective-permute-start.23 = (f32[48,256]{1,0:T(8,128)S(1)}, f32[48,256]{1,0:T(8,128)S(1)}, u32[]{:S(2)}, u32[]{:S(2)}) collective-permute-start(f32[48,256]{1,0:T(8,128)S(1)} %get-tuple-element.99), channel_id=1, source_target_pairs={{0,24},{8,16},{16,8},{24,0},{1,25},{9,17},{17,9},{25,1},{2,26},{10... | collective-permute-start | bytes 147464 | tf_op jit(solution)/shard_map/ppermute | solution.py:708
  130.6 7.7 %collective-permute-start.26 = (f32[48,256]{1,0:T(8,128)S(1)}, f32[48,256]{1,0:T(8,128)S(1)}, u32[]{:S(2)}, u32[]{:S(2)}) collective-permute-start(f32[48,256]{1,0:T(8,128)S(1)} %add_add_fusion.1), channel_id=1, source_target_pairs={{0,3},{1,2},{2,1},{3,0},{4,7},{5,6},{6,5},{7,4},{8,11},{9,10},{10,... | collective-permute-start | bytes 147464 | tf_op jit(solution)/shard_map/ppermute | solution.py:708
  132.6 5.8 %collective-permute-start.25 = (f32[48,256]{1,0:T(8,128)S(1)}, f32[48,256]{1,0:T(8,128)S(1)}, u32[]{:S(2)}, u32[]{:S(2)}) collective-permute-start(f32[48,256]{1,0:T(8,128)S(1)} %add_add_fusion.1), channel_id=1, source_target_pairs={{0,2},{1,3},{2,0},{3,1},{4,6},{5,7},{6,4},{7,5},{8,10},{9,11},{10,... | collective-permute-start | bytes 147464 | tf_op jit(solution)/shard_map/ppermute | solution.py:708
  133.2 5.2 %collective-permute-start.24 = (f32[48,256]{1,0:T(8,128)S(1)}, f32[48,256]{1,0:T(8,128)S(1)}, u32[]{:S(2)}, u32[]{:S(2)}) collective-permute-start(f32[48,256]{1,0:T(8,128)S(1)} %add_add_fusion.1), channel_id=1, source_target_pairs={{0,1},{1,0},{2,3},{3,2},{4,5},{5,4},{6,7},{7,6},{8,9},{9,8},{10,11... | collective-permute-start | bytes 147464 | tf_op jit(solution)/shard_map/ppermute | solution.py:708
  138.4 5.1 %collective-permute-start.29 = (f32[48,256]{1,0:T(8,128)S(1)}, f32[48,256]{1,0:T(8,128)S(1)}, u32[]{:S(2)}, u32[]{:S(2)}) collective-permute-start(f32[48,256]{1,0:T(8,128)S(1)} %add_add_fusion.refs_0_), channel_id=1, source_target_pairs={{0,24},{8,16},{16,8},{24,0},{1,25},{9,17},{17,9},{25,1},{2,26},{10... | collective-permute-start | bytes 147464 | tf_op jit(solution)/shard_map/ppermute | solution.py:708
  139.9 4.1 %collective-permute-start.28 = (f32[48,256]{1,0:T(8,128)S(1)}, f32[48,256]{1,0:T(8,128)S(1)}, u32[]{:S(2)}, u32[]{:S(2)}) collective-permute-start(f32[48,256]{1,0:T(8,128)S(1)} %add_add_fusion.refs_0_), channel_id=1, source_target_pairs={{0,16},{8,24},{16,0},{24,8},{1,17},{9,25},{17,1},{25,9},{2,18},{10... | collective-permute-start | bytes 147464 | tf_op jit(solution)/shard_map/ppermute | solution.py:708
  141.5 4.1 %collective-permute-start.27 = (f32[48,256]{1,0:T(8,128)S(1)}, f32[48,256]{1,0:T(8,128)S(1)}, u32[]{:S(2)}, u32[]{:S(2)}) collective-permute-start(f32[48,256]{1,0:T(8,128)S(1)} %add_add_fusion.refs_0_), channel_id=1, source_target_pairs={{0,8},{8,0},{16,24},{24,16},{1,9},{9,1},{17,25},{25,17},{2,10},{10... | collective-permute-start | bytes 147464 | tf_op jit(solution)/shard_map/ppermute | solution.py:708
  145.6 1.5 %collective-permute-start.30 = (f32[48,1024]{1,0:T(8,128)S(1)}, f32[48,1024]{1,0:T(8,128)S(1)}, u32[]{:S(2)}, u32[]{:S(2)}) collective-permute-start(f32[48,1024]{1,0:T(8,128)S(1)} %join.1), channel_id=1, source_target_pairs={{0,4},{4,0},{1,5},{5,1},{2,6},{6,2},{3,7},{7,3},{8,12},{12,8},{9,1... | collective-permute-start | bytes 589832 | tf_op jit(solution)/shard_map/ppermute | solution.py:708

commit v2 on v1

--- a/solution.py
+++ b/solution.py
@@ -222,13 +222,14 @@
     ]
     for copy in copies:
         copy.start()
-    for copy in copies:
+    columns = {}
+    for number, (tile, copy) in enumerate(zip(tiles, copies)):
         copy.wait()
-    columns = []
-    for cell in places:
-        at = tiles.index(cell // LANES) * LANES + cell % LANES
-        columns.append(held[:, at : at + 1])
-    out_ref[...] = jnp.concatenate(columns, axis=1)
+        for cell in places:
+            if cell // LANES == tile:
+                at = number * LANES + cell % LANES
+                columns[cell] = held[:, at : at + 1]
+    out_ref[...] = jnp.concatenate([columns[cell] for cell in places], axis=1)
     row_copy.wait()
 
 
@@ -720,7 +721,7 @@
     return value
 
 
-def sum_all(keep, send, upper, between):
+def sum_all(keep, send, between):
     members = lax.axis_size("member")
     other = swap(send, "lat", 1)
     values = [keep, other]
@@ -731,14 +732,43 @@
     value = functools.reduce(jnp.add, moved, pieces[0])
     value = sum_axis(between(value), "lon", 1)
     value = between(value)
-    half = join_members([value] + [swap(value, "member", d) for d in range(1, members)])
-    other = swap(half, "lat", 1)
-    total = jnp.where(
-        upper,
-        jnp.concatenate([other, half], axis=0),
-        jnp.concatenate([half, other], axis=0),
-    )
-    return total
+    moved = [swap(value, "member", d) for d in range(1, members)]
+    moved[0] = between(moved[0])
+    half = join_members([value, *moved])
+    return half, swap(half, "lat", 1)
+
+
+def finish_kernel(taps, channels, fields, scale, own_ref, other_ref, out_ref, bias_ref, rows_ref,
+                  turned):
+    upper = lax.axis_index("lat") & 1
+    half = own_ref.shape[0]
+    rows_ref[pl.ds(pl.multiple_of(upper * half, 8), half), :] = own_ref[...]
+    rows_ref[pl.ds(pl.multiple_of((1 - upper) * half, 8), half), :] = other_ref[...]
+    turned[...] = (rows_ref[:, : turned.shape[0]] * scale).T
+    pieces = [
+        turned[pl.ds(channel, taps, stride=channels), :][:, :fields]
+        for channel in range(channels)
+    ]
+    out_ref[...] = jnp.concatenate(pieces, axis=1)
+    bias_ref[...] = turned[pl.ds(taps * channels, 1), :][:, :fields]
+
+
+def finish(own, other, taps, channels, fields, scale):
+    half, lanes = own.shape
+    used = round_up(taps * channels + 1, LANES)
+    return pl.pallas_call(
+        functools.partial(finish_kernel, taps, channels, fields, scale),
+        in_specs=[in_vmem()] * 2,
+        out_specs=[in_vmem()] * 2,
+        out_shape=[shape_of((taps, channels * fields), F32), shape_of((1, fields), F32)],
+        scratch_shapes=[
+            pltpu.VMEM((2 * half, lanes), F32),
+            pltpu.VMEM((used, 2 * half), F32),
+        ],
+        compiler_params=params((4 * half, lanes, 4), (used, LANES, 4), (16, channels * fields, 4)),
+        cost_estimate=cost(lanes, 8 * half * lanes),
+        name="finish",
+    )(own, other)
 
 
 def weights_kernel(taps_ref, forward_ref, backward_ref):
@@ -849,7 +879,7 @@
             end = part.shape[1] - grid.padded + cells
             outer_rows = (part[:, : grid.halo], part[:, end - grid.halo : end])
             g_top, g_bottom = lat_halo(*outer_rows, g_sides, first_lat)
-        for _ in range(0 if final else 2):
+        for _ in range(0 if final else 1):
             grad_input = input_part(
                 grid, *blocks.pop(), chunks[:1], parts[:1], g_sides, g_top, g_bottom,
                 backward_weight, grad_input, False,
@@ -857,7 +887,7 @@
 
     def between(value):
         nonlocal grad_input
-        for _ in range(min((len(blocks) + 1) // 2, len(blocks))):
+        for _ in range(min(1, len(blocks))):
             grad_input = input_part(
                 grid, *blocks.pop(), chunks, parts, g_sides, g_top, g_bottom, backward_weight,
                 grad_input, True,
@@ -865,16 +895,15 @@
             value, grad_input = lax.optimization_barrier((value, grad_input))
         return value
 
-    total = sum_all(*sums, upper, between)
+    own, other = sum_all(*sums, between)
     while blocks:
         grad_input = input_part(
             grid, *blocks.pop(), chunks, parts, g_sides, g_top, g_bottom, backward_weight,
             grad_input, True,
         )
-    total = total / (cells * lax.axis_size("lat") * lax.axis_size("lon"))
-    grad_weight = total[:fields, : 9 * channels].T.reshape(9, channels * fields)
-    grad_bias = total[:fields, 9 * channels]
-    return (grad_input.reshape(1, channels, 1, 1, cells), grad_weight, grad_bias)
+    everywhere = cells * lax.axis_size("lat") * lax.axis_size("lon")
+    grad_weight, grad_bias = finish(own, other, 9, channels, fields, 1.0 / everywhere)
+    return (grad_input.reshape(1, channels, 1, 1, cells), grad_weight, grad_bias[0])
 
 
 def solution(mesh):

time: 149 us -> 149 us (level)
  local copies, waits for them, and re-layouts: 3.18 us -> 1.07 us
  transfers between devices with their start and end apart: 31 -> 31, of which waited for: 16 -> 15; matrix products, arithmetic and copies ran while one was open for 1% -> 1% of each run, Pallas kernels for 26% -> 26%
where the time goes in v2:
time: 149 us; the launch traced here: 148 us
  Pallas kernels  51.4 us (34%)
  waiting for transfers between devices  51.3 us (34%)
  starting transfers between devices  43 us (29%)
    ppermute x23, waiting for transfers between devices, swap(): lax.ppermute(value, axis, [(i, i ^ bits) for i in range(lax.axis_size(axi...  47.9 us
    ppermute x23, starting transfers between devices, swap(): lax.ppermute(value, axis, [(i, i ^ bits) for i in range(lax.axis_size(axi...  30 us
    pallas_call x2, Pallas kernels, weight_part(): pl.pallas_call(functools.partial(weight_kernel, grid, ranges, len(chained...  13.8 us
    pallas_call x4, Pallas kernels, input_part(): pl.pallas_call(functools.partial(input_kernel, grid, r0, r1, chunks, len(...  12.9 us
    pallas_call x2, Pallas kernels, forward(): pl.pallas_call(functools.partial(forward_kernel, grid, ranges, has_top, h...  12.8 us
    pallas_call x2, Pallas kernels, score(): pl.pallas_call(functools.partial(score_kernel, members), in_specs=[in_vme...  6.01 us
    ppermute x2, starting transfers between devices, lon_halo(): outer = lax.ppermute(jnp.where(odd, last, first), 'lon', far)  5.09 us
    pallas_call x1, Pallas kernels, edges_of(): pl.pallas_call(functools.partial(edges_kernel, grid, places, tiles), in_s...  3.05 us
  transfers between devices with their start and end apart: 31, of which 15 were waited for; matrix products, arithmetic and copies ran while one was open for 1% of the time, Pallas kernels for 26%

profile of v2, /device:TPU:0, one launch (start us, length us, event | category | flops | bytes accessed | tf_op | source)
XLA Modules:
  0.0 148.4 jit_solution(8615834749266723838)
XLA Ops:
  0.7 3.0 %edges.1 = (bf16[96,128]{1,0:T(8,128)(2,1)S(1)}, bf16[96,384]{1,0:T(8,128)(2,1)S(1)}) custom-call(bf16[96,23040]{1,0:T(8,128)(2,1)} %bitcast.6), custom_call_target="tpu_custom_call" | custom-call | flops 96 | bytes 96 | tf_op jit(solution)/shard_map/edges/pallas_call | solution.py:241
  3.8 3.0 %collective-permute-start = (bf16[96,64]{1,0:T(8,128)(2,1)S(1)}, bf16[96,64]{1,0:T(8,128)(2,1)S(1)}, u32[]{:S(2)}, u32[]{:S(2)}) collective-permute-start(bf16[96,64]{1,0:T(8,128)(2,1)S(1)} %get-tuple-element.121), channel_id=1, source_target_pairs={{0,1},{1,2},{2,3},{3,0},{4,5},{5,6},{6,7},{7,4},{8,9},{9,10},{10,1... | collective-permute-start | bytes 36872 | tf_op jit(solution)/shard_map/ppermute | solution.py:263
  6.8 2.1 %collective-permute-start.1 = (bf16[96,64]{1,0:T(8,128)(2,1)S(1)}, bf16[96,64]{1,0:T(8,128)(2,1)S(1)}, u32[]{:S(2)}, u32[]{:S(2)}) collective-permute-start(bf16[96,64]{1,0:T(8,128)(2,1)S(1)} %get-tuple-element.122), channel_id=1, source_target_pairs={{1,0},{2,1},{3,2},{0,3},{5,4},{6,5},{7,6},{4,7},{9,8},{10,9},{11,1... | collective-permute-start | bytes 36872 | tf_op jit(solution)/shard_map/ppermute | solution.py:263
  10.0 0.8 collective-permute-done
  11.3 1.2 collective-permute-done.2
  12.5 7.4 %forward_0.1 = (bf16[84,3072]{1,0:T(8,128)(2,1)S(1)}, bf16[84,3072]{1,0:T(8,128)(2,1)S(1)}, bf16[84,3072]{1,0:T(8,128)(2,1)S(1)}, bf16[84,3072]{1,0:T(8,128)(2,1...) custom-call(bf16[96,23040]{1,0:T(8,128)(2,1)} %bitcast.7, ...), custom_call_target="tpu_custom_call" | custom-call | flops 8026324992 | tf_op jit(solution)/shard_map/forward_0/pallas_call | solution.py:391
  19.9 1.6 %collective-permute-start.9 = (bf16[84,3072]{1,0:T(8,128)(2,1)S(1)}, bf16[84,3072]{1,0:T(8,128)(2,1)S(1)}, u32[]{:S(2)}, u32[]{:S(2)}) collective-permute-start(bf16[84,3072]{1,0:T(8,128)(2,1)S(1)} %get-tuple-element.80), channel_id=1, source_target_pairs={{0,8},{8,0},{16,24},{24,16},{1,9},{9,1},{17,25},{25,17},{2,10},{10... | collective-permute-start | bytes 1548296 | tf_op jit(solution)/shard_map/ppermute | solution.py:709
  21.5 1.5 %collective-permute-start.10 = (bf16[84,3072]{1,0:T(8,128)(2,1)S(1)}, bf16[84,3072]{1,0:T(8,128)(2,1)S(1)}, u32[]{:S(2)}, u32[]{:S(2)}) collective-permute-start(bf16[84,3072]{1,0:T(8,128)(2,1)S(1)} %get-tuple-element.81), channel_id=1, source_target_pairs={{0,16},{8,24},{16,0},{24,8},{1,17},{9,25},{17,1},{25,9},{2,18},{10... | collective-permute-start | bytes 1548296 | tf_op jit(solution)/shard_map/ppermute | solution.py:709
  23.5 5.4 %forward_6144.1 = (bf16[84,2688]{1,0:T(8,128)(2,1)S(1)}, bf16[84,2688]{1,0:T(8,128)(2,1)S(1)}, bf16[84,2688]{1,0:T(8,128)(2,1)S(1)}, bf16[84,2688]{1,0:T(8,128)(...) custom-call(bf16[96,23040]{1,0:T(8,128)(2,1)S(1)} %get-tuple-element.67.refs_0_, ...), custom_call_target="tpu_custom_call" | custom-call | flops 7023034368 | tf_op jit(solution)/shard_map/forward_6144/pallas_call | solution.py:391
  28.9 1.6 %collective-permute-start.3 = (bf16[84,2688]{1,0:T(8,128)(2,1)S(1)}, bf16[84,2688]{1,0:T(8,128)(2,1)S(1)}, u32[]{:S(2)}, u32[]{:S(2)}) collective-permute-start(bf16[84,2688]{1,0:T(8,128)(2,1)S(1)} %get-tuple-element.71), channel_id=1, source_target_pairs={{0,8},{8,0},{16,24},{24,16},{1,9},{9,1},{17,25},{25,17},{2,10},{10... | collective-permute-start | bytes 1354760 | tf_op jit(solution)/shard_map/ppermute | solution.py:709
  30.4 1.5 %collective-permute-start.4 = (bf16[84,2688]{1,0:T(8,128)(2,1)S(1)}, bf16[84,2688]{1,0:T(8,128)(2,1)S(1)}, u32[]{:S(2)}, u32[]{:S(2)}) collective-permute-start(bf16[84,2688]{1,0:T(8,128)(2,1)S(1)} %get-tuple-element.72), channel_id=1, source_target_pairs={{0,16},{8,24},{16,0},{24,8},{1,17},{9,25},{17,1},{25,9},{2,18},{10... | collective-permute-start | bytes 1354760 | tf_op jit(solution)/shard_map/ppermute | solution.py:709
  32.0 3.1 %collective-permute-done.9.refs_1_ = bf16[84,3072]{1,0:T(8,128)(2,1)S(1)} collective-permute-done((bf16[84,3072]{1,0:T(8,128)(2,1)S(1)}, bf16[84,3072]{1,0:T(8,128)(2,1)S(1)}, u32[]{:S(2)}, u32[]{:S(2)}) %collective-permute-start.9) | collective-permute-done | bytes 516128 | tf_op jit(solution)/shard_map/ppermute | solution.py:709
  35.1 2.5 %collective-permute-start.5 = (bf16[84,2688]{1,0:T(8,128)(2,1)S(1)}, bf16[84,2688]{1,0:T(8,128)(2,1)S(1)}, u32[]{:S(2)}, u32[]{:S(2)}) collective-permute-start(bf16[84,2688]{1,0:T(8,128)(2,1)S(1)} %get-tuple-element.73), channel_id=1, source_target_pairs={{0,24},{8,16},{16,8},{24,0},{1,25},{9,17},{17,9},{25,1},{2,26},{10... | collective-permute-start | bytes 1354760 | tf_op jit(solution)/shard_map/ppermute | solution.py:709
  37.6 10.6 %collective-permute-done.10.refs_2_ = bf16[84,3072]{1,0:T(8,128)(2,1)S(1)} collective-permute-done((bf16[84,3072]{1,0:T(8,128)(2,1)S(1)}, bf16[84,3072]{1,0:T(8,128)(2,1)S(1)}, u32[]{:S(2)}, u32[]{:S(2)}) %collective-permute-start.10) | collective-permute-done | bytes 516128 | tf_op jit(solution)/shard_map/ppermute | solution.py:709
  48.2 3.1 %score_0.1 = (bf16[84,3072]{1,0:T(8,128)(2,1)S(1)}, bf16[84,3072]{1,0:T(8,128)(2,1)S(1)}, bf16[84,3072]{1,0:T(8,128)(2,1)S(1)}, bf16[84,3072]{1,0:T(8,128)(2,1)S(1)}) custom-call(bf16[84,3072]{1,0:T(8,128)(2,1)S(1)} %get-tuple-element.78.target_ref, f32[84,128]{1,0:T(8,128)S(1)} %broadcast_in_dim.4.scale_ref, ...), custom_call_target="tpu_custom_call" | custom-call | flops 3354624000 | tf_op jit(solution)/shard_map/score_0/pallas_call | solution.py:453
  51.4 1.1 collective-permute-start.12
  52.4 1.1 collective-permute-start.13
  53.5 3.4 %collective-permute-done.3.refs_1_ = bf16[84,2688]{1,0:T(8,128)(2,1)S(1)} collective-permute-done((bf16[84,2688]{1,0:T(8,128)(2,1)S(1)}, bf16[84,2688]{1,0:T(8,128)(2,1)S(1)}, u32[]{:S(2)}, u32[]{:S(2)}) %collective-permute-start.3) | collective-permute-done | bytes 451616 | tf_op jit(solution)/shard_map/ppermute | solution.py:709
  56.9 2.5 %collective-permute-start.14 = (bf16[84,3072]{1,0:T(8,128)(2,1)S(1)}, bf16[84,3072]{1,0:T(8,128)(2,1)S(1)}, u32[]{:S(2)}, u32[]{:S(2)}) collective-permute-start(bf16[84,3072]{1,0:T(8,128)(2,1)S(1)} %get-tuple-element.86), channel_id=1, source_target_pairs={{0,24},{8,16},{16,8},{24,0},{1,25},{9,17},{17,9},{25,1},{2,26},{10... | collective-permute-start | bytes 1548296 | tf_op jit(solution)/shard_map/ppermute | solution.py:709
  59.3 9.1 %collective-permute-done.4.refs_2_ = bf16[84,2688]{1,0:T(8,128)(2,1)S(1)} collective-permute-done((bf16[84,2688]{1,0:T(8,128)(2,1)S(1)}, bf16[84,2688]{1,0:T(8,128)(2,1)S(1)}, u32[]{:S(2)}, u32[]{:S(2)}) %collective-permute-start.4) | collective-permute-done | bytes 451616 | tf_op jit(solution)/shard_map/ppermute | solution.py:709
  68.5 2.9 %score_6144.1 = (bf16[84,2688]{1,0:T(8,128)(2,1)S(1)}, bf16[84,2688]{1,0:T(8,128)(2,1)S(1)}, bf16[84,2688]{1,0:T(8,128)(2,1)S(1)}, bf16[84,2688]{1,0:T(8,128)(2,1)S(1)}) custom-call(bf16[84,2688]{1,0:T(8,128)(2,1)S(1)} %get-tuple-element.68.target_ref.refs_4_, f32[84,128]{1,0:T(8,128)S(1)} %broadcast_in_dim.4.scale_ref, ...), custom_call_target="tpu_custom_call" | custom-call | flops 2935296000 | tf_op jit(solution)/shard_map/score_6144/pallas_call | solution.py:453
  71.4 1.1 collective-permute-start.6
  72.5 1.0 collective-permute-start.7
  73.5 5.1 %collective-permute-done.12.refs_1_ = bf16[84,3072]{1,0:T(8,128)(2,1)S(1)} collective-permute-done((bf16[84,3072]{1,0:T(8,128)(2,1)S(1)}, bf16[84,3072]{1,0:T(8,128)(2,1)S(1)}, u32[]{:S(2)}, u32[]{:S(2)}) %collective-permute-start.12) | collective-permute-done | bytes 516128 | tf_op jit(solution)/shard_map/ppermute | solution.py:709
  78.6 2.5 %collective-permute-start.8 = (bf16[84,2688]{1,0:T(8,128)(2,1)S(1)}, bf16[84,2688]{1,0:T(8,128)(2,1)S(1)}, u32[]{:S(2)}, u32[]{:S(2)}) collective-permute-start(bf16[84,2688]{1,0:T(8,128)(2,1)S(1)} %get-tuple-element.77), channel_id=1, source_target_pairs={{0,24},{8,16},{16,8},{24,0},{1,25},{9,17},{17,9},{25,1},{2,26},{10... | collective-permute-start | bytes 1354760 | tf_op jit(solution)/shard_map/ppermute | solution.py:709
  81.1 10.6 %collective-permute-done.13.refs_2_ = bf16[84,3072]{1,0:T(8,128)(2,1)S(1)} collective-permute-done((bf16[84,3072]{1,0:T(8,128)(2,1)S(1)}, bf16[84,3072]{1,0:T(8,128)(2,1)S(1)}, u32[]{:S(2)}, u32[]{:S(2)}) %collective-permute-start.13) | collective-permute-done | bytes 516128 | tf_op jit(solution)/shard_map/ppermute | solution.py:709
  92.4 1.3 collective-permute-start.15
  93.8 2.5 %collective-permute-start.16 = (bf16[96,64]{1,0:T(8,128)(2,1)S(1)}, bf16[96,64]{1,0:T(8,128)(2,1)S(1)}, u32[]{:S(2)}, u32[]{:S(2)}) collective-permute-start(bf16[96,64]{1,0:T(8,128)(2,1)S(1)} %get-tuple-element.120), channel_id=1, source_target_pairs={{0,3},{1,2},{2,1},{3,0},{4,7},{5,6},{6,5},{7,4},{8,11},{9,10},{10,... | collective-permute-start | bytes 36872 | tf_op jit(solution)/shard_map/ppermute | solution.py:268
  96.3 7.3 %weight_0.1.refs_0_ = f32[96,1024]{1,0:T(8,128)S(1)} custom-call(bf16[288,15360]{1,0:T(8,128)(2,1)S(1)} %get-tuple-element.89.taps, bf16[96,12288]{1,0:T(8,128)(2,1)S(1)} %get-tuple-element.87.part_ref.refs_0_), custom_call_target="tpu_custom_call" | custom-call | flops 12288 | tf_op jit(solution)/shard_map/weight_0/pallas_call | solution.py:567
  103.9 1.3 collective-permute-done.17
  105.2 3.2 %input_48.1.refs_4_ = bf16[96,23040]{1,0:T(8,128)(2,1)} custom-call(bf16[96,12288]{1,0:T(8,128)(2,1)S(1)} %get-tuple-element.87.part_ref.refs_0_, bf16[96,128]{1,0:T(8,128)(2,1)S(1)} %maximum_select_fusion.refs_1_, bf16[96,864]{1,0:T(8,128)(2,1)S(1)} %get-tuple-element.91.refs_2_.refs_3_, bf16[96,512]{1,0:T(8,128)(2,1)S(1)} %get-tuple-element.114.refs_3_), custom_call_target="tpu_custom_call" | custom-call | flops 53084160 | bytes 5760 | tf_op jit(solution)/shard_map/input_48/pallas_call | solution.py:639
  108.4 2.4 %collective-permute-done.7.refs_2_ = bf16[84,2688]{1,0:T(8,128)(2,1)S(1)} collective-permute-done((bf16[84,2688]{1,0:T(8,128)(2,1)S(1)}, bf16[84,2688]{1,0:T(8,128)(2,1)S(1)}, u32[]{:S(2)}, u32[]{:S(2)}) %collective-permute-start.7) | collective-permute-done | bytes 451616 | tf_op jit(solution)/shard_map/ppermute | solution.py:709
  111.5 1.3 collective-permute-start.18
  112.9 2.5 %collective-permute-start.19 = (bf16[96,64]{1,0:T(8,128)(2,1)S(1)}, bf16[96,64]{1,0:T(8,128)(2,1)S(1)}, u32[]{:S(2)}, u32[]{:S(2)}) collective-permute-start(bf16[96,64]{1,0:T(8,128)(2,1)S(1)} %get-tuple-element.118), channel_id=1, source_target_pairs={{0,3},{1,2},{2,1},{3,0},{4,7},{5,6},{6,5},{7,4},{8,11},{9,10},{10,... | collective-permute-start | bytes 36872 | tf_op jit(solution)/shard_map/ppermute | solution.py:268
  115.4 6.5 %weight_6144.1 = (f32[48,1024]{1,0:T(8,128)S(1)}, f32[48,1024]{1,0:T(8,128)S(1)}) custom-call(bf16[288,12288]{1,0:T(8,128)(2,1)S(1)} %get-tuple-element.93.taps, bf16[96,10752]{1,0:T(8,128)(2,1)S(1)} %get-tuple-element.94.part_ref.refs_1_, f32[96,1024]{1,0:T(8,128)S(1)} %weight_0.1.refs_0_), custom_call_target="tpu_custom_call" | custom-call | flops 10752 | tf_op jit(solution)/shard_map/weight_6144/pallas_call | solution.py:567
  122.1 1.4 collective-permute-done.20.refs_1_
  123.5 1.5 collective-permute-start.21
  125.7 1.4 collective-permute-start.23
  127.1 3.2 %input_0.1.refs_4_ = bf16[96,23040]{1,0:T(8,128)(2,1)} custom-call(bf16[96,12288]{1,0:T(8,128)(2,1)S(1)} %get-tuple-element.87.part_ref.refs_0_, bf16[96,128]{1,0:T(8,128)(2,1)S(1)} %add.24.refs_1_.refs_2_, bf16[96,864]{1,0:T(8,128)(2,1)S(1)} %get-tuple-element.91.refs_2_.refs_3_, ...), custom_call_target="tpu_custom_call", output_to_operand_aliasing={{}: (4, {})} | custom-call | flops 4246732800 | bytes 5760 | tf_op jit(solution)/shard_map/input_0/pallas_call | solution.py:639
  130.7 1.3 collective-permute-start.26
  132.0 1.2 collective-permute-start.25
  133.2 1.9 %collective-permute-start.24 = (f32[48,256]{1,0:T(8,128)S(1)}, f32[48,256]{1,0:T(8,128)S(1)}, u32[]{:S(2)}, u32[]{:S(2)}) collective-permute-start(f32[48,256]{1,0:T(8,128)S(1)} %add_add_fusion.1), channel_id=1, source_target_pairs={{0,1},{1,0},{2,3},{3,2},{4,5},{5,4},{6,7},{7,6},{8,9},{9,8},{10,11... | collective-permute-start | bytes 147464 | tf_op jit(solution)/shard_map/ppermute | solution.py:709
  135.1 3.2 %input_32.1.refs_4_ = bf16[96,23040]{1,0:T(8,128)(2,1)} custom-call(bf16[96,12288]{1,0:T(8,128)(2,1)S(1)} %get-tuple-element.87.part_ref.refs_0_, bf16[96,10752]{1,0:T(8,128)(2,1)S(1)} %get-tuple-element.94.part_ref.refs_1_, bf16[96,128]{1,0:T(8,128)(2,1)S(1)} %add.24.refs_1_.refs_2_, ...), custom_call_target="tpu_custom_call", output_to_operand_aliasing={{}: (4, {})} | custom-call | flops 4246732800 | bytes 5760 | tf_op jit(solution)/shard_map/input_32/pallas_call | solution.py:639
  138.4 1.5 %collective-permute-start.29 = (f32[48,256]{1,0:T(8,128)S(1)}, f32[48,256]{1,0:T(8,128)S(1)}, u32[]{:S(2)}, u32[]{:S(2)}) collective-permute-start(f32[48,256]{1,0:T(8,128)S(1)} %add_add_fusion.refs_0_), channel_id=1, source_target_pairs={{0,24},{8,16},{16,8},{24,0},{1,25},{9,17},{17,9},{25,1},{2,26},{10... | collective-permute-start | bytes 147464 | tf_op jit(solution)/shard_map/ppermute | solution.py:709
  139.9 1.6 %collective-permute-start.28 = (f32[48,256]{1,0:T(8,128)S(1)}, f32[48,256]{1,0:T(8,128)S(1)}, u32[]{:S(2)}, u32[]{:S(2)}) collective-permute-start(f32[48,256]{1,0:T(8,128)S(1)} %add_add_fusion.refs_0_), channel_id=1, source_target_pairs={{0,16},{8,24},{16,0},{24,8},{1,17},{9,25},{17,1},{25,9},{2,18},{10... | collective-permute-start | bytes 147464 | tf_op jit(solution)/shard_map/ppermute | solution.py:709
  142.0 3.3 %input_16.1 = bf16[96,23040]{1,0:T(8,128)(2,1)} custom-call(bf16[96,12288]{1,0:T(8,128)(2,1)S(1)} %get-tuple-element.87.part_ref.refs_0_, bf16[96,10752]{1,0:T(8,128)(2,1)S(1)} %get-tuple-element.94.part_ref.refs_1_, bf16[96,128]{1,0:T(8,128)(2,1)S(1)} %add.24.refs_1_.refs_2_, ...), custom_call_target="tpu_custom_call", output_to_operand_aliasing={{}: (4, {})} | custom-call | flops 4246732800 | bytes 5760 | tf_op jit(solution)/shard_map/input_16/pallas_call | solution.py:639
  145.7 1.4 collective-permute-done.30.other_ref
  147.1 1.3 finish.1
  (54 shorter events, 5.9 us)
Async XLA Ops:
  0.6 8.3 %copy-start = (bf16[9,8064]{1,0:T(8,128)(2,1)S(1)}, bf16[9,8064]{1,0:T(8,128)(2,1)}, u32[]{:S(2)}) copy-start(bf16[9,8064]{1,0:T(8,128)(2,1)} %param.6) | copy-start | bytes 435460
  0.6 10.5 %copy-start.2 = (f32[84]{0:T(128)S(1)}, f32[84]{0:T(128)}, u32[]{:S(2)}) copy-start(f32[84]{0:T(128)} %param.7) | copy-start | bytes 1012
  0.7 10.3 %copy-start.1 = (f32[84]{0:T(128)S(1)}, f32[84]{0:T(128)}, u32[]{:S(2)}) copy-start(f32[84]{0:T(128)} %param.9) | copy-start | bytes 1012
  3.8 7.0 %collective-permute-start = (bf16[96,64]{1,0:T(8,128)(2,1)S(1)}, bf16[96,64]{1,0:T(8,128)(2,1)S(1)}, u32[]{:S(2)}, u32[]{:S(2)}) collective-permute-start(bf16[96,64]{1,0:T(8,128)(2,1)S(1)} %get-tuple-element.121), channel_id=1, source_target_pairs={{0,1},{1,2},{2,3},{3,0},{4,5},{5,6},{6,7},{7,4},{8,9},{9,10},{10,1... | collective-permute-start | bytes 36872 | tf_op jit(solution)/shard_map/ppermute | solution.py:263
  6.8 4.1 %collective-permute-start.1 = (bf16[96,64]{1,0:T(8,128)(2,1)S(1)}, bf16[96,64]{1,0:T(8,128)(2,1)S(1)}, u32[]{:S(2)}, u32[]{:S(2)}) collective-permute-start(bf16[96,64]{1,0:T(8,128)(2,1)S(1)} %get-tuple-element.122), channel_id=1, source_target_pairs={{1,0},{2,1},{3,2},{0,3},{5,4},{6,5},{7,6},{4,7},{9,8},{10,9},{11,1... | collective-permute-start | bytes 36872 | tf_op jit(solution)/shard_map/ppermute | solution.py:263
  11.1 1.4 collective-permute-start.2
  19.9 15.2 %collective-permute-start.9 = (bf16[84,3072]{1,0:T(8,128)(2,1)S(1)}, bf16[84,3072]{1,0:T(8,128)(2,1)S(1)}, u32[]{:S(2)}, u32[]{:S(2)}) collective-permute-start(bf16[84,3072]{1,0:T(8,128)(2,1)S(1)} %get-tuple-element.80), channel_id=1, source_target_pairs={{0,8},{8,0},{16,24},{24,16},{1,9},{9,1},{17,25},{25,17},{2,10},{10... | collective-permute-start | bytes 1548296 | tf_op jit(solution)/shard_map/ppermute | solution.py:709
  21.5 26.7 %collective-permute-start.10 = (bf16[84,3072]{1,0:T(8,128)(2,1)S(1)}, bf16[84,3072]{1,0:T(8,128)(2,1)S(1)}, u32[]{:S(2)}, u32[]{:S(2)}) collective-permute-start(bf16[84,3072]{1,0:T(8,128)(2,1)S(1)} %get-tuple-element.81), channel_id=1, source_target_pairs={{0,16},{8,24},{16,0},{24,8},{1,17},{9,25},{17,1},{25,9},{2,18},{10... | collective-permute-start | bytes 1548296 | tf_op jit(solution)/shard_map/ppermute | solution.py:709
  23.0 25.2 %collective-permute-start.11 = (bf16[84,3072]{1,0:T(8,128)(2,1)S(1)}, bf16[84,3072]{1,0:T(8,128)(2,1)S(1)}, u32[]{:S(2)}, u32[]{:S(2)}) collective-permute-start(bf16[84,3072]{1,0:T(8,128)(2,1)S(1)} %get-tuple-element.82), channel_id=1, source_target_pairs={{0,24},{8,16},{16,8},{24,0},{1,25},{9,17},{17,9},{25,1},{2,26},{10... | collective-permute-start | bytes 1548296 | tf_op jit(solution)/shard_map/ppermute | solution.py:709
  28.9 28.0 %collective-permute-start.3 = (bf16[84,2688]{1,0:T(8,128)(2,1)S(1)}, bf16[84,2688]{1,0:T(8,128)(2,1)S(1)}, u32[]{:S(2)}, u32[]{:S(2)}) collective-permute-start(bf16[84,2688]{1,0:T(8,128)(2,1)S(1)} %get-tuple-element.71), channel_id=1, source_target_pairs={{0,8},{8,0},{16,24},{24,16},{1,9},{9,1},{17,25},{25,17},{2,10},{10... | collective-permute-start | bytes 1354760 | tf_op jit(solution)/shard_map/ppermute | solution.py:709
  30.4 38.1 %collective-permute-start.4 = (bf16[84,2688]{1,0:T(8,128)(2,1)S(1)}, bf16[84,2688]{1,0:T(8,128)(2,1)S(1)}, u32[]{:S(2)}, u32[]{:S(2)}) collective-permute-start(bf16[84,2688]{1,0:T(8,128)(2,1)S(1)} %get-tuple-element.72), channel_id=1, source_target_pairs={{0,16},{8,24},{16,0},{24,8},{1,17},{9,25},{17,1},{25,9},{2,18},{10... | collective-permute-start | bytes 1354760 | tf_op jit(solution)/shard_map/ppermute | solution.py:709
  35.1 33.4 %collective-permute-start.5 = (bf16[84,2688]{1,0:T(8,128)(2,1)S(1)}, bf16[84,2688]{1,0:T(8,128)(2,1)S(1)}, u32[]{:S(2)}, u32[]{:S(2)}) collective-permute-start(bf16[84,2688]{1,0:T(8,128)(2,1)S(1)} %get-tuple-element.73), channel_id=1, source_target_pairs={{0,24},{8,16},{16,8},{24,0},{1,25},{9,17},{17,9},{25,1},{2,26},{10... | collective-permute-start | bytes 1354760 | tf_op jit(solution)/shard_map/ppermute | solution.py:709
  51.4 27.3 %collective-permute-start.12 = (bf16[84,3072]{1,0:T(8,128)(2,1)S(1)}, bf16[84,3072]{1,0:T(8,128)(2,1)S(1)}, u32[]{:S(2)}, u32[]{:S(2)}) collective-permute-start(bf16[84,3072]{1,0:T(8,128)(2,1)S(1)} %get-tuple-element.84), channel_id=1, source_target_pairs={{0,8},{8,0},{16,24},{24,16},{1,9},{9,1},{17,25},{25,17},{2,10},{10... | collective-permute-start | bytes 1548296 | tf_op jit(solution)/shard_map/ppermute | solution.py:709
  52.4 39.3 %collective-permute-start.13 = (bf16[84,3072]{1,0:T(8,128)(2,1)S(1)}, bf16[84,3072]{1,0:T(8,128)(2,1)S(1)}, u32[]{:S(2)}, u32[]{:S(2)}) collective-permute-start(bf16[84,3072]{1,0:T(8,128)(2,1)S(1)} %get-tuple-element.85), channel_id=1, source_target_pairs={{0,16},{8,24},{16,0},{24,8},{1,17},{9,25},{17,1},{25,9},{2,18},{10... | collective-permute-start | bytes 1548296 | tf_op jit(solution)/shard_map/ppermute | solution.py:709
  56.9 34.8 %collective-permute-start.14 = (bf16[84,3072]{1,0:T(8,128)(2,1)S(1)}, bf16[84,3072]{1,0:T(8,128)(2,1)S(1)}, u32[]{:S(2)}, u32[]{:S(2)}) collective-permute-start(bf16[84,3072]{1,0:T(8,128)(2,1)S(1)} %get-tuple-element.86), channel_id=1, source_target_pairs={{0,24},{8,16},{16,8},{24,0},{1,25},{9,17},{17,9},{25,1},{2,26},{10... | collective-permute-start | bytes 1548296 | tf_op jit(solution)/shard_map/ppermute | solution.py:709
  71.4 37.0 %collective-permute-start.6 = (bf16[84,2688]{1,0:T(8,128)(2,1)S(1)}, bf16[84,2688]{1,0:T(8,128)(2,1)S(1)}, u32[]{:S(2)}, u32[]{:S(2)}) collective-permute-start(bf16[84,2688]{1,0:T(8,128)(2,1)S(1)} %get-tuple-element.75), channel_id=1, source_target_pairs={{0,8},{8,0},{16,24},{24,16},{1,9},{9,1},{17,25},{25,17},{2,10},{10... | collective-permute-start | bytes 1354760 | tf_op jit(solution)/shard_map/ppermute | solution.py:709
  72.5 38.3 %collective-permute-start.7 = (bf16[84,2688]{1,0:T(8,128)(2,1)S(1)}, bf16[84,2688]{1,0:T(8,128)(2,1)S(1)}, u32[]{:S(2)}, u32[]{:S(2)}) collective-permute-start(bf16[84,2688]{1,0:T(8,128)(2,1)S(1)} %get-tuple-element.76), channel_id=1, source_target_pairs={{0,16},{8,24},{16,0},{24,8},{1,17},{9,25},{17,1},{25,9},{2,18},{10... | collective-permute-start | bytes 1354760 | tf_op jit(solution)/shard_map/ppermute | solution.py:709
  78.6 32.2 %collective-permute-start.8 = (bf16[84,2688]{1,0:T(8,128)(2,1)S(1)}, bf16[84,2688]{1,0:T(8,128)(2,1)S(1)}, u32[]{:S(2)}, u32[]{:S(2)}) collective-permute-start(bf16[84,2688]{1,0:T(8,128)(2,1)S(1)} %get-tuple-element.77), channel_id=1, source_target_pairs={{0,24},{8,16},{16,8},{24,0},{1,25},{9,17},{17,9},{25,1},{2,26},{10... | collective-permute-start | bytes 1354760 | tf_op jit(solution)/shard_map/ppermute | solution.py:709
  92.4 11.2 %collective-permute-start.15 = (bf16[96,64]{1,0:T(8,128)(2,1)S(1)}, bf16[96,64]{1,0:T(8,128)(2,1)S(1)}, u32[]{:S(2)}, u32[]{:S(2)}) collective-permute-start(bf16[96,64]{1,0:T(8,128)(2,1)S(1)} %get-tuple-element.119), channel_id=1, source_target_pairs={{0,1},{1,0},{2,3},{3,2},{4,5},{5,4},{6,7},{7,6},{8,9},{9,8},{10,11... | collective-permute-start | bytes 36872 | tf_op jit(solution)/shard_map/ppermute | solution.py:267
  93.8 9.9 %collective-permute-start.16 = (bf16[96,64]{1,0:T(8,128)(2,1)S(1)}, bf16[96,64]{1,0:T(8,128)(2,1)S(1)}, u32[]{:S(2)}, u32[]{:S(2)}) collective-permute-start(bf16[96,64]{1,0:T(8,128)(2,1)S(1)} %get-tuple-element.120), channel_id=1, source_target_pairs={{0,3},{1,2},{2,1},{3,0},{4,7},{5,6},{6,5},{7,4},{8,11},{9,10},{10,... | collective-permute-start | bytes 36872 | tf_op jit(solution)/shard_map/ppermute | solution.py:268
  103.8 1.4 collective-permute-start.17
  111.5 10.4 %collective-permute-start.18 = (bf16[96,64]{1,0:T(8,128)(2,1)S(1)}, bf16[96,64]{1,0:T(8,128)(2,1)S(1)}, u32[]{:S(2)}, u32[]{:S(2)}) collective-permute-start(bf16[96,64]{1,0:T(8,128)(2,1)S(1)} %get-tuple-element.117), channel_id=1, source_target_pairs={{0,1},{1,0},{2,3},{3,2},{4,5},{5,4},{6,7},{7,6},{8,9},{9,8},{10,11... | collective-permute-start | bytes 36872 | tf_op jit(solution)/shard_map/ppermute | solution.py:267
  112.9 9.0 %collective-permute-start.19 = (bf16[96,64]{1,0:T(8,128)(2,1)S(1)}, bf16[96,64]{1,0:T(8,128)(2,1)S(1)}, u32[]{:S(2)}, u32[]{:S(2)}) collective-permute-start(bf16[96,64]{1,0:T(8,128)(2,1)S(1)} %get-tuple-element.118), channel_id=1, source_target_pairs={{0,3},{1,2},{2,1},{3,0},{4,7},{5,6},{6,5},{7,4},{8,11},{9,10},{10,... | collective-permute-start | bytes 36872 | tf_op jit(solution)/shard_map/ppermute | solution.py:268
  122.0 1.5 %collective-permute-start.20 = (f32[48,1024]{1,0:T(8,128)S(1)}, f32[48,1024]{1,0:T(8,128)S(1)}, u32[]{:S(2)}, u32[]{:S(2)}) collective-permute-start(f32[48,1024]{1,0:T(8,128)S(1)} %get-tuple-element.99), channel_id=1, source_target_pairs={{0,4},{4,0},{1,5},{5,1},{2,6},{6,2},{3,7},{7,3},{8,12},{12,8},{9,1... | collective-permute-start | bytes 589832 | tf_op jit(solution)/shard_map/ppermute | solution.py:709
  123.5 6.8 %collective-permute-start.21 = (f32[48,256]{1,0:T(8,128)S(1)}, f32[48,256]{1,0:T(8,128)S(1)}, u32[]{:S(2)}, u32[]{:S(2)}) collective-permute-start(f32[48,256]{1,0:T(8,128)S(1)} %get-tuple-element.101), channel_id=1, source_target_pairs={{0,8},{8,0},{16,24},{24,16},{1,9},{9,1},{17,25},{25,17},{2,10},{10... | collective-permute-start | bytes 147464 | tf_op jit(solution)/shard_map/ppermute | solution.py:709
  125.0 5.3 %collective-permute-start.22 = (f32[48,256]{1,0:T(8,128)S(1)}, f32[48,256]{1,0:T(8,128)S(1)}, u32[]{:S(2)}, u32[]{:S(2)}) collective-permute-start(f32[48,256]{1,0:T(8,128)S(1)} %get-tuple-element.102), channel_id=1, source_target_pairs={{0,16},{8,24},{16,0},{24,8},{1,17},{9,25},{17,1},{25,9},{2,18},{10... | collective-permute-start | bytes 147464 | tf_op jit(solution)/shard_map/ppermute | solution.py:709
  125.7 5.0 %collective-permute-start.23 = (f32[48,256]{1,0:T(8,128)S(1)}, f32[48,256]{1,0:T(8,128)S(1)}, u32[]{:S(2)}, u32[]{:S(2)}) collective-permute-start(f32[48,256]{1,0:T(8,128)S(1)} %get-tuple-element.103), channel_id=1, source_target_pairs={{0,24},{8,16},{16,8},{24,0},{1,25},{9,17},{17,9},{25,1},{2,26},{10... | collective-permute-start | bytes 147464 | tf_op jit(solution)/shard_map/ppermute | solution.py:709
  130.7 7.7 %collective-permute-start.26 = (f32[48,256]{1,0:T(8,128)S(1)}, f32[48,256]{1,0:T(8,128)S(1)}, u32[]{:S(2)}, u32[]{:S(2)}) collective-permute-start(f32[48,256]{1,0:T(8,128)S(1)} %add_add_fusion.1), channel_id=1, source_target_pairs={{0,3},{1,2},{2,1},{3,0},{4,7},{5,6},{6,5},{7,4},{8,11},{9,10},{10,... | collective-permute-start | bytes 147464 | tf_op jit(solution)/shard_map/ppermute | solution.py:709
  132.0 6.4 %collective-permute-start.25 = (f32[48,256]{1,0:T(8,128)S(1)}, f32[48,256]{1,0:T(8,128)S(1)}, u32[]{:S(2)}, u32[]{:S(2)}) collective-permute-start(f32[48,256]{1,0:T(8,128)S(1)} %add_add_fusion.1), channel_id=1, source_target_pairs={{0,2},{1,3},{2,0},{3,1},{4,6},{5,7},{6,4},{7,5},{8,10},{9,11},{10,... | collective-permute-start | bytes 147464 | tf_op jit(solution)/shard_map/ppermute | solution.py:709
  133.2 5.1 %collective-permute-start.24 = (f32[48,256]{1,0:T(8,128)S(1)}, f32[48,256]{1,0:T(8,128)S(1)}, u32[]{:S(2)}, u32[]{:S(2)}) collective-permute-start(f32[48,256]{1,0:T(8,128)S(1)} %add_add_fusion.1), channel_id=1, source_target_pairs={{0,1},{1,0},{2,3},{3,2},{4,5},{5,4},{6,7},{7,6},{8,9},{9,8},{10,11... | collective-permute-start | bytes 147464 | tf_op jit(solution)/shard_map/ppermute | solution.py:709
  138.4 7.1 %collective-permute-start.29 = (f32[48,256]{1,0:T(8,128)S(1)}, f32[48,256]{1,0:T(8,128)S(1)}, u32[]{:S(2)}, u32[]{:S(2)}) collective-permute-start(f32[48,256]{1,0:T(8,128)S(1)} %add_add_fusion.refs_0_), channel_id=1, source_target_pairs={{0,24},{8,16},{16,8},{24,0},{1,25},{9,17},{17,9},{25,1},{2,26},{10... | collective-permute-start | bytes 147464 | tf_op jit(solution)/shard_map/ppermute | solution.py:709
  139.9 5.6 %collective-permute-start.28 = (f32[48,256]{1,0:T(8,128)S(1)}, f32[48,256]{1,0:T(8,128)S(1)}, u32[]{:S(2)}, u32[]{:S(2)}) collective-permute-start(f32[48,256]{1,0:T(8,128)S(1)} %add_add_fusion.refs_0_), channel_id=1, source_target_pairs={{0,16},{8,24},{16,0},{24,8},{1,17},{9,25},{17,1},{25,9},{2,18},{10... | collective-permute-start | bytes 147464 | tf_op jit(solution)/shard_map/ppermute | solution.py:709
  141.5 4.1 %collective-permute-start.27 = (f32[48,256]{1,0:T(8,128)S(1)}, f32[48,256]{1,0:T(8,128)S(1)}, u32[]{:S(2)}, u32[]{:S(2)}) collective-permute-start(f32[48,256]{1,0:T(8,128)S(1)} %add_add_fusion.refs_0_), channel_id=1, source_target_pairs={{0,8},{8,0},{16,24},{24,16},{1,9},{9,1},{17,25},{25,17},{2,10},{10... | collective-permute-start | bytes 147464 | tf_op jit(solution)/shard_map/ppermute | solution.py:709
  145.6 1.5 %collective-permute-start.30 = (f32[48,1024]{1,0:T(8,128)S(1)}, f32[48,1024]{1,0:T(8,128)S(1)}, u32[]{:S(2)}, u32[]{:S(2)}) collective-permute-start(f32[48,1024]{1,0:T(8,128)S(1)} %join.1.own_ref), channel_id=1, source_target_pairs={{0,4},{4,0},{1,5},{5,1},{2,6},{6,2},{3,7},{7,3},{8,12},{12,8},{9,1... | collective-permute-start | bytes 589832 | tf_op jit(solution)/shard_map/ppermute | solution.py:709

commit v3 on v2

--- a/solution.py
+++ b/solution.py
@@ -10,6 +10,7 @@
 LAT_DEV = 64
 LANES = 128
 ROW_GROUP = 2
+PRODUCT_ROWS = 4
 FLAT_LANES = 1024
 SLACK = 3 * 1024 * 1024
 F32 = jnp.float32
@@ -179,7 +180,7 @@
     taps_row, lane = place
     built, done = r0 - 1, 0
     order = (2, 1, 0) if backwards else (0, 1, 2)
-    for row, count in groups_of(r1 - r0):
+    for row, count in groups_of(r1 - r0, PRODUCT_ROWS):
         ready = min(r0 + row + count + 1 + ROW_GROUP, r1 + 1)
         if fetch is not None:
             fetch(ready)

time: 149 us -> 148 us (level)
  no operation moved by 1% of the time
where the time goes in v3:
time: 148 us
  waiting for transfers between devices  51.4 us (35%)
  Pallas kernels  51.1 us (35%)
  starting transfers between devices  43 us (29%)
    ppermute x23, waiting for transfers between devices, swap(): lax.ppermute(value, axis, [(i, i ^ bits) for i in range(lax.axis_size(axi...  48 us
    ppermute x23, starting transfers between devices, swap(): lax.ppermute(value, axis, [(i, i ^ bits) for i in range(lax.axis_size(axi...  30 us
    pallas_call x2, Pallas kernels, weight_part(): pl.pallas_call(functools.partial(weight_kernel, grid, ranges, len(chained...  13.8 us
    pallas_call x4, Pallas kernels, input_part(): pl.pallas_call(functools.partial(input_kernel, grid, r0, r1, chunks, len(...  12.9 us
    pallas_call x2, Pallas kernels, forward(): pl.pallas_call(functools.partial(forward_kernel, grid, ranges, has_top, h...  12.5 us
    pallas_call x2, Pallas kernels, score(): pl.pallas_call(functools.partial(score_kernel, members), in_specs=[in_vme...  6.01 us
    ppermute x2, starting transfers between devices, lon_halo(): outer = lax.ppermute(jnp.where(odd, last, first), 'lon', far)  5.09 us
    pallas_call x1, Pallas kernels, edges_of(): pl.pallas_call(functools.partial(edges_kernel, grid, places, tiles), in_s...  3.05 us
  transfers between devices with their start and end apart: 31, of which 15 were waited for; matrix products, arithmetic and copies ran while one was open for 1% of the time, Pallas kernels for 26%

profile of v3, /device:TPU:0, one launch (start us, length us, event | category | flops | bytes accessed | tf_op | source)
XLA Modules:
  0.0 148.2 jit_solution(8120316431058420013)
XLA Ops:
  0.7 3.0 %edges.1 = (bf16[96,128]{1,0:T(8,128)(2,1)S(1)}, bf16[96,384]{1,0:T(8,128)(2,1)S(1)}) custom-call(bf16[96,23040]{1,0:T(8,128)(2,1)} %bitcast.6), custom_call_target="tpu_custom_call" | custom-call | flops 96 | bytes 96 | tf_op jit(solution)/shard_map/edges/pallas_call | solution.py:242
  3.8 3.0 %collective-permute-start = (bf16[96,64]{1,0:T(8,128)(2,1)S(1)}, bf16[96,64]{1,0:T(8,128)(2,1)S(1)}, u32[]{:S(2)}, u32[]{:S(2)}) collective-permute-start(bf16[96,64]{1,0:T(8,128)(2,1)S(1)} %get-tuple-element.121), channel_id=1, source_target_pairs={{0,1},{1,2},{2,3},{3,0},{4,5},{5,6},{6,7},{7,4},{8,9},{9,10},{10,1... | collective-permute-start | bytes 36872 | tf_op jit(solution)/shard_map/ppermute | solution.py:264
  6.8 2.1 %collective-permute-start.1 = (bf16[96,64]{1,0:T(8,128)(2,1)S(1)}, bf16[96,64]{1,0:T(8,128)(2,1)S(1)}, u32[]{:S(2)}, u32[]{:S(2)}) collective-permute-start(bf16[96,64]{1,0:T(8,128)(2,1)S(1)} %get-tuple-element.122), channel_id=1, source_target_pairs={{1,0},{2,1},{3,2},{0,3},{5,4},{6,5},{7,6},{4,7},{9,8},{10,9},{11,1... | collective-permute-start | bytes 36872 | tf_op jit(solution)/shard_map/ppermute | solution.py:264
  10.0 0.8 collective-permute-done
  11.3 1.2 collective-permute-done.2
  12.5 7.2 %forward_0.1 = (bf16[84,3072]{1,0:T(8,128)(2,1)S(1)}, bf16[84,3072]{1,0:T(8,128)(2,1)S(1)}, bf16[84,3072]{1,0:T(8,128)(2,1)S(1)}, bf16[84,3072]{1,0:T(8,128)(2,1...) custom-call(bf16[96,23040]{1,0:T(8,128)(2,1)} %bitcast.7, ...), custom_call_target="tpu_custom_call" | custom-call | flops 8026324992 | tf_op jit(solution)/shard_map/forward_0/pallas_call | solution.py:392
  19.7 1.5 %collective-permute-start.9 = (bf16[84,3072]{1,0:T(8,128)(2,1)S(1)}, bf16[84,3072]{1,0:T(8,128)(2,1)S(1)}, u32[]{:S(2)}, u32[]{:S(2)}) collective-permute-start(bf16[84,3072]{1,0:T(8,128)(2,1)S(1)} %get-tuple-element.80), channel_id=1, source_target_pairs={{0,8},{8,0},{16,24},{24,16},{1,9},{9,1},{17,25},{25,17},{2,10},{10... | collective-permute-start | bytes 1548296 | tf_op jit(solution)/shard_map/ppermute | solution.py:710
  21.2 1.5 %collective-permute-start.10 = (bf16[84,3072]{1,0:T(8,128)(2,1)S(1)}, bf16[84,3072]{1,0:T(8,128)(2,1)S(1)}, u32[]{:S(2)}, u32[]{:S(2)}) collective-permute-start(bf16[84,3072]{1,0:T(8,128)(2,1)S(1)} %get-tuple-element.81), channel_id=1, source_target_pairs={{0,16},{8,24},{16,0},{24,8},{1,17},{9,25},{17,1},{25,9},{2,18},{10... | collective-permute-start | bytes 1548296 | tf_op jit(solution)/shard_map/ppermute | solution.py:710
  23.2 5.3 %forward_6144.1 = (bf16[84,2688]{1,0:T(8,128)(2,1)S(1)}, bf16[84,2688]{1,0:T(8,128)(2,1)S(1)}, bf16[84,2688]{1,0:T(8,128)(2,1)S(1)}, bf16[84,2688]{1,0:T(8,128)(...) custom-call(bf16[96,23040]{1,0:T(8,128)(2,1)S(1)} %get-tuple-element.67.refs_0_, ...), custom_call_target="tpu_custom_call" | custom-call | flops 7023034368 | tf_op jit(solution)/shard_map/forward_6144/pallas_call | solution.py:392
  28.6 1.5 %collective-permute-start.3 = (bf16[84,2688]{1,0:T(8,128)(2,1)S(1)}, bf16[84,2688]{1,0:T(8,128)(2,1)S(1)}, u32[]{:S(2)}, u32[]{:S(2)}) collective-permute-start(bf16[84,2688]{1,0:T(8,128)(2,1)S(1)} %get-tuple-element.71), channel_id=1, source_target_pairs={{0,8},{8,0},{16,24},{24,16},{1,9},{9,1},{17,25},{25,17},{2,10},{10... | collective-permute-start | bytes 1354760 | tf_op jit(solution)/shard_map/ppermute | solution.py:710
  30.1 1.6 %collective-permute-start.4 = (bf16[84,2688]{1,0:T(8,128)(2,1)S(1)}, bf16[84,2688]{1,0:T(8,128)(2,1)S(1)}, u32[]{:S(2)}, u32[]{:S(2)}) collective-permute-start(bf16[84,2688]{1,0:T(8,128)(2,1)S(1)} %get-tuple-element.72), channel_id=1, source_target_pairs={{0,16},{8,24},{16,0},{24,8},{1,17},{9,25},{17,1},{25,9},{2,18},{10... | collective-permute-start | bytes 1354760 | tf_op jit(solution)/shard_map/ppermute | solution.py:710
  31.7 3.2 %collective-permute-done.9.refs_1_ = bf16[84,3072]{1,0:T(8,128)(2,1)S(1)} collective-permute-done((bf16[84,3072]{1,0:T(8,128)(2,1)S(1)}, bf16[84,3072]{1,0:T(8,128)(2,1)S(1)}, u32[]{:S(2)}, u32[]{:S(2)}) %collective-permute-start.9) | collective-permute-done | bytes 516128 | tf_op jit(solution)/shard_map/ppermute | solution.py:710
  34.8 2.5 %collective-permute-start.5 = (bf16[84,2688]{1,0:T(8,128)(2,1)S(1)}, bf16[84,2688]{1,0:T(8,128)(2,1)S(1)}, u32[]{:S(2)}, u32[]{:S(2)}) collective-permute-start(bf16[84,2688]{1,0:T(8,128)(2,1)S(1)} %get-tuple-element.73), channel_id=1, source_target_pairs={{0,24},{8,16},{16,8},{24,0},{1,25},{9,17},{17,9},{25,1},{2,26},{10... | collective-permute-start | bytes 1354760 | tf_op jit(solution)/shard_map/ppermute | solution.py:710
  37.3 10.6 %collective-permute-done.10.refs_2_ = bf16[84,3072]{1,0:T(8,128)(2,1)S(1)} collective-permute-done((bf16[84,3072]{1,0:T(8,128)(2,1)S(1)}, bf16[84,3072]{1,0:T(8,128)(2,1)S(1)}, u32[]{:S(2)}, u32[]{:S(2)}) %collective-permute-start.10) | collective-permute-done | bytes 516128 | tf_op jit(solution)/shard_map/ppermute | solution.py:710
  48.0 3.1 %score_0.1 = (bf16[84,3072]{1,0:T(8,128)(2,1)S(1)}, bf16[84,3072]{1,0:T(8,128)(2,1)S(1)}, bf16[84,3072]{1,0:T(8,128)(2,1)S(1)}, bf16[84,3072]{1,0:T(8,128)(2,1)S(1)}) custom-call(bf16[84,3072]{1,0:T(8,128)(2,1)S(1)} %get-tuple-element.78.target_ref, f32[84,128]{1,0:T(8,128)S(1)} %broadcast_in_dim.4.scale_ref, ...), custom_call_target="tpu_custom_call" | custom-call | flops 3354624000 | tf_op jit(solution)/shard_map/score_0/pallas_call | solution.py:454
  51.1 1.1 collective-permute-start.12
  52.2 1.1 collective-permute-start.13
  53.2 3.4 %collective-permute-done.3.refs_1_ = bf16[84,2688]{1,0:T(8,128)(2,1)S(1)} collective-permute-done((bf16[84,2688]{1,0:T(8,128)(2,1)S(1)}, bf16[84,2688]{1,0:T(8,128)(2,1)S(1)}, u32[]{:S(2)}, u32[]{:S(2)}) %collective-permute-start.3) | collective-permute-done | bytes 451616 | tf_op jit(solution)/shard_map/ppermute | solution.py:710
  56.6 2.5 %collective-permute-start.14 = (bf16[84,3072]{1,0:T(8,128)(2,1)S(1)}, bf16[84,3072]{1,0:T(8,128)(2,1)S(1)}, u32[]{:S(2)}, u32[]{:S(2)}) collective-permute-start(bf16[84,3072]{1,0:T(8,128)(2,1)S(1)} %get-tuple-element.86), channel_id=1, source_target_pairs={{0,24},{8,16},{16,8},{24,0},{1,25},{9,17},{17,9},{25,1},{2,26},{10... | collective-permute-start | bytes 1548296 | tf_op jit(solution)/shard_map/ppermute | solution.py:710
  59.1 9.1 %collective-permute-done.4.refs_2_ = bf16[84,2688]{1,0:T(8,128)(2,1)S(1)} collective-permute-done((bf16[84,2688]{1,0:T(8,128)(2,1)S(1)}, bf16[84,2688]{1,0:T(8,128)(2,1)S(1)}, u32[]{:S(2)}, u32[]{:S(2)}) %collective-permute-start.4) | collective-permute-done | bytes 451616 | tf_op jit(solution)/shard_map/ppermute | solution.py:710
  68.2 2.9 %score_6144.1 = (bf16[84,2688]{1,0:T(8,128)(2,1)S(1)}, bf16[84,2688]{1,0:T(8,128)(2,1)S(1)}, bf16[84,2688]{1,0:T(8,128)(2,1)S(1)}, bf16[84,2688]{1,0:T(8,128)(2,1)S(1)}) custom-call(bf16[84,2688]{1,0:T(8,128)(2,1)S(1)} %get-tuple-element.68.target_ref.refs_4_, f32[84,128]{1,0:T(8,128)S(1)} %broadcast_in_dim.4.scale_ref, ...), custom_call_target="tpu_custom_call" | custom-call | flops 2935296000 | tf_op jit(solution)/shard_map/score_6144/pallas_call | solution.py:454
  71.1 1.1 collective-permute-start.6
  72.2 1.0 collective-permute-start.7
  73.3 5.1 %collective-permute-done.12.refs_1_ = bf16[84,3072]{1,0:T(8,128)(2,1)S(1)} collective-permute-done((bf16[84,3072]{1,0:T(8,128)(2,1)S(1)}, bf16[84,3072]{1,0:T(8,128)(2,1)S(1)}, u32[]{:S(2)}, u32[]{:S(2)}) %collective-permute-start.12) | collective-permute-done | bytes 516128 | tf_op jit(solution)/shard_map/ppermute | solution.py:710
  78.4 2.5 %collective-permute-start.8 = (bf16[84,2688]{1,0:T(8,128)(2,1)S(1)}, bf16[84,2688]{1,0:T(8,128)(2,1)S(1)}, u32[]{:S(2)}, u32[]{:S(2)}) collective-permute-start(bf16[84,2688]{1,0:T(8,128)(2,1)S(1)} %get-tuple-element.77), channel_id=1, source_target_pairs={{0,24},{8,16},{16,8},{24,0},{1,25},{9,17},{17,9},{25,1},{2,26},{10... | collective-permute-start | bytes 1354760 | tf_op jit(solution)/shard_map/ppermute | solution.py:710
  80.9 10.5 %collective-permute-done.13.refs_2_ = bf16[84,3072]{1,0:T(8,128)(2,1)S(1)} collective-permute-done((bf16[84,3072]{1,0:T(8,128)(2,1)S(1)}, bf16[84,3072]{1,0:T(8,128)(2,1)S(1)}, u32[]{:S(2)}, u32[]{:S(2)}) %collective-permute-start.13) | collective-permute-done | bytes 516128 | tf_op jit(solution)/shard_map/ppermute | solution.py:710
  92.2 1.3 collective-permute-start.15
  93.5 2.5 %collective-permute-start.16 = (bf16[96,64]{1,0:T(8,128)(2,1)S(1)}, bf16[96,64]{1,0:T(8,128)(2,1)S(1)}, u32[]{:S(2)}, u32[]{:S(2)}) collective-permute-start(bf16[96,64]{1,0:T(8,128)(2,1)S(1)} %get-tuple-element.120), channel_id=1, source_target_pairs={{0,3},{1,2},{2,1},{3,0},{4,7},{5,6},{6,5},{7,4},{8,11},{9,10},{10,... | collective-permute-start | bytes 36872 | tf_op jit(solution)/shard_map/ppermute | solution.py:269
  96.1 7.3 %weight_0.1.refs_0_ = f32[96,1024]{1,0:T(8,128)S(1)} custom-call(bf16[288,15360]{1,0:T(8,128)(2,1)S(1)} %get-tuple-element.89.taps, bf16[96,12288]{1,0:T(8,128)(2,1)S(1)} %get-tuple-element.87.part_ref.refs_0_), custom_call_target="tpu_custom_call" | custom-call | flops 12288 | tf_op jit(solution)/shard_map/weight_0/pallas_call | solution.py:568
  103.6 1.3 collective-permute-done.17
  104.9 3.2 %input_48.1.refs_4_ = bf16[96,23040]{1,0:T(8,128)(2,1)} custom-call(bf16[96,12288]{1,0:T(8,128)(2,1)S(1)} %get-tuple-element.87.part_ref.refs_0_, bf16[96,128]{1,0:T(8,128)(2,1)S(1)} %maximum_select_fusion.refs_1_, bf16[96,864]{1,0:T(8,128)(2,1)S(1)} %get-tuple-element.91.refs_2_.refs_3_, bf16[96,512]{1,0:T(8,128)(2,1)S(1)} %get-tuple-element.114.refs_3_), custom_call_target="tpu_custom_call" | custom-call | flops 53084160 | bytes 5760 | tf_op jit(solution)/shard_map/input_48/pallas_call | solution.py:640
  108.2 2.4 %collective-permute-done.7.refs_2_ = bf16[84,2688]{1,0:T(8,128)(2,1)S(1)} collective-permute-done((bf16[84,2688]{1,0:T(8,128)(2,1)S(1)}, bf16[84,2688]{1,0:T(8,128)(2,1)S(1)}, u32[]{:S(2)}, u32[]{:S(2)}) %collective-permute-start.7) | collective-permute-done | bytes 451616 | tf_op jit(solution)/shard_map/ppermute | solution.py:710
  111.3 1.3 collective-permute-start.18
  112.6 2.5 %collective-permute-start.19 = (bf16[96,64]{1,0:T(8,128)(2,1)S(1)}, bf16[96,64]{1,0:T(8,128)(2,1)S(1)}, u32[]{:S(2)}, u32[]{:S(2)}) collective-permute-start(bf16[96,64]{1,0:T(8,128)(2,1)S(1)} %get-tuple-element.118), channel_id=1, source_target_pairs={{0,3},{1,2},{2,1},{3,0},{4,7},{5,6},{6,5},{7,4},{8,11},{9,10},{10,... | collective-permute-start | bytes 36872 | tf_op jit(solution)/shard_map/ppermute | solution.py:269
  115.2 6.5 %weight_6144.1 = (f32[48,1024]{1,0:T(8,128)S(1)}, f32[48,1024]{1,0:T(8,128)S(1)}) custom-call(bf16[288,12288]{1,0:T(8,128)(2,1)S(1)} %get-tuple-element.93.taps, bf16[96,10752]{1,0:T(8,128)(2,1)S(1)} %get-tuple-element.94.part_ref.refs_1_, f32[96,1024]{1,0:T(8,128)S(1)} %weight_0.1.refs_0_), custom_call_target="tpu_custom_call" | custom-call | flops 10752 | tf_op jit(solution)/shard_map/weight_6144/pallas_call | solution.py:568
  121.8 1.4 collective-permute-done.20.refs_1_
  123.3 1.5 collective-permute-start.21
  125.4 1.4 collective-permute-start.23
  126.8 3.2 %input_0.1.refs_4_ = bf16[96,23040]{1,0:T(8,128)(2,1)} custom-call(bf16[96,12288]{1,0:T(8,128)(2,1)S(1)} %get-tuple-element.87.part_ref.refs_0_, bf16[96,128]{1,0:T(8,128)(2,1)S(1)} %add.24.refs_1_.refs_2_, bf16[96,864]{1,0:T(8,128)(2,1)S(1)} %get-tuple-element.91.refs_2_.refs_3_, ...), custom_call_target="tpu_custom_call", output_to_operand_aliasing={{}: (4, {})} | custom-call | flops 4246732800 | bytes 5760 | tf_op jit(solution)/shard_map/input_0/pallas_call | solution.py:640
  130.4 1.3 collective-permute-start.26
  131.8 1.2 collective-permute-start.25
  133.0 1.9 %collective-permute-start.24 = (f32[48,256]{1,0:T(8,128)S(1)}, f32[48,256]{1,0:T(8,128)S(1)}, u32[]{:S(2)}, u32[]{:S(2)}) collective-permute-start(f32[48,256]{1,0:T(8,128)S(1)} %add_add_fusion.1), channel_id=1, source_target_pairs={{0,1},{1,0},{2,3},{3,2},{4,5},{5,4},{6,7},{7,6},{8,9},{9,8},{10,11... | collective-permute-start | bytes 147464 | tf_op jit(solution)/shard_map/ppermute | solution.py:710
  134.9 3.2 %input_32.1.refs_4_ = bf16[96,23040]{1,0:T(8,128)(2,1)} custom-call(bf16[96,12288]{1,0:T(8,128)(2,1)S(1)} %get-tuple-element.87.part_ref.refs_0_, bf16[96,10752]{1,0:T(8,128)(2,1)S(1)} %get-tuple-element.94.part_ref.refs_1_, bf16[96,128]{1,0:T(8,128)(2,1)S(1)} %add.24.refs_1_.refs_2_, ...), custom_call_target="tpu_custom_call", output_to_operand_aliasing={{}: (4, {})} | custom-call | flops 4246732800 | bytes 5760 | tf_op jit(solution)/shard_map/input_32/pallas_call | solution.py:640
  138.1 1.5 %collective-permute-start.29 = (f32[48,256]{1,0:T(8,128)S(1)}, f32[48,256]{1,0:T(8,128)S(1)}, u32[]{:S(2)}, u32[]{:S(2)}) collective-permute-start(f32[48,256]{1,0:T(8,128)S(1)} %add_add_fusion.refs_0_), channel_id=1, source_target_pairs={{0,24},{8,16},{16,8},{24,0},{1,25},{9,17},{17,9},{25,1},{2,26},{10... | collective-permute-start | bytes 147464 | tf_op jit(solution)/shard_map/ppermute | solution.py:710
  139.7 1.5 %collective-permute-start.28 = (f32[48,256]{1,0:T(8,128)S(1)}, f32[48,256]{1,0:T(8,128)S(1)}, u32[]{:S(2)}, u32[]{:S(2)}) collective-permute-start(f32[48,256]{1,0:T(8,128)S(1)} %add_add_fusion.refs_0_), channel_id=1, source_target_pairs={{0,16},{8,24},{16,0},{24,8},{1,17},{9,25},{17,1},{25,9},{2,18},{10... | collective-permute-start | bytes 147464 | tf_op jit(solution)/shard_map/ppermute | solution.py:710
  141.7 3.3 %input_16.1 = bf16[96,23040]{1,0:T(8,128)(2,1)} custom-call(bf16[96,12288]{1,0:T(8,128)(2,1)S(1)} %get-tuple-element.87.part_ref.refs_0_, bf16[96,10752]{1,0:T(8,128)(2,1)S(1)} %get-tuple-element.94.part_ref.refs_1_, bf16[96,128]{1,0:T(8,128)(2,1)S(1)} %add.24.refs_1_.refs_2_, ...), custom_call_target="tpu_custom_call", output_to_operand_aliasing={{}: (4, {})} | custom-call | flops 4246732800 | bytes 5760 | tf_op jit(solution)/shard_map/input_16/pallas_call | solution.py:640
  145.4 1.4 collective-permute-done.30.other_ref
  146.8 1.3 finish.1
  (54 shorter events, 5.9 us)
Async XLA Ops:
  0.6 8.3 %copy-start = (bf16[9,8064]{1,0:T(8,128)(2,1)S(1)}, bf16[9,8064]{1,0:T(8,128)(2,1)}, u32[]{:S(2)}) copy-start(bf16[9,8064]{1,0:T(8,128)(2,1)} %param.6) | copy-start | bytes 435460
  0.6 10.5 %copy-start.2 = (f32[84]{0:T(128)S(1)}, f32[84]{0:T(128)}, u32[]{:S(2)}) copy-start(f32[84]{0:T(128)} %param.7) | copy-start | bytes 1012
  0.7 10.3 %copy-start.1 = (f32[84]{0:T(128)S(1)}, f32[84]{0:T(128)}, u32[]{:S(2)}) copy-start(f32[84]{0:T(128)} %param.9) | copy-start | bytes 1012
  3.8 7.0 %collective-permute-start = (bf16[96,64]{1,0:T(8,128)(2,1)S(1)}, bf16[96,64]{1,0:T(8,128)(2,1)S(1)}, u32[]{:S(2)}, u32[]{:S(2)}) collective-permute-start(bf16[96,64]{1,0:T(8,128)(2,1)S(1)} %get-tuple-element.121), channel_id=1, source_target_pairs={{0,1},{1,2},{2,3},{3,0},{4,5},{5,6},{6,7},{7,4},{8,9},{9,10},{10,1... | collective-permute-start | bytes 36872 | tf_op jit(solution)/shard_map/ppermute | solution.py:264
  6.8 4.1 %collective-permute-start.1 = (bf16[96,64]{1,0:T(8,128)(2,1)S(1)}, bf16[96,64]{1,0:T(8,128)(2,1)S(1)}, u32[]{:S(2)}, u32[]{:S(2)}) collective-permute-start(bf16[96,64]{1,0:T(8,128)(2,1)S(1)} %get-tuple-element.122), channel_id=1, source_target_pairs={{1,0},{2,1},{3,2},{0,3},{5,4},{6,5},{7,6},{4,7},{9,8},{10,9},{11,1... | collective-permute-start | bytes 36872 | tf_op jit(solution)/shard_map/ppermute | solution.py:264
  11.1 1.4 collective-permute-start.2
  19.7 15.2 %collective-permute-start.9 = (bf16[84,3072]{1,0:T(8,128)(2,1)S(1)}, bf16[84,3072]{1,0:T(8,128)(2,1)S(1)}, u32[]{:S(2)}, u32[]{:S(2)}) collective-permute-start(bf16[84,3072]{1,0:T(8,128)(2,1)S(1)} %get-tuple-element.80), channel_id=1, source_target_pairs={{0,8},{8,0},{16,24},{24,16},{1,9},{9,1},{17,25},{25,17},{2,10},{10... | collective-permute-start | bytes 1548296 | tf_op jit(solution)/shard_map/ppermute | solution.py:710
  21.2 26.7 %collective-permute-start.10 = (bf16[84,3072]{1,0:T(8,128)(2,1)S(1)}, bf16[84,3072]{1,0:T(8,128)(2,1)S(1)}, u32[]{:S(2)}, u32[]{:S(2)}) collective-permute-start(bf16[84,3072]{1,0:T(8,128)(2,1)S(1)} %get-tuple-element.81), channel_id=1, source_target_pairs={{0,16},{8,24},{16,0},{24,8},{1,17},{9,25},{17,1},{25,9},{2,18},{10... | collective-permute-start | bytes 1548296 | tf_op jit(solution)/shard_map/ppermute | solution.py:710
  22.8 25.2 %collective-permute-start.11 = (bf16[84,3072]{1,0:T(8,128)(2,1)S(1)}, bf16[84,3072]{1,0:T(8,128)(2,1)S(1)}, u32[]{:S(2)}, u32[]{:S(2)}) collective-permute-start(bf16[84,3072]{1,0:T(8,128)(2,1)S(1)} %get-tuple-element.82), channel_id=1, source_target_pairs={{0,24},{8,16},{16,8},{24,0},{1,25},{9,17},{17,9},{25,1},{2,26},{10... | collective-permute-start | bytes 1548296 | tf_op jit(solution)/shard_map/ppermute | solution.py:710
  28.6 28.1 %collective-permute-start.3 = (bf16[84,2688]{1,0:T(8,128)(2,1)S(1)}, bf16[84,2688]{1,0:T(8,128)(2,1)S(1)}, u32[]{:S(2)}, u32[]{:S(2)}) collective-permute-start(bf16[84,2688]{1,0:T(8,128)(2,1)S(1)} %get-tuple-element.71), channel_id=1, source_target_pairs={{0,8},{8,0},{16,24},{24,16},{1,9},{9,1},{17,25},{25,17},{2,10},{10... | collective-permute-start | bytes 1354760 | tf_op jit(solution)/shard_map/ppermute | solution.py:710
  30.1 38.1 %collective-permute-start.4 = (bf16[84,2688]{1,0:T(8,128)(2,1)S(1)}, bf16[84,2688]{1,0:T(8,128)(2,1)S(1)}, u32[]{:S(2)}, u32[]{:S(2)}) collective-permute-start(bf16[84,2688]{1,0:T(8,128)(2,1)S(1)} %get-tuple-element.72), channel_id=1, source_target_pairs={{0,16},{8,24},{16,0},{24,8},{1,17},{9,25},{17,1},{25,9},{2,18},{10... | collective-permute-start | bytes 1354760 | tf_op jit(solution)/shard_map/ppermute | solution.py:710
  34.8 33.4 %collective-permute-start.5 = (bf16[84,2688]{1,0:T(8,128)(2,1)S(1)}, bf16[84,2688]{1,0:T(8,128)(2,1)S(1)}, u32[]{:S(2)}, u32[]{:S(2)}) collective-permute-start(bf16[84,2688]{1,0:T(8,128)(2,1)S(1)} %get-tuple-element.73), channel_id=1, source_target_pairs={{0,24},{8,16},{16,8},{24,0},{1,25},{9,17},{17,9},{25,1},{2,26},{10... | collective-permute-start | bytes 1354760 | tf_op jit(solution)/shard_map/ppermute | solution.py:710
  51.1 27.3 %collective-permute-start.12 = (bf16[84,3072]{1,0:T(8,128)(2,1)S(1)}, bf16[84,3072]{1,0:T(8,128)(2,1)S(1)}, u32[]{:S(2)}, u32[]{:S(2)}) collective-permute-start(bf16[84,3072]{1,0:T(8,128)(2,1)S(1)} %get-tuple-element.84), channel_id=1, source_target_pairs={{0,8},{8,0},{16,24},{24,16},{1,9},{9,1},{17,25},{25,17},{2,10},{10... | collective-permute-start | bytes 1548296 | tf_op jit(solution)/shard_map/ppermute | solution.py:710
  52.2 39.2 %collective-permute-start.13 = (bf16[84,3072]{1,0:T(8,128)(2,1)S(1)}, bf16[84,3072]{1,0:T(8,128)(2,1)S(1)}, u32[]{:S(2)}, u32[]{:S(2)}) collective-permute-start(bf16[84,3072]{1,0:T(8,128)(2,1)S(1)} %get-tuple-element.85), channel_id=1, source_target_pairs={{0,16},{8,24},{16,0},{24,8},{1,17},{9,25},{17,1},{25,9},{2,18},{10... | collective-permute-start | bytes 1548296 | tf_op jit(solution)/shard_map/ppermute | solution.py:710
  56.6 34.8 %collective-permute-start.14 = (bf16[84,3072]{1,0:T(8,128)(2,1)S(1)}, bf16[84,3072]{1,0:T(8,128)(2,1)S(1)}, u32[]{:S(2)}, u32[]{:S(2)}) collective-permute-start(bf16[84,3072]{1,0:T(8,128)(2,1)S(1)} %get-tuple-element.86), channel_id=1, source_target_pairs={{0,24},{8,16},{16,8},{24,0},{1,25},{9,17},{17,9},{25,1},{2,26},{10... | collective-permute-start | bytes 1548296 | tf_op jit(solution)/shard_map/ppermute | solution.py:710
  71.1 37.0 %collective-permute-start.6 = (bf16[84,2688]{1,0:T(8,128)(2,1)S(1)}, bf16[84,2688]{1,0:T(8,128)(2,1)S(1)}, u32[]{:S(2)}, u32[]{:S(2)}) collective-permute-start(bf16[84,2688]{1,0:T(8,128)(2,1)S(1)} %get-tuple-element.75), channel_id=1, source_target_pairs={{0,8},{8,0},{16,24},{24,16},{1,9},{9,1},{17,25},{25,17},{2,10},{10... | collective-permute-start | bytes 1354760 | tf_op jit(solution)/shard_map/ppermute | solution.py:710
  72.2 38.4 %collective-permute-start.7 = (bf16[84,2688]{1,0:T(8,128)(2,1)S(1)}, bf16[84,2688]{1,0:T(8,128)(2,1)S(1)}, u32[]{:S(2)}, u32[]{:S(2)}) collective-permute-start(bf16[84,2688]{1,0:T(8,128)(2,1)S(1)} %get-tuple-element.76), channel_id=1, source_target_pairs={{0,16},{8,24},{16,0},{24,8},{1,17},{9,25},{17,1},{25,9},{2,18},{10... | collective-permute-start | bytes 1354760 | tf_op jit(solution)/shard_map/ppermute | solution.py:710
  78.4 32.2 %collective-permute-start.8 = (bf16[84,2688]{1,0:T(8,128)(2,1)S(1)}, bf16[84,2688]{1,0:T(8,128)(2,1)S(1)}, u32[]{:S(2)}, u32[]{:S(2)}) collective-permute-start(bf16[84,2688]{1,0:T(8,128)(2,1)S(1)} %get-tuple-element.77), channel_id=1, source_target_pairs={{0,24},{8,16},{16,8},{24,0},{1,25},{9,17},{17,9},{25,1},{2,26},{10... | collective-permute-start | bytes 1354760 | tf_op jit(solution)/shard_map/ppermute | solution.py:710
  92.2 11.2 %collective-permute-start.15 = (bf16[96,64]{1,0:T(8,128)(2,1)S(1)}, bf16[96,64]{1,0:T(8,128)(2,1)S(1)}, u32[]{:S(2)}, u32[]{:S(2)}) collective-permute-start(bf16[96,64]{1,0:T(8,128)(2,1)S(1)} %get-tuple-element.119), channel_id=1, source_target_pairs={{0,1},{1,0},{2,3},{3,2},{4,5},{5,4},{6,7},{7,6},{8,9},{9,8},{10,11... | collective-permute-start | bytes 36872 | tf_op jit(solution)/shard_map/ppermute | solution.py:268
  93.5 9.9 %collective-permute-start.16 = (bf16[96,64]{1,0:T(8,128)(2,1)S(1)}, bf16[96,64]{1,0:T(8,128)(2,1)S(1)}, u32[]{:S(2)}, u32[]{:S(2)}) collective-permute-start(bf16[96,64]{1,0:T(8,128)(2,1)S(1)} %get-tuple-element.120), channel_id=1, source_target_pairs={{0,3},{1,2},{2,1},{3,0},{4,7},{5,6},{6,5},{7,4},{8,11},{9,10},{10,... | collective-permute-start | bytes 36872 | tf_op jit(solution)/shard_map/ppermute | solution.py:269
  103.5 1.4 collective-permute-start.17
  111.3 10.3 %collective-permute-start.18 = (bf16[96,64]{1,0:T(8,128)(2,1)S(1)}, bf16[96,64]{1,0:T(8,128)(2,1)S(1)}, u32[]{:S(2)}, u32[]{:S(2)}) collective-permute-start(bf16[96,64]{1,0:T(8,128)(2,1)S(1)} %get-tuple-element.117), channel_id=1, source_target_pairs={{0,1},{1,0},{2,3},{3,2},{4,5},{5,4},{6,7},{7,6},{8,9},{9,8},{10,11... | collective-permute-start | bytes 36872 | tf_op jit(solution)/shard_map/ppermute | solution.py:268
  112.6 9.0 %collective-permute-start.19 = (bf16[96,64]{1,0:T(8,128)(2,1)S(1)}, bf16[96,64]{1,0:T(8,128)(2,1)S(1)}, u32[]{:S(2)}, u32[]{:S(2)}) collective-permute-start(bf16[96,64]{1,0:T(8,128)(2,1)S(1)} %get-tuple-element.118), channel_id=1, source_target_pairs={{0,3},{1,2},{2,1},{3,0},{4,7},{5,6},{6,5},{7,4},{8,11},{9,10},{10,... | collective-permute-start | bytes 36872 | tf_op jit(solution)/shard_map/ppermute | solution.py:269
  121.7 1.5 %collective-permute-start.20 = (f32[48,1024]{1,0:T(8,128)S(1)}, f32[48,1024]{1,0:T(8,128)S(1)}, u32[]{:S(2)}, u32[]{:S(2)}) collective-permute-start(f32[48,1024]{1,0:T(8,128)S(1)} %get-tuple-element.99), channel_id=1, source_target_pairs={{0,4},{4,0},{1,5},{5,1},{2,6},{6,2},{3,7},{7,3},{8,12},{12,8},{9,1... | collective-permute-start | bytes 589832 | tf_op jit(solution)/shard_map/ppermute | solution.py:710
  123.3 6.8 %collective-permute-start.21 = (f32[48,256]{1,0:T(8,128)S(1)}, f32[48,256]{1,0:T(8,128)S(1)}, u32[]{:S(2)}, u32[]{:S(2)}) collective-permute-start(f32[48,256]{1,0:T(8,128)S(1)} %get-tuple-element.101), channel_id=1, source_target_pairs={{0,8},{8,0},{16,24},{24,16},{1,9},{9,1},{17,25},{25,17},{2,10},{10... | collective-permute-start | bytes 147464 | tf_op jit(solution)/shard_map/ppermute | solution.py:710
  124.7 5.3 %collective-permute-start.22 = (f32[48,256]{1,0:T(8,128)S(1)}, f32[48,256]{1,0:T(8,128)S(1)}, u32[]{:S(2)}, u32[]{:S(2)}) collective-permute-start(f32[48,256]{1,0:T(8,128)S(1)} %get-tuple-element.102), channel_id=1, source_target_pairs={{0,16},{8,24},{16,0},{24,8},{1,17},{9,25},{17,1},{25,9},{2,18},{10... | collective-permute-start | bytes 147464 | tf_op jit(solution)/shard_map/ppermute | solution.py:710
  125.4 5.0 %collective-permute-start.23 = (f32[48,256]{1,0:T(8,128)S(1)}, f32[48,256]{1,0:T(8,128)S(1)}, u32[]{:S(2)}, u32[]{:S(2)}) collective-permute-start(f32[48,256]{1,0:T(8,128)S(1)} %get-tuple-element.103), channel_id=1, source_target_pairs={{0,24},{8,16},{16,8},{24,0},{1,25},{9,17},{17,9},{25,1},{2,26},{10... | collective-permute-start | bytes 147464 | tf_op jit(solution)/shard_map/ppermute | solution.py:710
  130.4 7.7 %collective-permute-start.26 = (f32[48,256]{1,0:T(8,128)S(1)}, f32[48,256]{1,0:T(8,128)S(1)}, u32[]{:S(2)}, u32[]{:S(2)}) collective-permute-start(f32[48,256]{1,0:T(8,128)S(1)} %add_add_fusion.1), channel_id=1, source_target_pairs={{0,3},{1,2},{2,1},{3,0},{4,7},{5,6},{6,5},{7,4},{8,11},{9,10},{10,... | collective-permute-start | bytes 147464 | tf_op jit(solution)/shard_map/ppermute | solution.py:710
  131.8 6.4 %collective-permute-start.25 = (f32[48,256]{1,0:T(8,128)S(1)}, f32[48,256]{1,0:T(8,128)S(1)}, u32[]{:S(2)}, u32[]{:S(2)}) collective-permute-start(f32[48,256]{1,0:T(8,128)S(1)} %add_add_fusion.1), channel_id=1, source_target_pairs={{0,2},{1,3},{2,0},{3,1},{4,6},{5,7},{6,4},{7,5},{8,10},{9,11},{10,... | collective-permute-start | bytes 147464 | tf_op jit(solution)/shard_map/ppermute | solution.py:710
  133.0 5.1 %collective-permute-start.24 = (f32[48,256]{1,0:T(8,128)S(1)}, f32[48,256]{1,0:T(8,128)S(1)}, u32[]{:S(2)}, u32[]{:S(2)}) collective-permute-start(f32[48,256]{1,0:T(8,128)S(1)} %add_add_fusion.1), channel_id=1, source_target_pairs={{0,1},{1,0},{2,3},{3,2},{4,5},{5,4},{6,7},{7,6},{8,9},{9,8},{10,11... | collective-permute-start | bytes 147464 | tf_op jit(solution)/shard_map/ppermute | solution.py:710
  138.1 7.1 %collective-permute-start.29 = (f32[48,256]{1,0:T(8,128)S(1)}, f32[48,256]{1,0:T(8,128)S(1)}, u32[]{:S(2)}, u32[]{:S(2)}) collective-permute-start(f32[48,256]{1,0:T(8,128)S(1)} %add_add_fusion.refs_0_), channel_id=1, source_target_pairs={{0,24},{8,16},{16,8},{24,0},{1,25},{9,17},{17,9},{25,1},{2,26},{10... | collective-permute-start | bytes 147464 | tf_op jit(solution)/shard_map/ppermute | solution.py:710
  139.7 5.6 %collective-permute-start.28 = (f32[48,256]{1,0:T(8,128)S(1)}, f32[48,256]{1,0:T(8,128)S(1)}, u32[]{:S(2)}, u32[]{:S(2)}) collective-permute-start(f32[48,256]{1,0:T(8,128)S(1)} %add_add_fusion.refs_0_), channel_id=1, source_target_pairs={{0,16},{8,24},{16,0},{24,8},{1,17},{9,25},{17,1},{25,9},{2,18},{10... | collective-permute-start | bytes 147464 | tf_op jit(solution)/shard_map/ppermute | solution.py:710
  141.2 4.1 %collective-permute-start.27 = (f32[48,256]{1,0:T(8,128)S(1)}, f32[48,256]{1,0:T(8,128)S(1)}, u32[]{:S(2)}, u32[]{:S(2)}) collective-permute-start(f32[48,256]{1,0:T(8,128)S(1)} %add_add_fusion.refs_0_), channel_id=1, source_target_pairs={{0,8},{8,0},{16,24},{24,16},{1,9},{9,1},{17,25},{25,17},{2,10},{10... | collective-permute-start | bytes 147464 | tf_op jit(solution)/shard_map/ppermute | solution.py:710
  145.3 1.5 %collective-permute-start.30 = (f32[48,1024]{1,0:T(8,128)S(1)}, f32[48,1024]{1,0:T(8,128)S(1)}, u32[]{:S(2)}, u32[]{:S(2)}) collective-permute-start(f32[48,1024]{1,0:T(8,128)S(1)} %join.1.own_ref), channel_id=1, source_target_pairs={{0,4},{4,0},{1,5},{5,1},{2,6},{6,2},{3,7},{7,3},{8,12},{12,8},{9,1... | collective-permute-start | bytes 589832 | tf_op jit(solution)/shard_map/ppermute | solution.py:710

commit v4 on v3

--- a/solution.py
+++ b/solution.py
@@ -871,9 +871,13 @@
         final = number == len(chunks) - 1
         after = [returned[-1][0]] if number == 0 else [kept_in_hbm(grad_input)]
         part, edge = gather(grid, ranges, rows, returned[number], after)
+        if final:
+            sums = weight_part(grid, ranges, members, taken[number], part, sums[0], [], final)
+            edge, sums = lax.optimization_barrier((edge, list(sums)))
         sides = lon_halo(edge, odd)
-        sums = weight_part(grid, ranges, members, taken[number], part, sums[0], [], final)
-        sides, sums = lax.optimization_barrier((sides, list(sums)))
+        if not final:
+            sums = weight_part(grid, ranges, members, taken[number], part, sums[0], [], final)
+            sides, sums = lax.optimization_barrier((sides, list(sums)))
         parts.append(part)
         g_sides = sides if number == 0 else g_sides + sides
         if number == 0:

time: 148 us -> 150 us (1.014)
  waiting for transfers between devices: 51.4 us -> 53 us
    ppermute x2, waiting for transfers between devices: 0.01 us -> 3.08 us  [lon_halo(): outer = lax.ppermute(jnp.where(odd, last, first), 'lon', far)]
  transfers between devices with their start and end apart: 31 -> 31, of which waited for: 15 -> 15; matrix products, arithmetic and copies ran while one was open for 1% -> 1% of each run, Pallas kernels for 26% -> 22%
where the time goes in v4:
time: 150 us
  waiting for transfers between devices  53 us (35%)
  Pallas kernels  51.2 us (34%)
  starting transfers between devices  43 us (29%)
    ppermute x23, waiting for transfers between devices, swap(): lax.ppermute(value, axis, [(i, i ^ bits) for i in range(lax.axis_size(axi...  46.6 us
    ppermute x23, starting transfers between devices, swap(): lax.ppermute(value, axis, [(i, i ^ bits) for i in range(lax.axis_size(axi...  29.9 us
    pallas_call x2, Pallas kernels, weight_part(): pl.pallas_call(functools.partial(weight_kernel, grid, ranges, len(chained...  13.8 us
    pallas_call x4, Pallas kernels, input_part(): pl.pallas_call(functools.partial(input_kernel, grid, r0, r1, chunks, len(...  12.9 us
    pallas_call x2, Pallas kernels, forward(): pl.pallas_call(functools.partial(forward_kernel, grid, ranges, has_top, h...  12.5 us
    pallas_call x2, Pallas kernels, score(): pl.pallas_call(functools.partial(score_kernel, members), in_specs=[in_vme...  6.01 us
    ppermute x2, starting transfers between devices, lon_halo(): outer = lax.ppermute(jnp.where(odd, last, first), 'lon', far)  5.09 us
    ppermute x2, waiting for transfers between devices, lon_halo(): outer = lax.ppermute(jnp.where(odd, last, first), 'lon', far)  3.08 us
  transfers between devices with their start and end apart: 31, of which 15 were waited for; matrix products, arithmetic and copies ran while one was open for 1% of the time, Pallas kernels for 22%

profile of v4, /device:TPU:0, one launch (start us, length us, event | category | flops | bytes accessed | tf_op | source)
XLA Modules:
  0.0 149.7 jit_solution(5692091485753928782)
XLA Ops:
  0.7 3.0 %edges.1 = (bf16[96,128]{1,0:T(8,128)(2,1)S(1)}, bf16[96,384]{1,0:T(8,128)(2,1)S(1)}) custom-call(bf16[96,23040]{1,0:T(8,128)(2,1)} %bitcast.6), custom_call_target="tpu_custom_call" | custom-call | flops 96 | bytes 96 | tf_op jit(solution)/shard_map/edges/pallas_call | solution.py:242
  3.8 3.0 %collective-permute-start = (bf16[96,64]{1,0:T(8,128)(2,1)S(1)}, bf16[96,64]{1,0:T(8,128)(2,1)S(1)}, u32[]{:S(2)}, u32[]{:S(2)}) collective-permute-start(bf16[96,64]{1,0:T(8,128)(2,1)S(1)} %get-tuple-element.121), channel_id=1, source_target_pairs={{0,1},{1,2},{2,3},{3,0},{4,5},{5,6},{6,7},{7,4},{8,9},{9,10},{10,1... | collective-permute-start | bytes 36872 | tf_op jit(solution)/shard_map/ppermute | solution.py:264
  6.8 2.1 %collective-permute-start.1 = (bf16[96,64]{1,0:T(8,128)(2,1)S(1)}, bf16[96,64]{1,0:T(8,128)(2,1)S(1)}, u32[]{:S(2)}, u32[]{:S(2)}) collective-permute-start(bf16[96,64]{1,0:T(8,128)(2,1)S(1)} %get-tuple-element.122), channel_id=1, source_target_pairs={{1,0},{2,1},{3,2},{0,3},{5,4},{6,5},{7,6},{4,7},{9,8},{10,9},{11,1... | collective-permute-start | bytes 36872 | tf_op jit(solution)/shard_map/ppermute | solution.py:264
  8.9 0.8 reshape.20.taps_ref
  10.0 0.8 collective-permute-done
  11.3 1.2 collective-permute-done.2
  12.5 7.2 %forward_0.1 = (bf16[84,3072]{1,0:T(8,128)(2,1)S(1)}, bf16[84,3072]{1,0:T(8,128)(2,1)S(1)}, bf16[84,3072]{1,0:T(8,128)(2,1)S(1)}, bf16[84,3072]{1,0:T(8,128)(2,1...) custom-call(bf16[96,23040]{1,0:T(8,128)(2,1)} %bitcast.7, ...), custom_call_target="tpu_custom_call" | custom-call | flops 8026324992 | tf_op jit(solution)/shard_map/forward_0/pallas_call | solution.py:392
  19.7 1.5 %collective-permute-start.9 = (bf16[84,3072]{1,0:T(8,128)(2,1)S(1)}, bf16[84,3072]{1,0:T(8,128)(2,1)S(1)}, u32[]{:S(2)}, u32[]{:S(2)}) collective-permute-start(bf16[84,3072]{1,0:T(8,128)(2,1)S(1)} %get-tuple-element.79), channel_id=1, source_target_pairs={{0,8},{8,0},{16,24},{24,16},{1,9},{9,1},{17,25},{25,17},{2,10},{10... | collective-permute-start | bytes 1548296 | tf_op jit(solution)/shard_map/ppermute | solution.py:710
  21.2 1.5 %collective-permute-start.10 = (bf16[84,3072]{1,0:T(8,128)(2,1)S(1)}, bf16[84,3072]{1,0:T(8,128)(2,1)S(1)}, u32[]{:S(2)}, u32[]{:S(2)}) collective-permute-start(bf16[84,3072]{1,0:T(8,128)(2,1)S(1)} %get-tuple-element.80), channel_id=1, source_target_pairs={{0,16},{8,24},{16,0},{24,8},{1,17},{9,25},{17,1},{25,9},{2,18},{10... | collective-permute-start | bytes 1548296 | tf_op jit(solution)/shard_map/ppermute | solution.py:710
  23.2 5.3 %forward_6144.1 = (bf16[84,2688]{1,0:T(8,128)(2,1)S(1)}, bf16[84,2688]{1,0:T(8,128)(2,1)S(1)}, bf16[84,2688]{1,0:T(8,128)(2,1)S(1)}, bf16[84,2688]{1,0:T(8,128)(...) custom-call(bf16[96,23040]{1,0:T(8,128)(2,1)S(1)} %get-tuple-element.66.refs_0_, ...), custom_call_target="tpu_custom_call" | custom-call | flops 7023034368 | tf_op jit(solution)/shard_map/forward_6144/pallas_call | solution.py:392
  28.6 1.5 %collective-permute-start.3 = (bf16[84,2688]{1,0:T(8,128)(2,1)S(1)}, bf16[84,2688]{1,0:T(8,128)(2,1)S(1)}, u32[]{:S(2)}, u32[]{:S(2)}) collective-permute-start(bf16[84,2688]{1,0:T(8,128)(2,1)S(1)} %get-tuple-element.70), channel_id=1, source_target_pairs={{0,8},{8,0},{16,24},{24,16},{1,9},{9,1},{17,25},{25,17},{2,10},{10... | collective-permute-start | bytes 1354760 | tf_op jit(solution)/shard_map/ppermute | solution.py:710
  30.1 1.6 %collective-permute-start.4 = (bf16[84,2688]{1,0:T(8,128)(2,1)S(1)}, bf16[84,2688]{1,0:T(8,128)(2,1)S(1)}, u32[]{:S(2)}, u32[]{:S(2)}) collective-permute-start(bf16[84,2688]{1,0:T(8,128)(2,1)S(1)} %get-tuple-element.71), channel_id=1, source_target_pairs={{0,16},{8,24},{16,0},{24,8},{1,17},{9,25},{17,1},{25,9},{2,18},{10... | collective-permute-start | bytes 1354760 | tf_op jit(solution)/shard_map/ppermute | solution.py:710
  31.7 3.2 %collective-permute-done.9.refs_1_ = bf16[84,3072]{1,0:T(8,128)(2,1)S(1)} collective-permute-done((bf16[84,3072]{1,0:T(8,128)(2,1)S(1)}, bf16[84,3072]{1,0:T(8,128)(2,1)S(1)}, u32[]{:S(2)}, u32[]{:S(2)}) %collective-permute-start.9) | collective-permute-done | bytes 516128 | tf_op jit(solution)/shard_map/ppermute | solution.py:710
  34.8 2.5 %collective-permute-start.5 = (bf16[84,2688]{1,0:T(8,128)(2,1)S(1)}, bf16[84,2688]{1,0:T(8,128)(2,1)S(1)}, u32[]{:S(2)}, u32[]{:S(2)}) collective-permute-start(bf16[84,2688]{1,0:T(8,128)(2,1)S(1)} %get-tuple-element.72), channel_id=1, source_target_pairs={{0,24},{8,16},{16,8},{24,0},{1,25},{9,17},{17,9},{25,1},{2,26},{10... | collective-permute-start | bytes 1354760 | tf_op jit(solution)/shard_map/ppermute | solution.py:710
  37.3 10.6 %collective-permute-done.10.refs_2_ = bf16[84,3072]{1,0:T(8,128)(2,1)S(1)} collective-permute-done((bf16[84,3072]{1,0:T(8,128)(2,1)S(1)}, bf16[84,3072]{1,0:T(8,128)(2,1)S(1)}, u32[]{:S(2)}, u32[]{:S(2)}) %collective-permute-start.10) | collective-permute-done | bytes 516128 | tf_op jit(solution)/shard_map/ppermute | solution.py:710
  48.0 3.1 %score_0.1 = (bf16[84,3072]{1,0:T(8,128)(2,1)S(1)}, bf16[84,3072]{1,0:T(8,128)(2,1)S(1)}, bf16[84,3072]{1,0:T(8,128)(2,1)S(1)}, bf16[84,3072]{1,0:T(8,128)(2,1)S(1)}) custom-call(bf16[84,3072]{1,0:T(8,128)(2,1)S(1)} %get-tuple-element.77.target_ref, f32[84,128]{1,0:T(8,128)S(1)} %broadcast_in_dim.4.scale_ref, ...), custom_call_target="tpu_custom_call" | custom-call | flops 3354624000 | tf_op jit(solution)/shard_map/score_0/pallas_call | solution.py:454
  51.1 1.1 collective-permute-start.12
  52.2 1.1 collective-permute-start.13
  53.2 3.4 %collective-permute-done.3.refs_1_ = bf16[84,2688]{1,0:T(8,128)(2,1)S(1)} collective-permute-done((bf16[84,2688]{1,0:T(8,128)(2,1)S(1)}, bf16[84,2688]{1,0:T(8,128)(2,1)S(1)}, u32[]{:S(2)}, u32[]{:S(2)}) %collective-permute-start.3) | collective-permute-done | bytes 451616 | tf_op jit(solution)/shard_map/ppermute | solution.py:710
  56.6 2.5 %collective-permute-start.14 = (bf16[84,3072]{1,0:T(8,128)(2,1)S(1)}, bf16[84,3072]{1,0:T(8,128)(2,1)S(1)}, u32[]{:S(2)}, u32[]{:S(2)}) collective-permute-start(bf16[84,3072]{1,0:T(8,128)(2,1)S(1)} %get-tuple-element.85), channel_id=1, source_target_pairs={{0,24},{8,16},{16,8},{24,0},{1,25},{9,17},{17,9},{25,1},{2,26},{10... | collective-permute-start | bytes 1548296 | tf_op jit(solution)/shard_map/ppermute | solution.py:710
  59.1 9.1 %collective-permute-done.4.refs_2_ = bf16[84,2688]{1,0:T(8,128)(2,1)S(1)} collective-permute-done((bf16[84,2688]{1,0:T(8,128)(2,1)S(1)}, bf16[84,2688]{1,0:T(8,128)(2,1)S(1)}, u32[]{:S(2)}, u32[]{:S(2)}) %collective-permute-start.4) | collective-permute-done | bytes 451616 | tf_op jit(solution)/shard_map/ppermute | solution.py:710
  68.2 2.9 %score_6144.1 = (bf16[84,2688]{1,0:T(8,128)(2,1)S(1)}, bf16[84,2688]{1,0:T(8,128)(2,1)S(1)}, bf16[84,2688]{1,0:T(8,128)(2,1)S(1)}, bf16[84,2688]{1,0:T(8,128)(2,1)S(1)}) custom-call(bf16[84,2688]{1,0:T(8,128)(2,1)S(1)} %get-tuple-element.67.target_ref.refs_4_, f32[84,128]{1,0:T(8,128)S(1)} %broadcast_in_dim.4.scale_ref, ...), custom_call_target="tpu_custom_call" | custom-call | flops 2935296000 | tf_op jit(solution)/shard_map/score_6144/pallas_call | solution.py:454
  71.1 1.1 collective-permute-start.6
  72.2 1.0 collective-permute-start.7
  73.3 5.1 %collective-permute-done.12.refs_1_ = bf16[84,3072]{1,0:T(8,128)(2,1)S(1)} collective-permute-done((bf16[84,3072]{1,0:T(8,128)(2,1)S(1)}, bf16[84,3072]{1,0:T(8,128)(2,1)S(1)}, u32[]{:S(2)}, u32[]{:S(2)}) %collective-permute-start.12) | collective-permute-done | bytes 516128 | tf_op jit(solution)/shard_map/ppermute | solution.py:710
  78.4 2.5 %collective-permute-start.8 = (bf16[84,2688]{1,0:T(8,128)(2,1)S(1)}, bf16[84,2688]{1,0:T(8,128)(2,1)S(1)}, u32[]{:S(2)}, u32[]{:S(2)}) collective-permute-start(bf16[84,2688]{1,0:T(8,128)(2,1)S(1)} %get-tuple-element.76), channel_id=1, source_target_pairs={{0,24},{8,16},{16,8},{24,0},{1,25},{9,17},{17,9},{25,1},{2,26},{10... | collective-permute-start | bytes 1354760 | tf_op jit(solution)/shard_map/ppermute | solution.py:710
  80.9 10.5 %collective-permute-done.13.refs_2_ = bf16[84,3072]{1,0:T(8,128)(2,1)S(1)} collective-permute-done((bf16[84,3072]{1,0:T(8,128)(2,1)S(1)}, bf16[84,3072]{1,0:T(8,128)(2,1)S(1)}, u32[]{:S(2)}, u32[]{:S(2)}) %collective-permute-start.13) | collective-permute-done | bytes 516128 | tf_op jit(solution)/shard_map/ppermute | solution.py:710
  92.2 1.3 collective-permute-start.15
  93.5 2.5 %collective-permute-start.16 = (bf16[96,64]{1,0:T(8,128)(2,1)S(1)}, bf16[96,64]{1,0:T(8,128)(2,1)S(1)}, u32[]{:S(2)}, u32[]{:S(2)}) collective-permute-start(bf16[96,64]{1,0:T(8,128)(2,1)S(1)} %get-tuple-element.120), channel_id=1, source_target_pairs={{0,3},{1,2},{2,1},{3,0},{4,7},{5,6},{6,5},{7,4},{8,11},{9,10},{10,... | collective-permute-start | bytes 36872 | tf_op jit(solution)/shard_map/ppermute | solution.py:269
  96.1 7.3 %weight_0.1.refs_0_ = f32[96,1024]{1,0:T(8,128)S(1)} custom-call(bf16[288,15360]{1,0:T(8,128)(2,1)S(1)} %get-tuple-element.89.taps, bf16[96,12288]{1,0:T(8,128)(2,1)S(1)} %get-tuple-element.86.part_ref.refs_0_), custom_call_target="tpu_custom_call" | custom-call | flops 12288 | tf_op jit(solution)/shard_map/weight_0/pallas_call | solution.py:568
  103.6 1.3 collective-permute-done.17
  104.9 3.2 %input_48.1.refs_4_ = bf16[96,23040]{1,0:T(8,128)(2,1)} custom-call(bf16[96,12288]{1,0:T(8,128)(2,1)S(1)} %get-tuple-element.86.part_ref.refs_0_, bf16[96,128]{1,0:T(8,128)(2,1)S(1)} %maximum_select_fusion.refs_1_, bf16[96,864]{1,0:T(8,128)(2,1)S(1)} %get-tuple-element.91.refs_2_.refs_3_, bf16[96,512]{1,0:T(8,128)(2,1)S(1)} %get-tuple-element.114.refs_3_), custom_call_target="tpu_custom_call" | custom-call | flops 53084160 | bytes 5760 | tf_op jit(solution)/shard_map/input_48/pallas_call | solution.py:640
  108.2 2.4 %collective-permute-done.7.refs_2_ = bf16[84,2688]{1,0:T(8,128)(2,1)S(1)} collective-permute-done((bf16[84,2688]{1,0:T(8,128)(2,1)S(1)}, bf16[84,2688]{1,0:T(8,128)(2,1)S(1)}, u32[]{:S(2)}, u32[]{:S(2)}) %collective-permute-start.7) | collective-permute-done | bytes 451616 | tf_op jit(solution)/shard_map/ppermute | solution.py:710
  111.2 6.5 %weight_6144.1 = (f32[48,1024]{1,0:T(8,128)S(1)}, f32[48,1024]{1,0:T(8,128)S(1)}) custom-call(bf16[288,12288]{1,0:T(8,128)(2,1)S(1)} %get-tuple-element.93.taps, bf16[96,10752]{1,0:T(8,128)(2,1)S(1)} %get-tuple-element.94.part_ref.refs_1_, f32[96,1024]{1,0:T(8,128)S(1)} %weight_0.1.refs_0_), custom_call_target="tpu_custom_call" | custom-call | flops 10752 | tf_op jit(solution)/shard_map/weight_6144/pallas_call | solution.py:568
  117.8 1.3 collective-permute-start.22
  119.1 2.5 %collective-permute-start.23 = (bf16[96,64]{1,0:T(8,128)(2,1)S(1)}, bf16[96,64]{1,0:T(8,128)(2,1)S(1)}, u32[]{:S(2)}, u32[]{:S(2)}) collective-permute-start(bf16[96,64]{1,0:T(8,128)(2,1)S(1)} %get-tuple-element.118), channel_id=1, source_target_pairs={{0,3},{1,2},{2,1},{3,0},{4,7},{5,6},{6,5},{7,4},{8,11},{9,10},{10,... | collective-permute-start | bytes 36872 | tf_op jit(solution)/shard_map/ppermute | solution.py:269
  121.6 3.1 %collective-permute-done.23 = bf16[96,64]{1,0:T(8,128)(2,1)S(1)} collective-permute-done((bf16[96,64]{1,0:T(8,128)(2,1)S(1)}, bf16[96,64]{1,0:T(8,128)(2,1)S(1)}, u32[]{:S(2)}, u32[]{:S(2)}) %collective-permute-start.23) | collective-permute-done | bytes 12320 | tf_op jit(solution)/shard_map/ppermute | solution.py:269
  124.9 1.4 collective-permute-start.19
  127.0 1.4 collective-permute-start.21
  128.4 3.2 %input_0.1.refs_4_ = bf16[96,23040]{1,0:T(8,128)(2,1)} custom-call(bf16[96,12288]{1,0:T(8,128)(2,1)S(1)} %get-tuple-element.86.part_ref.refs_0_, bf16[96,128]{1,0:T(8,128)(2,1)S(1)} %fusion.refs_1_.refs_2_, bf16[96,864]{1,0:T(8,128)(2,1)S(1)} %get-tuple-element.91.refs_2_.refs_3_, ...), custom_call_target="tpu_custom_call", output_to_operand_aliasing={{}: (4, {})} | custom-call | flops 4246732800 | bytes 5760 | tf_op jit(solution)/shard_map/input_0/pallas_call | solution.py:640
  132.0 2.6 %collective-permute-start.26 = (f32[48,256]{1,0:T(8,128)S(1)}, f32[48,256]{1,0:T(8,128)S(1)}, u32[]{:S(2)}, u32[]{:S(2)}) collective-permute-start(f32[48,256]{1,0:T(8,128)S(1)} %add_add_fusion.1), channel_id=1, source_target_pairs={{0,3},{1,2},{2,1},{3,0},{4,7},{5,6},{6,5},{7,4},{8,11},{9,10},{10,... | collective-permute-start | bytes 147464 | tf_op jit(solution)/shard_map/ppermute | solution.py:710
  134.6 1.8 %collective-permute-start.24 = (f32[48,256]{1,0:T(8,128)S(1)}, f32[48,256]{1,0:T(8,128)S(1)}, u32[]{:S(2)}, u32[]{:S(2)}) collective-permute-start(f32[48,256]{1,0:T(8,128)S(1)} %add_add_fusion.1), channel_id=1, source_target_pairs={{0,1},{1,0},{2,3},{3,2},{4,5},{5,4},{6,7},{7,6},{8,9},{9,8},{10,11... | collective-permute-start | bytes 147464 | tf_op jit(solution)/shard_map/ppermute | solution.py:710
  136.5 3.2 %input_32.1.refs_4_ = bf16[96,23040]{1,0:T(8,128)(2,1)} custom-call(bf16[96,12288]{1,0:T(8,128)(2,1)S(1)} %get-tuple-element.86.part_ref.refs_0_, bf16[96,10752]{1,0:T(8,128)(2,1)S(1)} %get-tuple-element.94.part_ref.refs_1_, bf16[96,128]{1,0:T(8,128)(2,1)S(1)} %fusion.refs_1_.refs_2_, ...), custom_call_target="tpu_custom_call", output_to_operand_aliasing={{}: (4, {})} | custom-call | flops 4246732800 | bytes 5760 | tf_op jit(solution)/shard_map/input_32/pallas_call | solution.py:640
  139.7 1.5 %collective-permute-start.29 = (f32[48,256]{1,0:T(8,128)S(1)}, f32[48,256]{1,0:T(8,128)S(1)}, u32[]{:S(2)}, u32[]{:S(2)}) collective-permute-start(f32[48,256]{1,0:T(8,128)S(1)} %add_add_fusion.refs_0_), channel_id=1, source_target_pairs={{0,24},{8,16},{16,8},{24,0},{1,25},{9,17},{17,9},{25,1},{2,26},{10... | collective-permute-start | bytes 147464 | tf_op jit(solution)/shard_map/ppermute | solution.py:710
  141.2 1.5 %collective-permute-start.28 = (f32[48,256]{1,0:T(8,128)S(1)}, f32[48,256]{1,0:T(8,128)S(1)}, u32[]{:S(2)}, u32[]{:S(2)}) collective-permute-start(f32[48,256]{1,0:T(8,128)S(1)} %add_add_fusion.refs_0_), channel_id=1, source_target_pairs={{0,16},{8,24},{16,0},{24,8},{1,17},{9,25},{17,1},{25,9},{2,18},{10... | collective-permute-start | bytes 147464 | tf_op jit(solution)/shard_map/ppermute | solution.py:710
  143.3 3.3 %input_16.1 = bf16[96,23040]{1,0:T(8,128)(2,1)} custom-call(bf16[96,12288]{1,0:T(8,128)(2,1)S(1)} %get-tuple-element.86.part_ref.refs_0_, bf16[96,10752]{1,0:T(8,128)(2,1)S(1)} %get-tuple-element.94.part_ref.refs_1_, bf16[96,128]{1,0:T(8,128)(2,1)S(1)} %fusion.refs_1_.refs_2_, ...), custom_call_target="tpu_custom_call", output_to_operand_aliasing={{}: (4, {})} | custom-call | flops 4246732800 | bytes 5760 | tf_op jit(solution)/shard_map/input_16/pallas_call | solution.py:640
  147.0 1.4 collective-permute-done.30.other_ref
  148.4 1.3 finish.1
  (53 shorter events, 5.1 us)
Async XLA Ops:
  0.6 8.3 %copy-start = (bf16[9,8064]{1,0:T(8,128)(2,1)S(1)}, bf16[9,8064]{1,0:T(8,128)(2,1)}, u32[]{:S(2)}) copy-start(bf16[9,8064]{1,0:T(8,128)(2,1)} %param.6) | copy-start | bytes 435460
  0.6 10.5 %copy-start.2 = (f32[84]{0:T(128)S(1)}, f32[84]{0:T(128)}, u32[]{:S(2)}) copy-start(f32[84]{0:T(128)} %param.7) | copy-start | bytes 1012
  0.7 10.3 %copy-start.1 = (f32[84]{0:T(128)S(1)}, f32[84]{0:T(128)}, u32[]{:S(2)}) copy-start(f32[84]{0:T(128)} %param.9) | copy-start | bytes 1012
  3.8 7.0 %collective-permute-start = (bf16[96,64]{1,0:T(8,128)(2,1)S(1)}, bf16[96,64]{1,0:T(8,128)(2,1)S(1)}, u32[]{:S(2)}, u32[]{:S(2)}) collective-permute-start(bf16[96,64]{1,0:T(8,128)(2,1)S(1)} %get-tuple-element.121), channel_id=1, source_target_pairs={{0,1},{1,2},{2,3},{3,0},{4,5},{5,6},{6,7},{7,4},{8,9},{9,10},{10,1... | collective-permute-start | bytes 36872 | tf_op jit(solution)/shard_map/ppermute | solution.py:264
  6.8 4.1 %collective-permute-start.1 = (bf16[96,64]{1,0:T(8,128)(2,1)S(1)}, bf16[96,64]{1,0:T(8,128)(2,1)S(1)}, u32[]{:S(2)}, u32[]{:S(2)}) collective-permute-start(bf16[96,64]{1,0:T(8,128)(2,1)S(1)} %get-tuple-element.122), channel_id=1, source_target_pairs={{1,0},{2,1},{3,2},{0,3},{5,4},{6,5},{7,6},{4,7},{9,8},{10,9},{11,1... | collective-permute-start | bytes 36872 | tf_op jit(solution)/shard_map/ppermute | solution.py:264
  11.1 1.4 collective-permute-start.2
  19.7 15.2 %collective-permute-start.9 = (bf16[84,3072]{1,0:T(8,128)(2,1)S(1)}, bf16[84,3072]{1,0:T(8,128)(2,1)S(1)}, u32[]{:S(2)}, u32[]{:S(2)}) collective-permute-start(bf16[84,3072]{1,0:T(8,128)(2,1)S(1)} %get-tuple-element.79), channel_id=1, source_target_pairs={{0,8},{8,0},{16,24},{24,16},{1,9},{9,1},{17,25},{25,17},{2,10},{10... | collective-permute-start | bytes 1548296 | tf_op jit(solution)/shard_map/ppermute | solution.py:710
  21.2 26.7 %collective-permute-start.10 = (bf16[84,3072]{1,0:T(8,128)(2,1)S(1)}, bf16[84,3072]{1,0:T(8,128)(2,1)S(1)}, u32[]{:S(2)}, u32[]{:S(2)}) collective-permute-start(bf16[84,3072]{1,0:T(8,128)(2,1)S(1)} %get-tuple-element.80), channel_id=1, source_target_pairs={{0,16},{8,24},{16,0},{24,8},{1,17},{9,25},{17,1},{25,9},{2,18},{10... | collective-permute-start | bytes 1548296 | tf_op jit(solution)/shard_map/ppermute | solution.py:710
  22.8 25.2 %collective-permute-start.11 = (bf16[84,3072]{1,0:T(8,128)(2,1)S(1)}, bf16[84,3072]{1,0:T(8,128)(2,1)S(1)}, u32[]{:S(2)}, u32[]{:S(2)}) collective-permute-start(bf16[84,3072]{1,0:T(8,128)(2,1)S(1)} %get-tuple-element.81), channel_id=1, source_target_pairs={{0,24},{8,16},{16,8},{24,0},{1,25},{9,17},{17,9},{25,1},{2,26},{10... | collective-permute-start | bytes 1548296 | tf_op jit(solution)/shard_map/ppermute | solution.py:710
  28.6 28.1 %collective-permute-start.3 = (bf16[84,2688]{1,0:T(8,128)(2,1)S(1)}, bf16[84,2688]{1,0:T(8,128)(2,1)S(1)}, u32[]{:S(2)}, u32[]{:S(2)}) collective-permute-start(bf16[84,2688]{1,0:T(8,128)(2,1)S(1)} %get-tuple-element.70), channel_id=1, source_target_pairs={{0,8},{8,0},{16,24},{24,16},{1,9},{9,1},{17,25},{25,17},{2,10},{10... | collective-permute-start | bytes 1354760 | tf_op jit(solution)/shard_map/ppermute | solution.py:710
  30.1 38.1 %collective-permute-start.4 = (bf16[84,2688]{1,0:T(8,128)(2,1)S(1)}, bf16[84,2688]{1,0:T(8,128)(2,1)S(1)}, u32[]{:S(2)}, u32[]{:S(2)}) collective-permute-start(bf16[84,2688]{1,0:T(8,128)(2,1)S(1)} %get-tuple-element.71), channel_id=1, source_target_pairs={{0,16},{8,24},{16,0},{24,8},{1,17},{9,25},{17,1},{25,9},{2,18},{10... | collective-permute-start | bytes 1354760 | tf_op jit(solution)/shard_map/ppermute | solution.py:710
  34.8 33.4 %collective-permute-start.5 = (bf16[84,2688]{1,0:T(8,128)(2,1)S(1)}, bf16[84,2688]{1,0:T(8,128)(2,1)S(1)}, u32[]{:S(2)}, u32[]{:S(2)}) collective-permute-start(bf16[84,2688]{1,0:T(8,128)(2,1)S(1)} %get-tuple-element.72), channel_id=1, source_target_pairs={{0,24},{8,16},{16,8},{24,0},{1,25},{9,17},{17,9},{25,1},{2,26},{10... | collective-permute-start | bytes 1354760 | tf_op jit(solution)/shard_map/ppermute | solution.py:710
  51.1 27.3 %collective-permute-start.12 = (bf16[84,3072]{1,0:T(8,128)(2,1)S(1)}, bf16[84,3072]{1,0:T(8,128)(2,1)S(1)}, u32[]{:S(2)}, u32[]{:S(2)}) collective-permute-start(bf16[84,3072]{1,0:T(8,128)(2,1)S(1)} %get-tuple-element.83), channel_id=1, source_target_pairs={{0,8},{8,0},{16,24},{24,16},{1,9},{9,1},{17,25},{25,17},{2,10},{10... | collective-permute-start | bytes 1548296 | tf_op jit(solution)/shard_map/ppermute | solution.py:710
  52.2 39.2 %collective-permute-start.13 = (bf16[84,3072]{1,0:T(8,128)(2,1)S(1)}, bf16[84,3072]{1,0:T(8,128)(2,1)S(1)}, u32[]{:S(2)}, u32[]{:S(2)}) collective-permute-start(bf16[84,3072]{1,0:T(8,128)(2,1)S(1)} %get-tuple-element.84), channel_id=1, source_target_pairs={{0,16},{8,24},{16,0},{24,8},{1,17},{9,25},{17,1},{25,9},{2,18},{10... | collective-permute-start | bytes 1548296 | tf_op jit(solution)/shard_map/ppermute | solution.py:710
  56.6 34.8 %collective-permute-start.14 = (bf16[84,3072]{1,0:T(8,128)(2,1)S(1)}, bf16[84,3072]{1,0:T(8,128)(2,1)S(1)}, u32[]{:S(2)}, u32[]{:S(2)}) collective-permute-start(bf16[84,3072]{1,0:T(8,128)(2,1)S(1)} %get-tuple-element.85), channel_id=1, source_target_pairs={{0,24},{8,16},{16,8},{24,0},{1,25},{9,17},{17,9},{25,1},{2,26},{10... | collective-permute-start | bytes 1548296 | tf_op jit(solution)/shard_map/ppermute | solution.py:710
  71.1 37.0 %collective-permute-start.6 = (bf16[84,2688]{1,0:T(8,128)(2,1)S(1)}, bf16[84,2688]{1,0:T(8,128)(2,1)S(1)}, u32[]{:S(2)}, u32[]{:S(2)}) collective-permute-start(bf16[84,2688]{1,0:T(8,128)(2,1)S(1)} %get-tuple-element.74), channel_id=1, source_target_pairs={{0,8},{8,0},{16,24},{24,16},{1,9},{9,1},{17,25},{25,17},{2,10},{10... | collective-permute-start | bytes 1354760 | tf_op jit(solution)/shard_map/ppermute | solution.py:710
  72.2 38.4 %collective-permute-start.7 = (bf16[84,2688]{1,0:T(8,128)(2,1)S(1)}, bf16[84,2688]{1,0:T(8,128)(2,1)S(1)}, u32[]{:S(2)}, u32[]{:S(2)}) collective-permute-start(bf16[84,2688]{1,0:T(8,128)(2,1)S(1)} %get-tuple-element.75), channel_id=1, source_target_pairs={{0,16},{8,24},{16,0},{24,8},{1,17},{9,25},{17,1},{25,9},{2,18},{10... | collective-permute-start | bytes 1354760 | tf_op jit(solution)/shard_map/ppermute | solution.py:710
  78.4 32.2 %collective-permute-start.8 = (bf16[84,2688]{1,0:T(8,128)(2,1)S(1)}, bf16[84,2688]{1,0:T(8,128)(2,1)S(1)}, u32[]{:S(2)}, u32[]{:S(2)}) collective-permute-start(bf16[84,2688]{1,0:T(8,128)(2,1)S(1)} %get-tuple-element.76), channel_id=1, source_target_pairs={{0,24},{8,16},{16,8},{24,0},{1,25},{9,17},{17,9},{25,1},{2,26},{10... | collective-permute-start | bytes 1354760 | tf_op jit(solution)/shard_map/ppermute | solution.py:710
  92.2 11.2 %collective-permute-start.15 = (bf16[96,64]{1,0:T(8,128)(2,1)S(1)}, bf16[96,64]{1,0:T(8,128)(2,1)S(1)}, u32[]{:S(2)}, u32[]{:S(2)}) collective-permute-start(bf16[96,64]{1,0:T(8,128)(2,1)S(1)} %get-tuple-element.119), channel_id=1, source_target_pairs={{0,1},{1,0},{2,3},{3,2},{4,5},{5,4},{6,7},{7,6},{8,9},{9,8},{10,11... | collective-permute-start | bytes 36872 | tf_op jit(solution)/shard_map/ppermute | solution.py:268
  93.5 9.9 %collective-permute-start.16 = (bf16[96,64]{1,0:T(8,128)(2,1)S(1)}, bf16[96,64]{1,0:T(8,128)(2,1)S(1)}, u32[]{:S(2)}, u32[]{:S(2)}) collective-permute-start(bf16[96,64]{1,0:T(8,128)(2,1)S(1)} %get-tuple-element.120), channel_id=1, source_target_pairs={{0,3},{1,2},{2,1},{3,0},{4,7},{5,6},{6,5},{7,4},{8,11},{9,10},{10,... | collective-permute-start | bytes 36872 | tf_op jit(solution)/shard_map/ppermute | solution.py:269
  103.5 1.4 collective-permute-start.17
  117.8 3.9 %collective-permute-start.22 = (bf16[96,64]{1,0:T(8,128)(2,1)S(1)}, bf16[96,64]{1,0:T(8,128)(2,1)S(1)}, u32[]{:S(2)}, u32[]{:S(2)}) collective-permute-start(bf16[96,64]{1,0:T(8,128)(2,1)S(1)} %get-tuple-element.117), channel_id=1, source_target_pairs={{0,1},{1,0},{2,3},{3,2},{4,5},{5,4},{6,7},{7,6},{8,9},{9,8},{10,11... | collective-permute-start | bytes 36872 | tf_op jit(solution)/shard_map/ppermute | solution.py:268
  119.1 5.6 %collective-permute-start.23 = (bf16[96,64]{1,0:T(8,128)(2,1)S(1)}, bf16[96,64]{1,0:T(8,128)(2,1)S(1)}, u32[]{:S(2)}, u32[]{:S(2)}) collective-permute-start(bf16[96,64]{1,0:T(8,128)(2,1)S(1)} %get-tuple-element.118), channel_id=1, source_target_pairs={{0,3},{1,2},{2,1},{3,0},{4,7},{5,6},{6,5},{7,4},{8,11},{9,10},{10,... | collective-permute-start | bytes 36872 | tf_op jit(solution)/shard_map/ppermute | solution.py:269
  121.6 3.2 %collective-permute-start.18 = (f32[48,1024]{1,0:T(8,128)S(1)}, f32[48,1024]{1,0:T(8,128)S(1)}, u32[]{:S(2)}, u32[]{:S(2)}) collective-permute-start(f32[48,1024]{1,0:T(8,128)S(1)} %get-tuple-element.99), channel_id=1, source_target_pairs={{0,4},{4,0},{1,5},{5,1},{2,6},{6,2},{3,7},{7,3},{8,12},{12,8},{9,1... | collective-permute-start | bytes 589832 | tf_op jit(solution)/shard_map/ppermute | solution.py:710
  124.9 6.8 %collective-permute-start.19 = (f32[48,256]{1,0:T(8,128)S(1)}, f32[48,256]{1,0:T(8,128)S(1)}, u32[]{:S(2)}, u32[]{:S(2)}) collective-permute-start(f32[48,256]{1,0:T(8,128)S(1)} %get-tuple-element.101), channel_id=1, source_target_pairs={{0,8},{8,0},{16,24},{24,16},{1,9},{9,1},{17,25},{25,17},{2,10},{10... | collective-permute-start | bytes 147464 | tf_op jit(solution)/shard_map/ppermute | solution.py:710
  126.3 5.3 %collective-permute-start.20 = (f32[48,256]{1,0:T(8,128)S(1)}, f32[48,256]{1,0:T(8,128)S(1)}, u32[]{:S(2)}, u32[]{:S(2)}) collective-permute-start(f32[48,256]{1,0:T(8,128)S(1)} %get-tuple-element.102), channel_id=1, source_target_pairs={{0,16},{8,24},{16,0},{24,8},{1,17},{9,25},{17,1},{25,9},{2,18},{10... | collective-permute-start | bytes 147464 | tf_op jit(solution)/shard_map/ppermute | solution.py:710
  127.0 5.0 %collective-permute-start.21 = (f32[48,256]{1,0:T(8,128)S(1)}, f32[48,256]{1,0:T(8,128)S(1)}, u32[]{:S(2)}, u32[]{:S(2)}) collective-permute-start(f32[48,256]{1,0:T(8,128)S(1)} %get-tuple-element.103), channel_id=1, source_target_pairs={{0,24},{8,16},{16,8},{24,0},{1,25},{9,17},{17,9},{25,1},{2,26},{10... | collective-permute-start | bytes 147464 | tf_op jit(solution)/shard_map/ppermute | solution.py:710
  132.0 7.7 %collective-permute-start.26 = (f32[48,256]{1,0:T(8,128)S(1)}, f32[48,256]{1,0:T(8,128)S(1)}, u32[]{:S(2)}, u32[]{:S(2)}) collective-permute-start(f32[48,256]{1,0:T(8,128)S(1)} %add_add_fusion.1), channel_id=1, source_target_pairs={{0,3},{1,2},{2,1},{3,0},{4,7},{5,6},{6,5},{7,4},{8,11},{9,10},{10,... | collective-permute-start | bytes 147464 | tf_op jit(solution)/shard_map/ppermute | solution.py:710
  134.6 5.1 %collective-permute-start.25 = (f32[48,256]{1,0:T(8,128)S(1)}, f32[48,256]{1,0:T(8,128)S(1)}, u32[]{:S(2)}, u32[]{:S(2)}) collective-permute-start(f32[48,256]{1,0:T(8,128)S(1)} %add_add_fusion.1), channel_id=1, source_target_pairs={{0,2},{1,3},{2,0},{3,1},{4,6},{5,7},{6,4},{7,5},{8,10},{9,11},{10,... | collective-permute-start | bytes 147464 | tf_op jit(solution)/shard_map/ppermute | solution.py:710
  134.6 5.1 %collective-permute-start.24 = (f32[48,256]{1,0:T(8,128)S(1)}, f32[48,256]{1,0:T(8,128)S(1)}, u32[]{:S(2)}, u32[]{:S(2)}) collective-permute-start(f32[48,256]{1,0:T(8,128)S(1)} %add_add_fusion.1), channel_id=1, source_target_pairs={{0,1},{1,0},{2,3},{3,2},{4,5},{5,4},{6,7},{7,6},{8,9},{9,8},{10,11... | collective-permute-start | bytes 147464 | tf_op jit(solution)/shard_map/ppermute | solution.py:710
  139.7 7.1 %collective-permute-start.29 = (f32[48,256]{1,0:T(8,128)S(1)}, f32[48,256]{1,0:T(8,128)S(1)}, u32[]{:S(2)}, u32[]{:S(2)}) collective-permute-start(f32[48,256]{1,0:T(8,128)S(1)} %add_add_fusion.refs_0_), channel_id=1, source_target_pairs={{0,24},{8,16},{16,8},{24,0},{1,25},{9,17},{17,9},{25,1},{2,26},{10... | collective-permute-start | bytes 147464 | tf_op jit(solution)/shard_map/ppermute | solution.py:710
  141.2 5.6 %collective-permute-start.28 = (f32[48,256]{1,0:T(8,128)S(1)}, f32[48,256]{1,0:T(8,128)S(1)}, u32[]{:S(2)}, u32[]{:S(2)}) collective-permute-start(f32[48,256]{1,0:T(8,128)S(1)} %add_add_fusion.refs_0_), channel_id=1, source_target_pairs={{0,16},{8,24},{16,0},{24,8},{1,17},{9,25},{17,1},{25,9},{2,18},{10... | collective-permute-start | bytes 147464 | tf_op jit(solution)/shard_map/ppermute | solution.py:710
  142.8 4.1 %collective-permute-start.27 = (f32[48,256]{1,0:T(8,128)S(1)}, f32[48,256]{1,0:T(8,128)S(1)}, u32[]{:S(2)}, u32[]{:S(2)}) collective-permute-start(f32[48,256]{1,0:T(8,128)S(1)} %add_add_fusion.refs_0_), channel_id=1, source_target_pairs={{0,8},{8,0},{16,24},{24,16},{1,9},{9,1},{17,25},{25,17},{2,10},{10... | collective-permute-start | bytes 147464 | tf_op jit(solution)/shard_map/ppermute | solution.py:710
  146.9 1.5 %collective-permute-start.30 = (f32[48,1024]{1,0:T(8,128)S(1)}, f32[48,1024]{1,0:T(8,128)S(1)}, u32[]{:S(2)}, u32[]{:S(2)}) collective-permute-start(f32[48,1024]{1,0:T(8,128)S(1)} %join.1.own_ref), channel_id=1, source_target_pairs={{0,4},{4,0},{1,5},{5,1},{2,6},{6,2},{3,7},{7,3},{8,12},{12,8},{9,1... | collective-permute-start | bytes 589832 | tf_op jit(solution)/shard_map/ppermute | solution.py:710
